TPU v7x, 256 devices: a whole 4x4x8 slice. The times are simulated.
256 devices in a mesh: vseq: 64 (over y, x, z_hi), aseq: 4 (over z_lo, core).
Axes of the slice: x: 4, y: 4, z: 8 (z_hi: 4, z_lo: 2; z = z_hi * 2 + z_lo), core: 2. Of those that a mesh axis runs over, the one named last changes fastest.
Arguments:
- video_query: bfloat16 [32768, 3072], P('vseq', 'aseq'), may hold values from -40 to 40
- audio_key: bfloat16 [8192, 3072], P('vseq', 'aseq'), may hold values from -40 to 40
- audio_value: bfloat16 [8192, 3072], P('vseq', 'aseq'), may hold values from -6 to 6
- window_first: int32 [256], P('vseq'), may hold values from 0 to 252, as said below
- window_count: int32 [256], P('vseq'), may hold values from 4 to 20
- out_weight: bfloat16 [3072, 3072], P(None, 'aseq'), may hold values from -0.109375 to 0.109375
- cotangent: bfloat16 [32768, 3072], P('vseq', 'aseq'), may hold values from -16 to 16
Outputs:
- mixed_video: bfloat16 [32768, 3072], P('vseq', 'aseq')
- grad_query: float32 [32768, 3072], P('vseq', 'aseq')
- grad_key: float32 [8192, 3072], P('vseq', 'aseq')
- grad_value: float32 [8192, 3072], P('vseq', 'aseq')
- grad_weight: float32 [3072, 3072], P('vseq', 'aseq')
Inputs may be any that keep to these rules, and one draw needn't show every extreme that they name: `window_first`: the window of a video block in shard s of vseq (tokens s * 512 onward) starts at or after audio block (s - 2) * (4) and at or before s * 4, and ends at or after (s + 1) * (4) and at or before (s + 3) * 4, inside the audio sequence.
All inputs are finite; a program needn't handle non-finite values.
Results may differ from a plain program's by a relative error of at most 0.023.
Values may be sent and summed in bfloat16 or wider, within the bound.
No kernel may reach another device: no remote copies, remote signals or barrier semaphores. Data moves between devices by JAX's collectives and lax.ppermute only.
A program may use at most 128 MiB of HBM per device.

v0:
```python
import math

import jax
import jax.numpy as jnp
from jax import lax
from jax.sharding import PartitionSpec as P

HEAD = 128
VBLK = 128
ABLK = 32
REACH = 2


def from_behind(block, axis, distance):
    devices = range(lax.axis_size(axis))
    route = [(i - distance, i) for i in devices if i - distance in devices]
    return lax.ppermute(block, axis, route)


def local(video_query, audio_key, audio_value, window_first, window_count, out_weight, cotangent):
    token_rows, feature = video_query.shape
    audio_rows = audio_key.shape[0]
    head_count = feature // HEAD
    score_scale = 1.0 / math.sqrt(HEAD)
    own_index = lax.axis_index("vseq")
    stacked = jnp.stack([audio_key, audio_value])
    fetched = {}
    for offset in range(-REACH, REACH + 1):
        if offset != 0:
            fetched[offset] = from_behind(stacked, "vseq", -offset)
    ordered = [stacked if offset == 0 else fetched[offset] for offset in range(-REACH, REACH + 1)]
    audio_band = jnp.concatenate(ordered, axis=1)
    band_rows = audio_band.shape[1]
    per_shard = audio_rows // ABLK
    video_blocks = token_rows // VBLK
    key_block = (own_index - REACH) * per_shard + lax.iota(jnp.int32, band_rows) // ABLK
    row_first = jnp.broadcast_to(window_first[:, None], (video_blocks, VBLK)).reshape(token_rows)
    row_end = jnp.broadcast_to(
        (window_first + window_count)[:, None], (video_blocks, VBLK)
    ).reshape(token_rows)
    allowed = (key_block[None, :] >= row_first[:, None]) & (key_block[None, :] < row_end[:, None])
    query_heads = video_query.reshape(token_rows, head_count, HEAD)
    key_heads = audio_band[0].reshape(band_rows, head_count, HEAD)
    value_heads = audio_band[1].reshape(band_rows, head_count, HEAD)
    scores = (
        jnp.einsum("thd,khd->htk", query_heads, key_heads, preferred_element_type=jnp.float32)
        * score_scale
    )
    masked = jnp.where(allowed[None], scores, -jnp.inf)
    exponent = jnp.exp(masked - jnp.max(masked, axis=-1, keepdims=True))
    probs_full = exponent / jnp.sum(exponent, axis=-1, keepdims=True)
    probs_half = probs_full.astype(jnp.bfloat16)
    attended = jnp.einsum(
        "htk,khd->thd", probs_half, value_heads, preferred_element_type=jnp.float32
    ).astype(jnp.bfloat16)
    attended_flat = attended.reshape(token_rows, feature)
    partial_out = lax.dot_general(
        attended_flat, out_weight, (((1,), (1,)), ((), ())), preferred_element_type=jnp.float32
    )
    mixed_video = lax.psum_scatter(partial_out, "aseq", scatter_dimension=1, tiled=True).astype(
        jnp.bfloat16
    )
    cot_full = lax.all_gather(cotangent, "aseq", axis=1, tiled=True)
    grad_weight = lax.psum_scatter(
        lax.dot_general(
            cot_full, attended_flat, (((0,), (0,)), ((), ())), preferred_element_type=jnp.float32
        ),
        "vseq",
        scatter_dimension=0,
        tiled=True,
    )
    grad_attn = jnp.dot(cot_full, out_weight, preferred_element_type=jnp.float32).astype(
        jnp.bfloat16
    )
    grad_heads = grad_attn.reshape(token_rows, head_count, HEAD)
    row_delta = jnp.sum(grad_heads.astype(jnp.float32) * attended.astype(jnp.float32), axis=-1)
    prob_grad = jnp.einsum(
        "thd,khd->htk", grad_heads, value_heads, preferred_element_type=jnp.float32
    )
    score_grad = (probs_full * (prob_grad - jnp.transpose(row_delta)[:, :, None])).astype(
        jnp.bfloat16
    )
    grad_query = (
        jnp.einsum("htk,khd->thd", score_grad, key_heads, preferred_element_type=jnp.float32)
        * score_scale
    )
    band_key_grad = (
        jnp.einsum("htk,thd->khd", score_grad, query_heads, preferred_element_type=jnp.float32)
        * score_scale
    )
    band_value_grad = jnp.einsum(
        "htk,thd->khd", probs_half, grad_heads, preferred_element_type=jnp.float32
    )
    band_grad = jnp.stack(
        [band_key_grad.reshape(band_rows, feature), band_value_grad.reshape(band_rows, feature)]
    )

    def band_piece(offset):
        return band_grad[:, (offset + REACH) * audio_rows : (offset + REACH + 1) * audio_rows]

    summed = band_piece(0)
    for offset in range(-REACH, REACH + 1):
        if offset != 0:
            summed = summed + from_behind(
                band_piece(offset).astype(jnp.bfloat16), "vseq", offset
            ).astype(jnp.float32)
    return (mixed_video, grad_query.reshape(token_rows, feature), summed[0], summed[1], grad_weight)


def solution(mesh):
    in_specs = (
        P("vseq", "aseq"),
        P("vseq", "aseq"),
        P("vseq", "aseq"),
        P("vseq"),
        P("vseq"),
        P(None, "aseq"),
        P("vseq", "aseq"),
    )
    out_specs = (
        P("vseq", "aseq"),
        P("vseq", "aseq"),
        P("vseq", "aseq"),
        P("vseq", "aseq"),
        P("vseq", "aseq"),
    )
    return jax.shard_map(local, mesh=mesh, in_specs=in_specs, out_specs=out_specs, check_vma=False)
```

profile of v0, /device:TPU:32, one launch (start us, length us, event | category | flops | bytes accessed | tf_op | source)
XLA Modules:
  0.0 515.8 jit_solution(5956251727860288075)
XLA Ops:
  9.0 1.1 copy.46
  10.2 1.3 collective-permute-start.3
  11.5 1.3 collective-permute-start.2
  12.8 5.8 %collective-permute-start.1 = (bf16[2,128,768]{1,2,0:T(8,128)(2,1)S(1)}, bf16[2,128,768]{1,2,0:T(8,128)(2,1)S(1)}, u32[]{:S(2)}, u32[]{:S(2)}) collective-permute-start(bf16[2,128,768]{1,2,0:T(8,128)(2,1)S(1)} %pad_maximum_fusion.1), channel_id=1, source_target_pairs={{0,4},{4,8},{8,12},{12,16},{16,20},{20,24},{24,28},{28,32},{32,36}... | collective-permute-start | bytes 1179656 | tf_op jit(solution)/shard_map/ppermute | solution.py:17
  18.6 9.2 %collective-permute-start = (bf16[2,128,768]{1,2,0:T(8,128)(2,1)S(1)}, bf16[2,128,768]{1,2,0:T(8,128)(2,1)}, u32[]{:S(2)}, u32[]{:S(2)}) collective-permute-start(bf16[2,128,768]{1,2,0:T(8,128)(2,1)S(1)} %pad_maximum_fusion.1), channel_id=1, source_target_pairs={{0,8},{4,12},{8,16},{12,20},{16,24},{20,28},{24,32},{28,36},{32,40... | collective-permute-start | bytes 1179656 | tf_op jit(solution)/shard_map/ppermute | solution.py:17
  30.6 26.6 %collective-permute-done = bf16[2,128,768]{1,2,0:T(8,128)(2,1)} collective-permute-done((bf16[2,128,768]{1,2,0:T(8,128)(2,1)S(1)}, bf16[2,128,768]{1,2,0:T(8,128)(2,1)}, u32[]{:S(2)}, u32[]{:S(2)}) %collective-permute-start) | collective-permute-done | bytes 393248 | tf_op jit(solution)/shard_map/ppermute | solution.py:17
  59.3 5.1 fusion.22
  64.4 6.3 %fusion.6 = bf16[6,512,640]{1,2,0:T(8,128)(2,1)} fusion(f32[6,512,640]{1,2,0:T(8,128)} %get-tuple-element.29, f32[6,512]{1,0:T(8,128)S(1)} %get-tuple-element.28), kind=kLoop, calls=%fused_computation.14 | loop fusion | flops 3932160 | bytes 11808768 | tf_op jit(solution)/shard_map/convert_element_type | solution.py:52
  70.7 9.1 %all-gather.2.cloned.1.call-done = bf16[512,3072]{1,0:T(8,128)(2,1)} async-done(((bf16[512,768]{1,0:T(8,128)(2,1)}), bf16[512,3072]{1,0:T(8,128)(2,1)}) %all-gather.2.cloned.1.call-update) | async-done | bytes 3145744 | tf_op jit(solution)/shard_map/all_gather | solution.py:63
  79.8 5.9 %convolution_convert_fusion = bf16[512,768]{1,0:T(8,128)(2,1)S(1)} fusion(bf16[512,3072]{1,0:T(8,128)(2,1)} %all-gather.2.cloned.1.call-done, bf16[3072,768]{1,0:T(8,128)(2,1)} %param.12), kind=kOutput, calls=%fused_computation.18 | convolution fusion | flops 2416312320 | bytes 8650752 | tf_op jit(solution)/shard_map/dot_general | solution.py:72
  86.0 3.5 multiply_reduce_fusion
  89.5 6.9 %fusion.23 = f32[512,3072]{1,0:T(8,128)} fusion(bf16[512,768]{0,1:T(8,128)(2,1)S(1)} %bitcast.78, bf16[3072,768]{1,0:T(8,128)(2,1)} %param.12), kind=kOutput, calls=%fused_computation.50 | convolution fusion | flops 2415919104 | bytes 11796480 | tf_op jit(solution)/shard_map/dot_general | solution.py:57
  96.7 7.0 %convolution_bitcast_fusion = f32[3072,768]{0,1:T(8,128)} fusion(bf16[512,768]{0,1:T(8,128)(2,1)S(1)} %bitcast.79, bf16[512,3072]{1,0:T(8,128)(2,1)} %all-gather.2.cloned.1.call-done), kind=kOutput, calls=%fused_computation.5 | convolution fusion | flops 2415919104 | bytes 13369344 | tf_op jit(solution)/shard_map/dot_general | solution.py:65
  103.6 9.6 %copy.71 = f32[3072,768]{1,0:T(8,128)} copy(f32[3072,768]{0,1:T(8,128)} %convolution_bitcast_fusion) | data formatting | bytes 18874368
  113.3 4.7 fusion.24
  118.0 1.9 copy.59
  119.9 4.8 multiply_convert_fusion
  124.7 2.6 convolution_multiply_fusion
  127.3 2.8 copy.58
  130.2 2.0 fusion.2
  132.2 1.2 fusion.20
  133.4 1.3 collective-permute-start.4
  134.7 29.0 %collective-permute-start.7 = (bf16[2,128,768]{2,1,0:T(8,128)(2,1)}, bf16[2,128,768]{2,1,0:T(8,128)(2,1)}, u32[]{:S(2)}, u32[]{:S(2)}) collective-permute-start(bf16[2,128,768]{2,1,0:T(8,128)(2,1)} %get-tuple-element.21), channel_id=1, source_target_pairs={{0,8},{4,12},{8,16},{12,20},{16,24},{20,28},{24,32},{28,36},{32,40... | collective-permute-start | bytes 1179656 | tf_op jit(solution)/shard_map/ppermute | solution.py:17
  163.7 2.0 collective-permute-start.6
  165.7 1.3 collective-permute-start.5
  167.8 1.6 copy.60
  169.4 31.4 %collective-permute-done.4 = bf16[2,128,768]{2,1,0:T(8,128)(2,1)} collective-permute-done((bf16[2,128,768]{2,1,0:T(8,128)(2,1)}, bf16[2,128,768]{2,1,0:T(8,128)(2,1)}, u32[]{:S(2)}, u32[]{:S(2)}) %collective-permute-start.4) | collective-permute-done | bytes 393248 | tf_op jit(solution)/shard_map/ppermute | solution.py:17
  200.8 14.7 %collective-permute-done.5 = bf16[2,128,768]{2,1,0:T(8,128)(2,1)} collective-permute-done((bf16[2,128,768]{2,1,0:T(8,128)(2,1)}, bf16[2,128,768]{2,1,0:T(8,128)(2,1)}, u32[]{:S(2)}, u32[]{:S(2)}) %collective-permute-start.5) | collective-permute-done | bytes 393248 | tf_op jit(solution)/shard_map/ppermute | solution.py:17
  215.5 1.7 fusion.11
  218.1 13.7 %reduce-scatter.5.cloned.1.call-done = f32[512,768]{1,0:T(8,128)} async-done(((f32[512,3072]{1,0:T(8,128)}), f32[512,768]{1,0:T(8,128)}) %reduce-scatter.5.cloned.1.call-update) | async-done | bytes 1572880 | tf_op jit(solution)/shard_map/reduce_scatter | solution.py:60
  231.9 2.4 convert_element_type.43
  234.2 275.1 %reduce-scatter.7.cloned.1.call-done = f32[48,768]{1,0:T(8,128)} async-done(((f32[3072,768]{1,0:T(8,128)}), f32[48,768]{1,0:T(8,128)}) %reduce-scatter.7.cloned.1.call-update) | async-done | bytes 147472
  (41 shorter events, 8.9 us)
Async XLA Ops:
  7.2 23.1 %copy-start.5 = (bf16[512,768]{1,0:T(8,128)(2,1)S(1)}, bf16[512,768]{1,0:T(8,128)(2,1)}, u32[]{:S(2)}) copy-start(bf16[512,768]{1,0:T(8,128)(2,1)} %param.7) | copy-start | bytes 2359300
  7.2 72.7 %all-gather.2.cloned.1.call-start = ((), (), s32[]{:S(2)}) async-start(), calls=%async_computation.3 | async-start | bytes 3932160 | tf_op jit(solution)/shard_map/all_gather | solution.py:63
  7.9 224.0 %reduce-scatter.5.cloned.1.call-start = ((), (), s32[]{:S(2)}) async-start(), calls=%async_computation.2 | async-start | bytes 7864320 | tf_op jit(solution)/shard_map/reduce_scatter | solution.py:60
  10.2 48.4 %collective-permute-start.3 = (bf16[2,128,768]{1,2,0:T(8,128)(2,1)S(1)}, bf16[2,128,768]{1,2,0:T(8,128)(2,1)S(1)}, u32[]{:S(2)}, u32[]{:S(2)}) collective-permute-start(bf16[2,128,768]{1,2,0:T(8,128)(2,1)S(1)} %pad_maximum_fusion.1), channel_id=1, source_target_pairs={{8,0},{12,4},{16,8},{20,12},{24,16},{28,20},{32,24},{36,28},{40,32... | collective-permute-start | bytes 1179656 | tf_op jit(solution)/shard_map/ppermute | solution.py:17
  11.5 47.0 %collective-permute-start.2 = (bf16[2,128,768]{1,2,0:T(8,128)(2,1)S(1)}, bf16[2,128,768]{1,2,0:T(8,128)(2,1)S(1)}, u32[]{:S(2)}, u32[]{:S(2)}) collective-permute-start(bf16[2,128,768]{1,2,0:T(8,128)(2,1)S(1)} %pad_maximum_fusion.1), channel_id=1, source_target_pairs={{4,0},{8,4},{12,8},{16,12},{20,16},{24,20},{28,24},{32,28},{36,32}... | collective-permute-start | bytes 1179656 | tf_op jit(solution)/shard_map/ppermute | solution.py:17
  12.8 45.5 %collective-permute-start.1 = (bf16[2,128,768]{1,2,0:T(8,128)(2,1)S(1)}, bf16[2,128,768]{1,2,0:T(8,128)(2,1)S(1)}, u32[]{:S(2)}, u32[]{:S(2)}) collective-permute-start(bf16[2,128,768]{1,2,0:T(8,128)(2,1)S(1)} %pad_maximum_fusion.1), channel_id=1, source_target_pairs={{0,4},{4,8},{8,12},{12,16},{16,20},{20,24},{24,28},{28,32},{32,36}... | collective-permute-start | bytes 1179656 | tf_op jit(solution)/shard_map/ppermute | solution.py:17
  18.6 38.6 %collective-permute-start = (bf16[2,128,768]{1,2,0:T(8,128)(2,1)S(1)}, bf16[2,128,768]{1,2,0:T(8,128)(2,1)}, u32[]{:S(2)}, u32[]{:S(2)}) collective-permute-start(bf16[2,128,768]{1,2,0:T(8,128)(2,1)S(1)} %pad_maximum_fusion.1), channel_id=1, source_target_pairs={{0,8},{4,12},{8,16},{12,20},{16,24},{20,28},{24,32},{28,36},{32,40... | collective-permute-start | bytes 1179656 | tf_op jit(solution)/shard_map/ppermute | solution.py:17
  58.4 1.0 copy-start.6
  58.9 5.5 %copy-start.2 = (bf16[1,640,768]{1,2,0:T(8,128)(2,1)}, bf16[1,640,768]{1,2,0:T(8,128)(2,1)S(1)}, u32[]{:S(2)}) copy-start(bf16[1,640,768]{1,2,0:T(8,128)(2,1)S(1)} %get-tuple-element.24) | copy-start | bytes 2949124
  58.9 27.1 %copy-start.4 = (bf16[1,640,768]{1,2,0:T(8,128)(2,1)}, bf16[1,640,768]{1,2,0:T(8,128)(2,1)S(1)}, u32[]{:S(2)}) copy-start(bf16[1,640,768]{1,2,0:T(8,128)(2,1)S(1)} %get-tuple-element.25) | copy-start | bytes 2949124
  96.4 412.9 %reduce-scatter.7.cloned.1.call-start = ((), (), s32[]{:S(2)}) async-start(), calls=%async_computation.4 | async-start | bytes 9584640
  124.7 2.6 copy-start
  130.2 36.8 %copy-start.1 = (bf16[6,512,640]{1,2,0:T(8,128)(2,1)S(1)}, bf16[6,512,640]{1,2,0:T(8,128)(2,1)}, u32[]{:S(2)}) copy-start(bf16[6,512,640]{1,2,0:T(8,128)(2,1)} %copy-done) | copy-start | bytes 11796484
  130.2 36.8 %copy-start.3 = (bf16[1,640,768]{1,2,0:T(8,128)(2,1)S(1)}, bf16[1,640,768]{1,2,0:T(8,128)(2,1)}, u32[]{:S(2)}) copy-start(bf16[1,640,768]{1,2,0:T(8,128)(2,1)} %copy-done.2) | copy-start | bytes 2949124
  133.4 67.4 %collective-permute-start.4 = (bf16[2,128,768]{2,1,0:T(8,128)(2,1)}, bf16[2,128,768]{2,1,0:T(8,128)(2,1)}, u32[]{:S(2)}, u32[]{:S(2)}) collective-permute-start(bf16[2,128,768]{2,1,0:T(8,128)(2,1)} %get-tuple-element.20), channel_id=1, source_target_pairs={{8,0},{12,4},{16,8},{20,12},{24,16},{28,20},{32,24},{36,28},{40,32... | collective-permute-start | bytes 1179656 | tf_op jit(solution)/shard_map/ppermute | solution.py:17
  134.7 66.1 %collective-permute-start.7 = (bf16[2,128,768]{2,1,0:T(8,128)(2,1)}, bf16[2,128,768]{2,1,0:T(8,128)(2,1)}, u32[]{:S(2)}, u32[]{:S(2)}) collective-permute-start(bf16[2,128,768]{2,1,0:T(8,128)(2,1)} %get-tuple-element.21), channel_id=1, source_target_pairs={{0,8},{4,12},{8,16},{12,20},{16,24},{20,28},{24,32},{28,36},{32,40... | collective-permute-start | bytes 1179656 | tf_op jit(solution)/shard_map/ppermute | solution.py:17
  163.7 37.1 %collective-permute-start.6 = (bf16[2,128,768]{2,1,0:T(8,128)(2,1)}, bf16[2,128,768]{2,1,0:T(8,128)(2,1)}, u32[]{:S(2)}, u32[]{:S(2)}) collective-permute-start(bf16[2,128,768]{2,1,0:T(8,128)(2,1)} %get-tuple-element.22), channel_id=1, source_target_pairs={{0,4},{4,8},{8,12},{12,16},{16,20},{20,24},{24,28},{28,32},{32,36}... | collective-permute-start | bytes 1179656 | tf_op jit(solution)/shard_map/ppermute | solution.py:17
  165.7 49.8 %collective-permute-start.5 = (bf16[2,128,768]{2,1,0:T(8,128)(2,1)}, bf16[2,128,768]{2,1,0:T(8,128)(2,1)}, u32[]{:S(2)}, u32[]{:S(2)}) collective-permute-start(bf16[2,128,768]{2,1,0:T(8,128)(2,1)} %get-tuple-element.23), channel_id=1, source_target_pairs={{4,0},{8,4},{12,8},{16,12},{20,16},{24,20},{28,24},{32,28},{36,32}... | collective-permute-start | bytes 1179656 | tf_op jit(solution)/shard_map/ppermute | solution.py:17
Sparse Core Ops, SparseCore 0:
  9.8 69.9 all-gather.1
  96.5 135.2 reduce-scatter.4
  237.5 271.7 reduce-scatter.6
where the time goes:
time: 518 us; the launch traced here: 516 us
  waiting for transfers between devices  371 us (72%)
  starting transfers between devices  51.5 us (10%)
  matrix products  41.3 us (8%)
  local copies, waits for them, and re-layouts  23.6 us (5%)
  other arithmetic  14.2 us (3%)
  between operations  14 us (3%)
    unnamed x4, waiting for transfers between devices  276 us
    ppermute x8, waiting for transfers between devices, from_behind(): return lax.ppermute(block, axis, route)  72.7 us
    ppermute x8, starting transfers between devices, from_behind(): return lax.ppermute(block, axis, route)  51.2 us
    unnamed x22, local copies, waits for them, and re-layouts  15.4 us
    reduce_scatter x1, waiting for transfers between devices, local(): lax.psum_scatter(partial_out, 'aseq', scatter_dimension=1, tiled=True)  13.7 us
  transfers between devices with their start and end apart: 11, of which 6 were waited for; matrix products, arithmetic and copies ran while one was open for 12% of the time, Pallas kernels for 0%

commit v1 on v0

v1 whole, which is shorter than its diff:
```python
import functools
import math

import jax
import jax.numpy as jnp
from jax import lax
from jax.experimental import pallas as pl
from jax.experimental.pallas import tpu as pltpu
from jax.sharding import PartitionSpec as P

HEAD = 128
VBLK = 128
ABLK = 32
RING = 4
SCALE = 1.0 / math.sqrt(HEAD)
LOG2E = math.log2(math.e)
NT = (((1,), (1,)), ((), ()))
TN = (((0,), (0,)), ((), ()))
NN = (((1,), (0,)), ((), ()))
F32 = jnp.float32
BF = jnp.bfloat16
CORE = [(a, a ^ 1) for a in range(4)]
PAIR = [(a, a ^ 2) for a in range(4)]


def dot(a, b, dims):
    return lax.dot_general(a, b, dims, preferred_element_type=F32)


def attend_forward(q_ref, k0, k1, k2, k3, k4, bias_ref, att_ref, p_ref):
    pieces = (k0, k1, k2, k3, k4)
    q = q_ref[...]
    tokens = q.shape[0]
    rows = k0.shape[1]
    blocks = rows // ABLK
    scores = []
    for i, kv in enumerate(pieces):
        tile = dot(kv[0], q, NT).reshape(blocks, ABLK, tokens)
        tile = tile + bias_ref[blocks * i : blocks * (i + 1), :][:, None, :]
        scores.append(tile.reshape(rows, tokens))
    top = jnp.max(functools.reduce(jnp.maximum, scores), axis=0, keepdims=True)
    exponent = [jnp.exp2((tile - top) * (SCALE * LOG2E)) for tile in scores]
    total = jnp.sum(functools.reduce(jnp.add, exponent), axis=0, keepdims=True)
    share = 1.0 / total
    for i, tile in enumerate(exponent):
        p_ref[0, rows * i : rows * (i + 1), :] = (tile * share).astype(BF)
    values = jnp.concatenate([kv[1] for kv in pieces], axis=0)
    att_ref[...] = dot(values, p_ref[0], TN).T.astype(BF)


def attend_backward(
    q_ref, k0, k1, k2, k3, k4, p_ref, att_ref, do_ref, dq_ref, g0, g1, g2, g3, g4
):
    pieces = (k0, k1, k2, k3, k4)
    grads = (g0, g1, g2, g3, g4)
    q = q_ref[...]
    do = do_ref[...]
    rows = k0.shape[1]
    do_t = do.T
    delta = jnp.sum(
        do_t.astype(F32) * att_ref[...].T.astype(F32), axis=0, keepdims=True
    )
    score_grads = []
    for i, kv in enumerate(pieces):
        p = p_ref[0, rows * i : rows * (i + 1), :]
        prob_grad = dot(kv[1], do_t, NN)
        ds = (p.astype(F32) * (prob_grad - delta)).astype(BF)
        score_grads.append(ds)
        grads[i][0] = (dot(ds, q, NN) * SCALE).astype(grads[i].dtype)
        grads[i][1] = dot(p, do, NN).astype(grads[i].dtype)
    keys = jnp.concatenate([kv[0] for kv in pieces], axis=0)
    dq_ref[...] = (dot(keys, jnp.concatenate(score_grads, axis=0), TN) * SCALE).T


def forward_call(q, pieces, bias):
    tokens, feature = q.shape
    heads = feature // HEAD
    rows = pieces[0].shape[1]
    band = rows * len(pieces)
    by_head = pl.BlockSpec((tokens, HEAD), lambda h: (0, h))
    kv_head = pl.BlockSpec((2, rows, HEAD), lambda h: (0, 0, h))
    return pl.pallas_call(
        attend_forward,
        grid=(heads,),
        in_specs=[by_head] + [kv_head] * 5 + [pl.BlockSpec(bias.shape, lambda h: (0, 0))],
        out_specs=[by_head, pl.BlockSpec((1, band, tokens), lambda h: (h, 0, 0))],
        out_shape=[
            jax.ShapeDtypeStruct((tokens, feature), BF),
            jax.ShapeDtypeStruct((heads, band, tokens), BF),
        ],
        compiler_params=pltpu.CompilerParams(vmem_limit_bytes=40 << 20),
        cost_estimate=pl.CostEstimate(
            flops=4 * tokens * band * feature,
            bytes_accessed=heads * band * tokens * 2 + 2 * tokens * feature * 2,
            transcendentals=heads * band * tokens,
        ),
        name="attend_forward",
    )(q, *pieces, bias)


def backward_call(q, pieces, p, att, do):
    tokens, feature = q.shape
    heads = feature // HEAD
    rows = pieces[0].shape[1]
    band = rows * len(pieces)
    by_head = pl.BlockSpec((tokens, HEAD), lambda h: (0, h))
    kv_head = pl.BlockSpec((2, rows, HEAD), lambda h: (0, 0, h))
    piece = lambda kind: jax.ShapeDtypeStruct((2, rows, feature), kind)
    return pl.pallas_call(
        attend_backward,
        grid=(heads,),
        in_specs=[by_head]
        + [kv_head] * 5
        + [pl.BlockSpec((1, band, tokens), lambda h: (h, 0, 0)), by_head, by_head],
        out_specs=[by_head] + [kv_head] * 5,
        out_shape=[jax.ShapeDtypeStruct((tokens, feature), F32)]
        + [piece(F32), piece(F32), piece(F32), piece(BF), piece(BF)],
        compiler_params=pltpu.CompilerParams(vmem_limit_bytes=40 << 20),
        cost_estimate=pl.CostEstimate(
            flops=8 * tokens * band * feature,
            bytes_accessed=heads * band * tokens * 2 + tokens * feature * 10,
            transcendentals=0,
        ),
        name="attend_backward",
    )(q, *pieces, p, att, do)


def place(s):
    return s // (RING * RING), (s // RING) % RING, s % RING


def index(y, x, z):
    return (y * RING + x) * RING + z


def odd_swap(i, n):
    return (((i + 1) % n ^ 1) - 1) % n


def at(array, i):
    return lax.dynamic_index_in_dim(array, i, 0, keepdims=False)


def ring_sum(chunk, pos, even, odd):
    halves = lambda v: (v[: v.shape[0] // 2], v[v.shape[0] // 2 :])
    far = halves(chunk((pos + 2) % RING).astype(BF))
    from_even = lax.ppermute(far[0], "vseq", even)
    from_odd = lax.ppermute(far[1], "vseq", odd)
    to_even = halves(chunk(pos ^ 1))
    to_odd = halves(chunk(odd_swap(pos, RING)))
    to_even = jnp.concatenate(
        [to_even[0].astype(BF), (to_even[1].astype(F32) + from_odd.astype(F32)).astype(BF)], 0
    )
    to_odd = jnp.concatenate(
        [(to_odd[0].astype(F32) + from_even.astype(F32)).astype(BF), to_odd[1].astype(BF)], 0
    )
    even_sum = lax.ppermute(to_even, "vseq", even)
    odd_sum = lax.ppermute(to_odd, "vseq", odd)
    return chunk(pos).astype(F32) + even_sum.astype(F32) + odd_sum.astype(F32)


def local(video_query, audio_key, audio_value, window_first, window_count, out_weight, cotangent):
    tokens, feature = video_query.shape
    audio_rows = audio_key.shape[0]
    shards = lax.axis_size("vseq")
    s = lax.axis_index("vseq")
    a = lax.axis_index("aseq")
    y, x, z = place(s)
    each = range(shards)
    pa = [(i, i ^ 1) for i in each]
    pb = [(i, odd_swap(i, shards)) for i in each]

    def along(change):
        return [(i, index(*change(*place(i)))) for i in each]

    x_even = along(lambda y, x, z: (y, x ^ 1, z))
    x_odd = along(lambda y, x, z: (y, odd_swap(x, RING), z))
    y_even = along(lambda y, x, z: (y ^ 1, x, z))
    y_odd = along(lambda y, x, z: (odd_swap(y, RING), x, z))

    kv = jnp.stack([audio_key, audio_value])
    kv_a = lax.ppermute(kv, "vseq", pa)
    kv_b = lax.ppermute(kv, "vseq", pb)
    kv_aa = lax.ppermute(kv_b, "vseq", pa)
    kv_bb = lax.ppermute(kv_a, "vseq", pb)
    pieces = (kv, kv_a, kv_b, kv_aa, kv_bb)

    cot_core = lax.ppermute(cotangent, "aseq", CORE)
    cot_own, _, _ = lax.optimization_barrier((cotangent, kv_a, kv_b))
    cot_pair = lax.ppermute(cot_own, "aseq", PAIR)
    cot_both = lax.ppermute(cot_pair, "aseq", CORE)

    per_shard = audio_rows // ABLK
    step = 1 - 2 * (s % 2)
    offsets = jnp.stack([0 * step, step, -step, 2 * step, -2 * step])
    key_block = ((s + offsets)[:, None] * per_shard + jnp.arange(per_shard)[None, :]).reshape(-1)
    first = jnp.repeat(window_first, VBLK)
    end = jnp.repeat(window_first + window_count, VBLK)
    allowed = (key_block[:, None] >= first[None, :]) & (key_block[:, None] < end[None, :])
    bias = jnp.where(allowed, 0.0, -1e30).astype(F32)

    weight_parts = out_weight.reshape(4, feature, feature)
    weight = [at(weight_parts, a ^ j) for j in range(4)]

    att, p = forward_call(video_query, pieces, bias)

    far_core = dot(att, jnp.concatenate([weight[1], weight[3]], 0), NT).astype(BF)
    got_core = lax.ppermute(far_core, "aseq", CORE).astype(F32)
    far_pair = (dot(att, weight[2], NT) + got_core[:, feature:]).astype(BF)
    got_pair = lax.ppermute(far_pair, "aseq", PAIR).astype(F32)
    mixed_video = (dot(att, weight[0], NT) + got_core[:, :feature] + got_pair).astype(BF)

    cot = jnp.concatenate([cotangent, cot_core, cot_pair, cot_both], axis=1)
    grad_attn = dot(cot, jnp.concatenate(weight, 0), NN).astype(BF)
    grad_query, g_own, g_a, g_b, g_aa, g_bb = backward_call(
        video_query, pieces, p, att, grad_attn
    )

    back_a = lax.ppermute(g_aa, "vseq", pa)
    back_b = lax.ppermute(g_bb, "vseq", pb)
    sum_b = lax.ppermute((g_b + back_a.astype(F32)).astype(BF), "vseq", pb)
    sum_a = lax.ppermute((g_a + back_b.astype(F32)).astype(BF), "vseq", pa)
    grad_kv = g_own + sum_a.astype(F32) + sum_b.astype(F32)

    half = feature // 2
    part = feature // RING
    gw_x = dot(cot, att[:, :half], TN).astype(BF).reshape(RING, RING, part, half)
    gw_y = dot(cot, att[:, half:], TN).astype(BF).reshape(RING, feature, half)
    sum_x = ring_sum(lambda i: lax.dynamic_index_in_dim(gw_x, i, 1, keepdims=False), x, x_even, x_odd)
    sum_y = ring_sum(lambda i: at(gw_y, i ^ a), y, y_even, y_odd)
    sum_xy = ring_sum(lambda i: at(sum_x, i ^ a), y, y_even, y_odd)
    sum_yx = ring_sum(lambda i: at(sum_y.reshape(RING, part, half), i), x, x_even, x_odd)
    plane = jnp.concatenate([sum_xy, sum_yx], axis=1).reshape(RING, part // RING, feature)
    grad_weight = at(plane, z)
    for j in range(1, RING):
        swap = along(lambda y, x, z: (y, x, z ^ j))
        got = lax.ppermute(at(plane, z ^ j).astype(BF), "vseq", swap)
        grad_weight = grad_weight + got.astype(F32)
    return (mixed_video, grad_query, grad_kv[0], grad_kv[1], grad_weight)


def solution(mesh):
    both = P("vseq", "aseq")
    in_specs = (both, both, both, P("vseq"), P("vseq"), P(None, "aseq"), both)
    return jax.shard_map(
        local, mesh=mesh, in_specs=in_specs, out_specs=(both,) * 5, check_vma=False
    )
```

time: 518 us -> 188 us (0.36)
  waiting for transfers between devices: 371 us -> 79 us
  matrix products: 41.3 us -> 11.8 us
  Pallas kernels: 0 us -> 17.5 us
  between operations: 14 us -> 1.04 us
  local copies, waits for them, and re-layouts: 23.6 us -> 11.3 us
  starting transfers between devices: 51.5 us -> 61.8 us
  other arithmetic: 14.2 us -> 5.41 us
    unnamed x4 -> x0, waiting for transfers between devices: 276 us -> none
    dot_general x8 -> x6, matrix products: 36.2 us -> 11.8 us  [dot(): return lax.dot_general(a, b, dims, preferred_element_type=F32)]
    pallas_call x0 -> x2, Pallas kernels: none -> 17.5 us  [the longest x1 10.8 us: backward_call(): pl.pallas_call(attend_backward, grid=(heads,), in_specs=[by_head] + [kv_h...]
    reduce_scatter x1 -> x0, waiting for transfers between devices: 13.7 us -> none  [local(): lax.psum_scatter(partial_out, 'aseq', scatter_dimension=1, tiled=True)]
    unnamed x22 -> x15, local copies, waits for them, and re-layouts: 15.4 us -> 2.57 us
    ppermute x8 -> x32, starting transfers between devices: 51.2 us -> 61.8 us  [the longest x1 10.1 us: local(): kv_b = lax.ppermute(kv, 'vseq', pb)]
    all_gather x1 -> x0, waiting for transfers between devices: 9.09 us -> none  [local(): cot_full = lax.all_gather(cotangent, 'aseq', axis=1, tiled=True)]
    convert_element_type x2 -> x8, other arithmetic: 8.68 us -> 1.88 us  [the longest x4 1.27 us: ring_sum(): (to_even[1].astype(F32) + from_odd.astype(F32)).astype(BF)]
  transfers between devices with their start and end apart: 11 -> 32, of which waited for: 6 -> 16; matrix products, arithmetic and copies ran while one was open for 12% -> 14% of each run, Pallas kernels for 0% -> 9%
where the time goes in v1:
time: 188 us
  waiting for transfers between devices  79 us (42%)
  starting transfers between devices  61.8 us (33%)
  Pallas kernels  17.5 us (9%)
  matrix products  11.8 us (6%)
  local copies, waits for them, and re-layouts  11.3 us (6%)
  other arithmetic  5.41 us (3%)
    ppermute x1, waiting for transfers between devices, local(): cot_pair = lax.ppermute(cot_own, 'aseq', PAIR)  16.4 us
    ppermute x1, waiting for transfers between devices, local(): kv_b = lax.ppermute(kv, 'vseq', pb)  16.1 us
    dot_general x6, matrix products, dot(): return lax.dot_general(a, b, dims, preferred_element_type=F32)  11.8 us
    pallas_call x1, Pallas kernels, backward_call(): pl.pallas_call(attend_backward, grid=(heads,), in_specs=[by_head] + [kv_h...  10.8 us
    ppermute x1, waiting for transfers between devices, local(): back_b = lax.ppermute(g_bb, 'vseq', pb)  10.6 us
    ppermute x1, starting transfers between devices, local(): kv_b = lax.ppermute(kv, 'vseq', pb)  10.1 us
    ppermute x3, starting transfers between devices, local(): got = lax.ppermute(at(plane, z ^ j).astype(BF), 'vseq', swap)  9.52 us
    ppermute x1, waiting for transfers between devices, local(): sum_b = lax.ppermute((g_b + back_a.astype(F32)).astype(BF), 'vseq', pb)  7.52 us
  transfers between devices with their start and end apart: 32, of which 16 were waited for; matrix products, arithmetic and copies ran while one was open for 14% of the time, Pallas kernels for 9%

profile of v1, /device:TPU:32, one launch (start us, length us, event | category | flops | bytes accessed | tf_op | source)
XLA Modules:
  0.0 187.8 jit_solution(10993199395161136563)
XLA Ops:
  1.7 10.1 %collective-permute-start.1 = (bf16[2,128,768]{2,1,0:T(8,128)(2,1)S(1)}, bf16[2,128,768]{2,1,0:T(8,128)(2,1)S(1)}, u32[]{:S(2)}, u32[]{:S(2)}) collective-permute-start(bf16[2,128,768]{2,1,0:T(8,128)(2,1)S(1)} %pad_maximum_fusion.5.k0), channel_id=1, source_target_pairs={{0,252},{4,8},{8,4},{12,16},{16,12},{20,24},{24,20},{28,32},{32,28... | collective-permute-start | bytes 1179656 | tf_op jit(solution)/shard_map/ppermute | solution.py:183
  13.3 16.1 %collective-permute-done.1.k2 = bf16[2,128,768]{2,1,0:T(8,128)(2,1)S(1)} collective-permute-done((bf16[2,128,768]{2,1,0:T(8,128)(2,1)S(1)}, bf16[2,128,768]{2,1,0:T(8,128)(2,1)S(1)}, u32[]{:S(2)}, u32[]{:S(2)}) %collective-permute-start.1) | collective-permute-done | bytes 393248 | tf_op jit(solution)/shard_map/ppermute | solution.py:183
  30.4 2.4 %collective-permute-start.7 = (bf16[512,768]{1,0:T(8,128)(2,1)}, bf16[512,768]{1,0:T(8,128)(2,1)}, u32[]{:S(2)}, u32[]{:S(2)}) collective-permute-start(bf16[512,768]{1,0:T(8,128)(2,1)} %param.13), channel_id=1, source_target_pairs={{0,2},{1,3},{2,0},{3,1},{4,6},{5,7},{6,4},{7,5},{8,10},{9,11},{10,... | collective-permute-start | bytes 2359304 | tf_op jit(solution)/shard_map/ppermute | solution.py:190
  32.8 4.7 %dynamic-slice_bitcast_fusion.3 = (bf16[768,768]{1,0:T(8,128)(2,1)}, bf16[768,768]{1,0:T(8,128)(2,1)}, bf16[768,768]{1,0:T(8,128)(2,1)}, bf16[768,768]{1,0:T(8,128)(2,1)}) fusion(bf16[4,768,768]{2,1,0:T(8,128)(2,1)} %bitcast.151, s32[]{:T(128)S(6)} %select_n.125, s32[]{:T(128)S(6)} %select_n.128, s32[]{:T(128)S(6)} %select_n.127, s32[]{:T(128)S(6)} %select_n.126), kind=kLoop, calls=%fused_computation.27 | loop fusion | bytes 9437200 | tf_op jit(solution)/shard_map/jit(dynamic_index_in_dim)/squeeze | solution.py:141
  37.5 5.9 %collective-permute-start.3 = (bf16[2,128,768]{2,1,0:T(8,128)(2,1)S(1)}, bf16[2,128,768]{2,1,0:T(8,128)(2,1)S(1)}, u32[]{:S(2)}, u32[]{:S(2)}) collective-permute-start(bf16[2,128,768]{2,1,0:T(8,128)(2,1)S(1)} %collective-permute-done.k1), channel_id=1, source_target_pairs={{0,252},{4,8},{8,4},{12,16},{16,12},{20,24},{24,20},{28,32},{32,28... | collective-permute-start | bytes 1179656 | tf_op jit(solution)/shard_map/ppermute | solution.py:185
  43.5 16.4 %collective-permute-done.7 = bf16[512,768]{1,0:T(8,128)(2,1)} collective-permute-done((bf16[512,768]{1,0:T(8,128)(2,1)}, bf16[512,768]{1,0:T(8,128)(2,1)}, u32[]{:S(2)}, u32[]{:S(2)}) %collective-permute-start.7) | collective-permute-done | bytes 786464 | tf_op jit(solution)/shard_map/ppermute | solution.py:190
  60.1 6.3 %collective-permute-done.2.k3 = bf16[2,128,768]{2,1,0:T(8,128)(2,1)S(1)} collective-permute-done((bf16[2,128,768]{2,1,0:T(8,128)(2,1)S(1)}, bf16[2,128,768]{2,1,0:T(8,128)(2,1)S(1)}, u32[]{:S(2)}, u32[]{:S(2)}) %collective-permute-start.2) | collective-permute-done | bytes 393248 | tf_op jit(solution)/shard_map/ppermute | solution.py:184
  66.3 6.7 %attend_forward.1 = (bf16[512,768]{1,0:T(8,128)(2,1)S(1)}, bf16[6,640,512]{2,1,0:T(8,128)(2,1)S(1)}) custom-call(bf16[512,768]{1,0:T(8,128)(2,1)S(1)} %copy-done, bf16[2,128,768]{2,1,0:T(8,128)(2,1)S(1)} %pad_maximum_fusion.5.k0, bf16[2,128,768]{2,1,0:T(8,128)(2,1)S(1)} %collective-permute-done.k1, bf16[2,128,768]{2,1,0:T(8,128)(2,1)S(1)} %collective-permute-done.1.k2, ...), custom_call_target="tpu_custom_call" | custom-call | flops 1006632960 | bytes 5505024 | tf_op jit(solution)/shard_map/attend_forward/pallas_call | solution.py:82
  73.0 2.6 %convolution_convert_fusion.2 = bf16[512,1536]{1,0:T(8,128)(2,1)} fusion(bf16[512,768]{1,0:T(8,128)(2,1)S(1)} %get-tuple-element.14.att_ref, bf16[768,768]{1,0:T(8,128)(2,1)S(1)} %copy-done.3, bf16[768,768]{1,0:T(8,128)(2,1)S(1)} %copy-done.4), kind=kOutput, calls=%fused_computation.10 | convolution fusion | flops 1213464576 | bytes 4718592 | tf_op jit(solution)/shard_map/dot_general | solution.py:27
  78.2 1.8 convolution_convert_fusion
  80.1 1.8 convolution_convert_fusion.1
  84.5 1.6 collective-permute-start.13
  86.3 3.0 %fusion.14.do_ref = bf16[512,768]{1,0:T(8,128)(2,1)S(1)} fusion(bf16[512,3072]{1,0:T(8,128)(2,1)S(1)} %constant_dynamic-update-slice_fusion, bf16[768,768]{1,0:T(8,128)(2,1)S(1)} %copy-done.3, bf16[768,768]{1,0:T(8,128)(2,1)S(1)} %copy-done.2, bf16[768,768]{1,0:T(8,128)(2,1)S(1)} %copy-done.4, bf16[768,768]{1,0:T(8,128)(2,1)S(1)} %copy-done.1), kind=kOutput, calls=%fused_computation.19 | convolution fusion | flops 2435186688 | bytes 8650752 | tf_op jit(solution)/shard_map/dot_general | solution.py:27
  89.4 10.8 %attend_backward.1 = (f32[512,768]{1,0:T(8,128)}, f32[2,128,768]{2,1,0:T(8,128)S(1)}, f32[2,128,768]{2,1,0:T(8,128)S(1)}, f32[2,128,768]{2,1,0:T(8,128)S(1)}, bf...) custom-call(bf16[512,768]{1,0:T(8,128)(2,1)S(1)} %copy-done, ...), custom_call_target="tpu_custom_call" | custom-call | flops 2013265920 | bytes 7864320 | tf_op jit(solution)/shard_map/attend_backward/pallas_call | solution.py:109
  100.2 7.2 %collective-permute-start.9 = (bf16[2,128,768]{2,1,0:T(8,128)(2,1)S(1)}, bf16[2,128,768]{2,1,0:T(8,128)(2,1)S(1)}, u32[]{:S(2)}, u32[]{:S(2)}) collective-permute-start(bf16[2,128,768]{2,1,0:T(8,128)(2,1)S(1)} %get-tuple-element.20), channel_id=1, source_target_pairs={{0,252},{4,8},{8,4},{12,16},{16,12},{20,24},{24,20},{28,32},{32,28... | collective-permute-start | bytes 1179656 | tf_op jit(solution)/shard_map/ppermute | solution.py:220
  107.7 1.5 collective-permute-start.24
  109.3 1.9 collective-permute-start.22
  112.3 10.6 %collective-permute-done.9 = bf16[2,128,768]{2,1,0:T(8,128)(2,1)S(1)} collective-permute-done((bf16[2,128,768]{2,1,0:T(8,128)(2,1)S(1)}, bf16[2,128,768]{2,1,0:T(8,128)(2,1)S(1)}, u32[]{:S(2)}, u32[]{:S(2)}) %collective-permute-start.9) | collective-permute-done | bytes 393248 | tf_op jit(solution)/shard_map/ppermute | solution.py:220
  123.1 3.8 %collective-permute-done.11 = bf16[2,128,768]{2,1,0:T(8,128)(2,1)S(1)} collective-permute-done((bf16[2,128,768]{2,1,0:T(8,128)(2,1)S(1)}, bf16[2,128,768]{2,1,0:T(8,128)(2,1)S(1)}, u32[]{:S(2)}, u32[]{:S(2)}) %collective-permute-start.11) | collective-permute-done | bytes 393248 | tf_op jit(solution)/shard_map/ppermute | solution.py:219
  127.0 5.2 %collective-permute-start.12 = (bf16[2,128,768]{2,1,0:T(8,128)(2,1)S(1)}, bf16[2,128,768]{2,1,0:T(8,128)(2,1)S(1)}, u32[]{:S(2)}, u32[]{:S(2)}) collective-permute-start(bf16[2,128,768]{2,1,0:T(8,128)(2,1)S(1)} %add_convert_fusion), channel_id=1, source_target_pairs={{0,252},{4,8},{8,4},{12,16},{16,12},{20,24},{24,20},{28,32},{32,28... | collective-permute-start | bytes 1179656 | tf_op jit(solution)/shard_map/ppermute | solution.py:221
  133.5 5.8 %collective-permute-done.10 = bf16[2,128,768]{2,1,0:T(8,128)(2,1)S(1)} collective-permute-done((bf16[2,128,768]{2,1,0:T(8,128)(2,1)S(1)}, bf16[2,128,768]{2,1,0:T(8,128)(2,1)S(1)}, u32[]{:S(2)}, u32[]{:S(2)}) %collective-permute-start.10) | collective-permute-done | bytes 393248 | tf_op jit(solution)/shard_map/ppermute | solution.py:222
  139.4 2.1 %collective-permute-start.14 = (bf16[4,192,384]{2,1,0:T(8,128)(2,1)S(1)}, bf16[4,192,384]{2,1,0:T(8,128)(2,1)S(1)}, u32[]{:S(2)}, u32[]{:S(2)}) collective-permute-start(bf16[4,192,384]{2,1,0:T(8,128)(2,1)S(1)} %pad_maximum_fusion), channel_id=1, source_target_pairs={{0,16},{4,20},{8,24},{12,28},{16,0},{20,4},{24,8},{28,12},{32,48},... | collective-permute-start | bytes 1769480 | tf_op jit(solution)/shard_map/ppermute | solution.py:157
  141.5 7.5 %collective-permute-done.12 = bf16[2,128,768]{2,1,0:T(8,128)(2,1)S(1)} collective-permute-done((bf16[2,128,768]{2,1,0:T(8,128)(2,1)S(1)}, bf16[2,128,768]{2,1,0:T(8,128)(2,1)S(1)}, u32[]{:S(2)}, u32[]{:S(2)}) %collective-permute-start.12) | collective-permute-done | bytes 393248 | tf_op jit(solution)/shard_map/ppermute | solution.py:221
  149.0 5.6 %collective-permute-start.5 = (bf16[512,768]{1,0:T(8,128)(2,1)S(1)}, bf16[512,768]{1,0:T(8,128)(2,1)S(1)}, u32[]{:S(2)}, u32[]{:S(2)}) collective-permute-start(bf16[512,768]{1,0:T(8,128)(2,1)S(1)} %fusion.11), channel_id=1, source_target_pairs={{0,2},{1,3},{2,0},{3,1},{4,6},{5,7},{6,4},{7,5},{8,10},{9,11},{10,... | collective-permute-start | bytes 2359304 | tf_op jit(solution)/shard_map/ppermute | solution.py:210
  157.4 2.2 %collective-permute-start.17 = (bf16[96,384]{1,0:T(8,128)(2,1)S(1)}, bf16[96,384]{1,0:T(8,128)(2,1)S(1)}, u32[]{:S(2)}, u32[]{:S(2)}) collective-permute-start(bf16[96,384]{1,0:T(8,128)(2,1)S(1)} %get-tuple-element.50), channel_id=1, source_target_pairs={{0,192},{4,196},{8,200},{12,204},{16,208},{20,212},{24,216},{28,22... | collective-permute-start | bytes 221192 | tf_op jit(solution)/shard_map/ppermute | solution.py:148
  161.6 2.1 %collective-permute-start.28 = (bf16[192,384]{1,0:T(8,128)(2,1)S(1)}, bf16[192,384]{1,0:T(8,128)(2,1)S(1)}, u32[]{:S(2)}, u32[]{:S(2)}) collective-permute-start(bf16[192,384]{1,0:T(8,128)(2,1)S(1)} %pad_maximum_fusion.9), channel_id=1, source_target_pairs={{0,48},{4,52},{8,56},{12,60},{16,32},{20,36},{24,40},{28,44},{32,1... | collective-permute-start | bytes 442376 | tf_op jit(solution)/shard_map/ppermute | solution.py:158
  166.5 1.6 collective-permute-done.28
  170.8 2.2 %collective-permute-start.29 = (bf16[48,768]{1,0:T(8,128)(2,1)S(1)}, bf16[48,768]{1,0:T(8,128)(2,1)S(1)}, u32[]{:S(2)}, u32[]{:S(2)}) collective-permute-start(bf16[48,768]{1,0:T(8,128)(2,1)S(1)} %get-tuple-element.47), channel_id=1, source_target_pairs={{0,4},{4,0},{8,12},{12,8},{16,20},{20,16},{24,28},{28,24},{32,36},... | collective-permute-start | bytes 221192 | tf_op jit(solution)/shard_map/ppermute | solution.py:237
  173.0 5.8 %collective-permute-start.31 = (bf16[48,768]{1,0:T(8,128)(2,1)S(1)}, bf16[48,768]{1,0:T(8,128)(2,1)S(1)}, u32[]{:S(2)}, u32[]{:S(2)}) collective-permute-start(bf16[48,768]{1,0:T(8,128)(2,1)S(1)} %get-tuple-element.48), channel_id=1, source_target_pairs={{0,12},{4,8},{8,4},{12,0},{16,28},{20,24},{24,20},{28,16},{32,44},... | collective-permute-start | bytes 221192 | tf_op jit(solution)/shard_map/ppermute | solution.py:237
  178.8 1.5 collective-permute-start.30
  180.3 1.7 fusion.13
  182.6 4.5 %collective-permute-done.30 = bf16[48,768]{1,0:T(8,128)(2,1)S(1)} collective-permute-done((bf16[48,768]{1,0:T(8,128)(2,1)S(1)}, bf16[48,768]{1,0:T(8,128)(2,1)S(1)}, u32[]{:S(2)}, u32[]{:S(2)}) %collective-permute-start.30) | collective-permute-done | bytes 73760 | tf_op jit(solution)/shard_map/ppermute | solution.py:237
  (99 shorter events, 23.7 us)
Async XLA Ops:
  1.7 27.7 %collective-permute-start.1 = (bf16[2,128,768]{2,1,0:T(8,128)(2,1)S(1)}, bf16[2,128,768]{2,1,0:T(8,128)(2,1)S(1)}, u32[]{:S(2)}, u32[]{:S(2)}) collective-permute-start(bf16[2,128,768]{2,1,0:T(8,128)(2,1)S(1)} %pad_maximum_fusion.5.k0), channel_id=1, source_target_pairs={{0,252},{4,8},{8,4},{12,16},{16,12},{20,24},{24,20},{28,32},{32,28... | collective-permute-start | bytes 1179656 | tf_op jit(solution)/shard_map/ppermute | solution.py:183
  11.8 18.5 %collective-permute-start = (bf16[2,128,768]{2,1,0:T(8,128)(2,1)S(1)}, bf16[2,128,768]{2,1,0:T(8,128)(2,1)S(1)}, u32[]{:S(2)}, u32[]{:S(2)}) collective-permute-start(bf16[2,128,768]{2,1,0:T(8,128)(2,1)S(1)} %pad_maximum_fusion.5.k0), channel_id=1, source_target_pairs={{0,4},{4,0},{8,12},{12,8},{16,20},{20,16},{24,28},{28,24},{32,36},... | collective-permute-start | bytes 1179656 | tf_op jit(solution)/shard_map/ppermute | solution.py:182
  11.8 63.8 %collective-permute-start.6 = (bf16[512,768]{1,0:T(8,128)(2,1)}, bf16[512,768]{1,0:T(8,128)(2,1)}, u32[]{:S(2)}, u32[]{:S(2)}) collective-permute-start(bf16[512,768]{1,0:T(8,128)(2,1)} %param.13), channel_id=1, source_target_pairs={{0,1},{1,0},{2,3},{3,2},{4,5},{5,4},{6,7},{7,6},{8,9},{9,8},{10,11... | collective-permute-start | bytes 2359304 | tf_op jit(solution)/shard_map/ppermute | solution.py:188
  30.4 29.6 %collective-permute-start.7 = (bf16[512,768]{1,0:T(8,128)(2,1)}, bf16[512,768]{1,0:T(8,128)(2,1)}, u32[]{:S(2)}, u32[]{:S(2)}) collective-permute-start(bf16[512,768]{1,0:T(8,128)(2,1)} %param.13), channel_id=1, source_target_pairs={{0,2},{1,3},{2,0},{3,1},{4,6},{5,7},{6,4},{7,5},{8,10},{9,11},{10,... | collective-permute-start | bytes 2359304 | tf_op jit(solution)/shard_map/ppermute | solution.py:190
  37.5 28.9 %collective-permute-start.2 = (bf16[2,128,768]{2,1,0:T(8,128)(2,1)S(1)}, bf16[2,128,768]{2,1,0:T(8,128)(2,1)S(1)}, u32[]{:S(2)}, u32[]{:S(2)}) collective-permute-start(bf16[2,128,768]{2,1,0:T(8,128)(2,1)S(1)} %collective-permute-done.1.k2), channel_id=1, source_target_pairs={{0,4},{4,0},{8,12},{12,8},{16,20},{20,16},{24,28},{28,24},{32,36},... | collective-permute-start | bytes 1179656 | tf_op jit(solution)/shard_map/ppermute | solution.py:184
  37.5 28.9 %collective-permute-start.3 = (bf16[2,128,768]{2,1,0:T(8,128)(2,1)S(1)}, bf16[2,128,768]{2,1,0:T(8,128)(2,1)S(1)}, u32[]{:S(2)}, u32[]{:S(2)}) collective-permute-start(bf16[2,128,768]{2,1,0:T(8,128)(2,1)S(1)} %collective-permute-done.k1), channel_id=1, source_target_pairs={{0,252},{4,8},{8,4},{12,16},{16,12},{20,24},{24,20},{28,32},{32,28... | collective-permute-start | bytes 1179656 | tf_op jit(solution)/shard_map/ppermute | solution.py:185
  59.9 18.2 %collective-permute-start.8 = (bf16[512,768]{1,0:T(8,128)(2,1)}, bf16[512,768]{1,0:T(8,128)(2,1)S(1)}, u32[]{:S(2)}, u32[]{:S(2)}) collective-permute-start(bf16[512,768]{1,0:T(8,128)(2,1)} %collective-permute-done.7), channel_id=1, source_target_pairs={{0,1},{1,0},{2,3},{3,2},{4,5},{5,4},{6,7},{7,6},{8,9},{9,8},{10,11... | collective-permute-start | bytes 2359304 | tf_op jit(solution)/shard_map/ppermute | solution.py:191
  75.6 56.6 %collective-permute-start.4 = (bf16[512,1536]{1,0:T(8,128)(2,1)}, bf16[512,1536]{1,0:T(8,128)(2,1)S(1)}, u32[]{:S(2)}, u32[]{:S(2)}) collective-permute-start(bf16[512,1536]{1,0:T(8,128)(2,1)} %convolution_convert_fusion.2), channel_id=1, source_target_pairs={{0,1},{1,0},{2,3},{3,2},{4,5},{5,4},{6,7},{7,6},{8,9},{9,8},{10,11... | collective-permute-start | bytes 4718600 | tf_op jit(solution)/shard_map/ppermute | solution.py:208
  82.9 17.3 %collective-permute-start.21 = (bf16[384,384]{1,0:T(8,128)(2,1)}, bf16[384,384]{1,0:T(8,128)(2,1)S(1)}, u32[]{:S(2)}, u32[]{:S(2)}) collective-permute-start(bf16[384,384]{1,0:T(8,128)(2,1)} %get-tuple-element.32), channel_id=1, source_target_pairs={{0,192},{4,196},{8,200},{12,204},{16,208},{20,212},{24,216},{28,22... | collective-permute-start | bytes 884744 | tf_op jit(solution)/shard_map/ppermute | solution.py:148
  83.5 23.9 %collective-permute-start.23 = (bf16[384,384]{1,0:T(8,128)(2,1)}, bf16[384,384]{1,0:T(8,128)(2,1)S(1)}, u32[]{:S(2)}, u32[]{:S(2)}) collective-permute-start(bf16[384,384]{1,0:T(8,128)(2,1)} %get-tuple-element.34), channel_id=1, source_target_pairs={{0,64},{4,68},{8,72},{12,76},{16,80},{20,84},{24,88},{28,92},{32,9... | collective-permute-start | bytes 884744 | tf_op jit(solution)/shard_map/ppermute | solution.py:147
  84.5 24.9 %collective-permute-start.13 = (bf16[2,192,384]{2,1,0:T(8,128)(2,1)}, bf16[2,192,384]{2,1,0:T(8,128)(2,1)}, u32[]{:S(2)}, u32[]{:S(2)}) collective-permute-start(bf16[2,192,384]{2,1,0:T(8,128)(2,1)} %get-tuple-element.29), channel_id=1, source_target_pairs={{0,48},{4,52},{8,56},{12,60},{16,32},{20,36},{24,40},{28,44},{32,1... | collective-permute-start | bytes 884744 | tf_op jit(solution)/shard_map/ppermute | solution.py:148
  86.0 21.6 %collective-permute-start.15 = (bf16[2,192,384]{2,1,0:T(8,128)(2,1)}, bf16[2,192,384]{2,1,0:T(8,128)(2,1)S(1)}, u32[]{:S(2)}, u32[]{:S(2)}) collective-permute-start(bf16[2,192,384]{2,1,0:T(8,128)(2,1)} %get-tuple-element.30), channel_id=1, source_target_pairs={{0,16},{4,20},{8,24},{12,28},{16,0},{20,4},{24,8},{28,12},{32,48},... | collective-permute-start | bytes 884744 | tf_op jit(solution)/shard_map/ppermute | solution.py:147
  100.2 22.7 %collective-permute-start.9 = (bf16[2,128,768]{2,1,0:T(8,128)(2,1)S(1)}, bf16[2,128,768]{2,1,0:T(8,128)(2,1)S(1)}, u32[]{:S(2)}, u32[]{:S(2)}) collective-permute-start(bf16[2,128,768]{2,1,0:T(8,128)(2,1)S(1)} %get-tuple-element.20), channel_id=1, source_target_pairs={{0,252},{4,8},{8,4},{12,16},{16,12},{20,24},{24,20},{28,32},{32,28... | collective-permute-start | bytes 1179656 | tf_op jit(solution)/shard_map/ppermute | solution.py:220
  107.4 19.5 %collective-permute-start.11 = (bf16[2,128,768]{2,1,0:T(8,128)(2,1)S(1)}, bf16[2,128,768]{2,1,0:T(8,128)(2,1)S(1)}, u32[]{:S(2)}, u32[]{:S(2)}) collective-permute-start(bf16[2,128,768]{2,1,0:T(8,128)(2,1)S(1)} %get-tuple-element.22), channel_id=1, source_target_pairs={{0,4},{4,0},{8,12},{12,8},{16,20},{20,16},{24,28},{28,24},{32,36},... | collective-permute-start | bytes 1179656 | tf_op jit(solution)/shard_map/ppermute | solution.py:219
  107.7 48.0 %collective-permute-start.24 = (bf16[768,384]{1,0:T(8,128)(2,1)S(1)}, bf16[768,384]{1,0:T(8,128)(2,1)S(1)}, u32[]{:S(2)}, u32[]{:S(2)}) collective-permute-start(bf16[768,384]{1,0:T(8,128)(2,1)S(1)} %pad_maximum_fusion.3), channel_id=1, source_target_pairs={{0,192},{4,196},{8,200},{12,204},{16,208},{20,212},{24,216},{28,22... | collective-permute-start | bytes 1769480 | tf_op jit(solution)/shard_map/ppermute | solution.py:158
  109.3 46.3 %collective-permute-start.22 = (bf16[768,384]{1,0:T(8,128)(2,1)S(1)}, bf16[768,384]{1,0:T(8,128)(2,1)S(1)}, u32[]{:S(2)}, u32[]{:S(2)}) collective-permute-start(bf16[768,384]{1,0:T(8,128)(2,1)S(1)} %pad_maximum_fusion.2), channel_id=1, source_target_pairs={{0,64},{4,68},{8,72},{12,76},{16,80},{20,84},{24,88},{28,92},{32,9... | collective-permute-start | bytes 1769480 | tf_op jit(solution)/shard_map/ppermute | solution.py:157
  123.0 16.4 %collective-permute-start.10 = (bf16[2,128,768]{2,1,0:T(8,128)(2,1)S(1)}, bf16[2,128,768]{2,1,0:T(8,128)(2,1)S(1)}, u32[]{:S(2)}, u32[]{:S(2)}) collective-permute-start(bf16[2,128,768]{2,1,0:T(8,128)(2,1)S(1)} %add_convert_fusion.1), channel_id=1, source_target_pairs={{0,4},{4,0},{8,12},{12,8},{16,20},{20,16},{24,28},{28,24},{32,36},... | collective-permute-start | bytes 1179656 | tf_op jit(solution)/shard_map/ppermute | solution.py:222
  127.0 22.0 %collective-permute-start.12 = (bf16[2,128,768]{2,1,0:T(8,128)(2,1)S(1)}, bf16[2,128,768]{2,1,0:T(8,128)(2,1)S(1)}, u32[]{:S(2)}, u32[]{:S(2)}) collective-permute-start(bf16[2,128,768]{2,1,0:T(8,128)(2,1)S(1)} %add_convert_fusion), channel_id=1, source_target_pairs={{0,252},{4,8},{8,4},{12,16},{16,12},{20,24},{24,20},{28,32},{32,28... | collective-permute-start | bytes 1179656 | tf_op jit(solution)/shard_map/ppermute | solution.py:221
  132.2 24.0 %collective-permute-start.16 = (bf16[4,192,384]{2,1,0:T(8,128)(2,1)S(1)}, bf16[4,192,384]{2,1,0:T(8,128)(2,1)S(1)}, u32[]{:S(2)}, u32[]{:S(2)}) collective-permute-start(bf16[4,192,384]{2,1,0:T(8,128)(2,1)S(1)} %pad_maximum_fusion.1), channel_id=1, source_target_pairs={{0,48},{4,52},{8,56},{12,60},{16,32},{20,36},{24,40},{28,44},{32,1... | collective-permute-start | bytes 1769480 | tf_op jit(solution)/shard_map/ppermute | solution.py:158
  139.4 17.7 %collective-permute-start.14 = (bf16[4,192,384]{2,1,0:T(8,128)(2,1)S(1)}, bf16[4,192,384]{2,1,0:T(8,128)(2,1)S(1)}, u32[]{:S(2)}, u32[]{:S(2)}) collective-permute-start(bf16[4,192,384]{2,1,0:T(8,128)(2,1)S(1)} %pad_maximum_fusion), channel_id=1, source_target_pairs={{0,16},{4,20},{8,24},{12,28},{16,0},{20,4},{24,8},{28,12},{32,48},... | collective-permute-start | bytes 1769480 | tf_op jit(solution)/shard_map/ppermute | solution.py:157
  149.0 31.3 %collective-permute-start.5 = (bf16[512,768]{1,0:T(8,128)(2,1)S(1)}, bf16[512,768]{1,0:T(8,128)(2,1)S(1)}, u32[]{:S(2)}, u32[]{:S(2)}) collective-permute-start(bf16[512,768]{1,0:T(8,128)(2,1)S(1)} %fusion.11), channel_id=1, source_target_pairs={{0,2},{1,3},{2,0},{3,1},{4,6},{5,7},{6,4},{7,5},{8,10},{9,11},{10,... | collective-permute-start | bytes 2359304 | tf_op jit(solution)/shard_map/ppermute | solution.py:210
  155.9 5.7 %collective-permute-start.25 = (bf16[96,384]{1,0:T(8,128)(2,1)S(1)}, bf16[96,384]{1,0:T(8,128)(2,1)S(1)}, u32[]{:S(2)}, u32[]{:S(2)}) collective-permute-start(bf16[96,384]{1,0:T(8,128)(2,1)S(1)} %get-tuple-element.52), channel_id=1, source_target_pairs={{0,48},{4,52},{8,56},{12,60},{16,32},{20,36},{24,40},{28,44},{32,1... | collective-permute-start | bytes 221192 | tf_op jit(solution)/shard_map/ppermute | solution.py:148
  156.0 5.6 %collective-permute-start.27 = (bf16[96,384]{1,0:T(8,128)(2,1)S(1)}, bf16[96,384]{1,0:T(8,128)(2,1)S(1)}, u32[]{:S(2)}, u32[]{:S(2)}) collective-permute-start(bf16[96,384]{1,0:T(8,128)(2,1)S(1)} %get-tuple-element.53), channel_id=1, source_target_pairs={{0,16},{4,20},{8,24},{12,28},{16,0},{20,4},{24,8},{28,12},{32,48},... | collective-permute-start | bytes 221192 | tf_op jit(solution)/shard_map/ppermute | solution.py:147
  157.4 6.5 %collective-permute-start.17 = (bf16[96,384]{1,0:T(8,128)(2,1)S(1)}, bf16[96,384]{1,0:T(8,128)(2,1)S(1)}, u32[]{:S(2)}, u32[]{:S(2)}) collective-permute-start(bf16[96,384]{1,0:T(8,128)(2,1)S(1)} %get-tuple-element.50), channel_id=1, source_target_pairs={{0,192},{4,196},{8,200},{12,204},{16,208},{20,212},{24,216},{28,22... | collective-permute-start | bytes 221192 | tf_op jit(solution)/shard_map/ppermute | solution.py:148
  159.5 4.4 %collective-permute-start.19 = (bf16[96,384]{1,0:T(8,128)(2,1)S(1)}, bf16[96,384]{1,0:T(8,128)(2,1)S(1)}, u32[]{:S(2)}, u32[]{:S(2)}) collective-permute-start(bf16[96,384]{1,0:T(8,128)(2,1)S(1)} %get-tuple-element.51), channel_id=1, source_target_pairs={{0,64},{4,68},{8,72},{12,76},{16,80},{20,84},{24,88},{28,92},{32,9... | collective-permute-start | bytes 221192 | tf_op jit(solution)/shard_map/ppermute | solution.py:147
  161.6 6.4 %collective-permute-start.28 = (bf16[192,384]{1,0:T(8,128)(2,1)S(1)}, bf16[192,384]{1,0:T(8,128)(2,1)S(1)}, u32[]{:S(2)}, u32[]{:S(2)}) collective-permute-start(bf16[192,384]{1,0:T(8,128)(2,1)S(1)} %pad_maximum_fusion.9), channel_id=1, source_target_pairs={{0,48},{4,52},{8,56},{12,60},{16,32},{20,36},{24,40},{28,44},{32,1... | collective-permute-start | bytes 442376 | tf_op jit(solution)/shard_map/ppermute | solution.py:158
  163.8 5.2 %collective-permute-start.26 = (bf16[192,384]{1,0:T(8,128)(2,1)S(1)}, bf16[192,384]{1,0:T(8,128)(2,1)S(1)}, u32[]{:S(2)}, u32[]{:S(2)}) collective-permute-start(bf16[192,384]{1,0:T(8,128)(2,1)S(1)} %pad_maximum_fusion.8), channel_id=1, source_target_pairs={{0,16},{4,20},{8,24},{12,28},{16,0},{20,4},{24,8},{28,12},{32,48},... | collective-permute-start | bytes 442376 | tf_op jit(solution)/shard_map/ppermute | solution.py:157
  164.0 6.4 %collective-permute-start.20 = (bf16[192,384]{1,0:T(8,128)(2,1)S(1)}, bf16[192,384]{1,0:T(8,128)(2,1)S(1)}, u32[]{:S(2)}, u32[]{:S(2)}) collective-permute-start(bf16[192,384]{1,0:T(8,128)(2,1)S(1)} %pad_maximum_fusion.7), channel_id=1, source_target_pairs={{0,192},{4,196},{8,200},{12,204},{16,208},{20,212},{24,216},{28,22... | collective-permute-start | bytes 442376 | tf_op jit(solution)/shard_map/ppermute | solution.py:158
  165.4 5.2 %collective-permute-start.18 = (bf16[192,384]{1,0:T(8,128)(2,1)S(1)}, bf16[192,384]{1,0:T(8,128)(2,1)S(1)}, u32[]{:S(2)}, u32[]{:S(2)}) collective-permute-start(bf16[192,384]{1,0:T(8,128)(2,1)S(1)} %pad_maximum_fusion.6), channel_id=1, source_target_pairs={{0,64},{4,68},{8,72},{12,76},{16,80},{20,84},{24,88},{28,92},{32,9... | collective-permute-start | bytes 442376 | tf_op jit(solution)/shard_map/ppermute | solution.py:157
  170.8 11.2 %collective-permute-start.29 = (bf16[48,768]{1,0:T(8,128)(2,1)S(1)}, bf16[48,768]{1,0:T(8,128)(2,1)S(1)}, u32[]{:S(2)}, u32[]{:S(2)}) collective-permute-start(bf16[48,768]{1,0:T(8,128)(2,1)S(1)} %get-tuple-element.47), channel_id=1, source_target_pairs={{0,4},{4,0},{8,12},{12,8},{16,20},{20,16},{24,28},{28,24},{32,36},... | collective-permute-start | bytes 221192 | tf_op jit(solution)/shard_map/ppermute | solution.py:237
  173.0 9.6 %collective-permute-start.31 = (bf16[48,768]{1,0:T(8,128)(2,1)S(1)}, bf16[48,768]{1,0:T(8,128)(2,1)S(1)}, u32[]{:S(2)}, u32[]{:S(2)}) collective-permute-start(bf16[48,768]{1,0:T(8,128)(2,1)S(1)} %get-tuple-element.48), channel_id=1, source_target_pairs={{0,12},{4,8},{8,4},{12,0},{16,28},{20,24},{24,20},{28,16},{32,44},... | collective-permute-start | bytes 221192 | tf_op jit(solution)/shard_map/ppermute | solution.py:237
  178.8 8.3 %collective-permute-start.30 = (bf16[48,768]{1,0:T(8,128)(2,1)S(1)}, bf16[48,768]{1,0:T(8,128)(2,1)S(1)}, u32[]{:S(2)}, u32[]{:S(2)}) collective-permute-start(bf16[48,768]{1,0:T(8,128)(2,1)S(1)} %get-tuple-element.49), channel_id=1, source_target_pairs={{0,8},{4,12},{8,0},{12,4},{16,24},{20,28},{24,16},{28,20},{32,40},... | collective-permute-start | bytes 221192 | tf_op jit(solution)/shard_map/ppermute | solution.py:237
  (6 other events, 88.8 us)

commit v2 on v1

v2 whole, which is shorter than its diff:
```python
import functools
import math

import jax
import jax.numpy as jnp
import numpy as np
from jax import lax
from jax.experimental import pallas as pl
from jax.experimental.pallas import tpu as pltpu
from jax.sharding import PartitionSpec as P

HEAD = 128
VBLK = 128
ABLK = 32
RING = 4
SCALE = 1.0 / math.sqrt(HEAD)
LOG2E = math.log2(math.e)
NT = (((1,), (1,)), ((), ()))
TN = (((0,), (0,)), ((), ()))
NN = (((1,), (0,)), ((), ()))
F32 = jnp.float32
BF = jnp.bfloat16
VMEM = 32 << 20
CORE = [(a, a ^ 1) for a in range(4)]
PAIR = [(a, a ^ 2) for a in range(4)]


def dot(a, b, dims):
    return lax.dot_general(a, b, dims, preferred_element_type=F32)


def attend_forward(
    pos, q_ref, k0, k1, k2, k3, k4, v0, v1, v2, v3, v4, bias_ref, w_ref, l0, l1,
    att_ref, p_ref, out_ref, gw_ref, far0, far1, all_ref,
):
    q = q_ref[...]
    tokens = q.shape[0]
    rows = k0.shape[0]
    blocks = rows // ABLK
    scores = []
    for i, k in enumerate((k0, k1, k2, k3, k4)):
        tile = dot(k[...], q, NT).reshape(blocks, ABLK, tokens)
        tile = tile + bias_ref[blocks * i : blocks * (i + 1), :][:, None, :]
        scores.append(tile.reshape(rows, tokens))
    top = jnp.max(functools.reduce(jnp.maximum, scores), axis=0, keepdims=True)
    exponent = [jnp.exp2((tile - top) * (SCALE * LOG2E)) for tile in scores]
    total = jnp.sum(functools.reduce(jnp.add, exponent), axis=0, keepdims=True)
    share = 1.0 / total
    for i, tile in enumerate(exponent):
        p_ref[0, rows * i : rows * (i + 1), :] = (tile * share).astype(BF)
    values = jnp.concatenate([v[...] for v in (v0, v1, v2, v3, v4)], axis=0)
    att = dot(values, p_ref[0], TN).T.astype(BF)
    att_ref[...] = att
    head = pl.program_id(0)
    all_ref[:, pl.ds(pl.multiple_of(head * HEAD, HEAD), HEAD)] = att

    @pl.when(head == pl.num_programs(0) - 1)
    def _():
        out_ref[...] = dot(all_ref[...], w_ref[...], NT).astype(BF)
        weight_rows((l0, l1), all_ref, gw_ref)
        far0[...] = gw_ref[0, pos[FAR]]
        far1[...] = gw_ref[1, pos[FAR]]


def weight_rows(lefts, att_ref, gw_ref):
    part = gw_ref.shape[2]
    for j, left in enumerate(lefts):
        rows = dot(left[...], att_ref[...], TN).astype(BF)
        for i in range(RING):
            gw_ref[j, i] = rows[i * part : (i + 1) * part]


def attend_backward(
    given, q_ref, k0, k1, k2, k3, k4, v0, v1, v2, v3, v4, p_ref, att_ref, near_ref, c0, c1, w0, w1, *refs
):
    dq_ref, g0, g1, g2, g3, g4, all_ref = refs[given:]
    head = pl.program_id(0)

    @pl.when(head == 0)
    def _():
        total = near_ref[...] + dot(c0[...], w0[...], NN) + dot(c1[...], w1[...], NN)
        all_ref[...] = total.astype(BF)

    grads = (g0, g1, g2, g3, g4)
    q = q_ref[...]
    do = all_ref[:, pl.ds(pl.multiple_of(head * HEAD, HEAD), HEAD)]
    rows = k0.shape[0]
    do_t = do.T
    delta = jnp.sum(
        do_t.astype(F32) * att_ref[...].T.astype(F32), axis=0, keepdims=True
    )
    score_grads = []
    for i, v in enumerate((v0, v1, v2, v3, v4)):
        p = p_ref[0, rows * i : rows * (i + 1), :]
        prob_grad = dot(v[...], do_t, NN)
        ds = (p.astype(F32) * (prob_grad - delta)).astype(BF)
        score_grads.append(ds)
        grads[i][0] = (dot(ds, q, NN) * SCALE).astype(grads[i].dtype)
        grads[i][1] = dot(p, do, NN).astype(grads[i].dtype)
    keys = jnp.concatenate([k[...] for k in (k0, k1, k2, k3, k4)], axis=0)
    dq_ref[...] = (dot(keys, jnp.concatenate(score_grads, axis=0), TN) * SCALE).T


def call(kernel, grid, scalars, in_specs, out_specs, out_shape, scratch=(), name=None, cost=None):
    return pl.pallas_call(
        kernel,
        grid_spec=pltpu.PrefetchScalarGridSpec(
            num_scalar_prefetch=len(scalars),
            grid=grid,
            in_specs=in_specs,
            out_specs=out_specs,
            scratch_shapes=scratch,
        ),
        out_shape=out_shape,
        compiler_params=pltpu.CompilerParams(vmem_limit_bytes=VMEM),
        cost_estimate=cost,
        name=name,
    )


def whole(v):
    return pl.BlockSpec(v.shape, lambda *_: (0,) * len(v.shape))


def weight_far_kernel(pos, l0, l1, att_ref, gw_ref, far0, far1):
    weight_rows((l0, l1), att_ref, gw_ref)
    far0[...] = gw_ref[0, pos[FAR]]
    far1[...] = gw_ref[1, pos[FAR]]


def weight_far(pos, l0, l1, att):
    part, feature = l0.shape[1] // RING, att.shape[1]
    far = jax.ShapeDtypeStruct((part, feature), BF)
    shapes = [jax.ShapeDtypeStruct((2, RING, part, feature), BF), far, far]
    return call(
        weight_far_kernel,
        (1,),
        (pos,),
        [whole(l0), whole(l1), whole(att)],
        [whole(v) for v in shapes],
        shapes,
        name="weight_far",
    )(pos, l0, l1, att)


def beside_kernel(pos, even, odd, got_even, got_odd, to_even, to_odd):
    to_even[0] = even[0, 0]
    to_even[1] = (even[1, 0].astype(F32) + got_odd[...].astype(F32)).astype(BF)
    to_odd[0] = (odd[0, 0].astype(F32) + got_even[...].astype(F32)).astype(BF)
    to_odd[1] = odd[1, 0]


def beside(pos, chunks, got):
    _, _, part, feature = chunks.shape
    send = jax.ShapeDtypeStruct((2, part, feature), BF)
    pick = lambda k: pl.BlockSpec((2, 1, part, feature), lambda i, pos: (0, pos[k], 0, 0))
    return call(
        beside_kernel,
        (1,),
        (pos,),
        [pick(EVEN), pick(ODD), whole(got[0]), whole(got[1])],
        [whole(send)] * 2,
        [send] * 2,
        name="beside",
    )(pos, chunks, chunks, *got)


def rows_kernel(pos, near, near_even, near_odd, more, more_even, more_odd, keep, s1, s2, s3, rows):
    for j, (own, even, odd) in enumerate(((near, near_even, near_odd), (more, more_even, more_odd))):
        total = own[:, 0].astype(F32) + even[...].astype(F32) + odd[...].astype(F32)
        rows[2 * j : 2 * j + 2] = total.astype(BF)
    for k, out in enumerate((keep, s1, s2, s3)):
        out[...] = rows[pos[PART + k]]


def rows_of(pos, near, near_got, more, more_got):
    _, _, part, feature = near.shape
    send = jax.ShapeDtypeStruct((part, feature), BF)
    own = pl.BlockSpec((2, 1, part, feature), lambda i, pos: (0, pos[OWN], 0, 0))
    got = whole(near_got[0])
    return call(
        rows_kernel,
        (1,),
        (pos,),
        [own, got, got] * 2,
        [whole(send)] * 4,
        [send] * 4,
        scratch=[pltpu.VMEM((RING, part, feature), BF)],
        name="rows",
    )(pos, near, *near_got, more, *more_got)


def plane_kernel(pos, own, g1, g2, g3, keep, s1, s2, s3, rows):
    each = own.shape[0] // RING
    total = own[...].astype(F32) + g1[...].astype(F32) + g2[...].astype(F32) + g3[...].astype(F32)
    for i in range(RING):
        rows[i] = total[i * each : (i + 1) * each]
    keep[...] = rows[pos[SHARE]]
    for k, out in enumerate((s1, s2, s3)):
        out[...] = rows[pos[SHARE + 1 + k]].astype(BF)


def plane_of(pos, own, got):
    part, feature = own.shape
    each = part // RING
    shapes = [jax.ShapeDtypeStruct((each, feature), F32)] + [jax.ShapeDtypeStruct((each, feature), BF)] * 3
    return call(
        plane_kernel,
        (1,),
        (pos,),
        [whole(own)] + [whole(v) for v in got],
        [whole(v) for v in shapes],
        shapes,
        scratch=[pltpu.VMEM((RING, each, feature), F32)],
        name="plane",
    )(pos, own, *got)


def forward_call(pos, q, keys, values, bias, weight, lefts):
    tokens, feature = q.shape
    heads = feature // HEAD
    rows = keys[0].shape[0]
    band = rows * len(keys)
    part = feature // RING
    by_head = pl.BlockSpec((tokens, HEAD), lambda h, pos: (0, h))
    kv_head = pl.BlockSpec((rows, HEAD), lambda h, pos: (0, h))
    once = [
        jax.ShapeDtypeStruct((tokens, weight.shape[0]), BF),
        jax.ShapeDtypeStruct((2, RING, part, feature), BF),
        jax.ShapeDtypeStruct((part, feature), BF),
        jax.ShapeDtypeStruct((part, feature), BF),
    ]
    return call(
        attend_forward,
        (heads,),
        (pos,),
        [by_head] + [kv_head] * 10 + [whole(v) for v in (bias, weight, *lefts)],
        [by_head, pl.BlockSpec((1, band, tokens), lambda h, pos: (h, 0, 0))] + [whole(v) for v in once],
        [
            jax.ShapeDtypeStruct((tokens, feature), BF),
            jax.ShapeDtypeStruct((heads, band, tokens), BF),
        ]
        + once,
        scratch=[pltpu.VMEM((tokens, feature), BF)],
        name="attend_forward",
        cost=pl.CostEstimate(
            flops=8 * tokens * band * feature, bytes_accessed=0, transcendentals=heads * band * tokens
        ),
    )(pos, q, *keys, *values, bias, weight, *lefts)


def backward_call(q, keys, values, p, att, near, cots, weights, half, done):
    tokens, feature = q.shape
    heads = feature // HEAD // 2
    first = half * heads
    rows = keys[0].shape[0]
    band = rows * len(keys)
    by_head = pl.BlockSpec((tokens, HEAD), lambda h: (0, first + h))
    kv_head = pl.BlockSpec((rows, HEAD), lambda h: (0, first + h))
    both_head = pl.BlockSpec((2, rows, HEAD), lambda h: (0, 0, first + h))
    columns = lambda v: pl.BlockSpec((v.shape[0], feature // 2), lambda h: (0, half))
    piece = lambda kind: jax.ShapeDtypeStruct((2, rows, feature), kind)
    given = 18
    return pl.pallas_call(
        functools.partial(attend_backward, len(done)),
        grid=(heads,),
        in_specs=[by_head]
        + [kv_head] * 10
        + [pl.BlockSpec((1, band, tokens), lambda h: (first + h, 0, 0)), by_head, columns(near)]
        + [whole(v) for v in cots]
        + [columns(v) for v in weights]
        + [pl.BlockSpec(memory_space=pl.ANY)] * len(done),
        out_specs=[by_head] + [both_head] * 5,
        out_shape=[jax.ShapeDtypeStruct((tokens, feature), F32)]
        + [piece(F32), piece(F32), piece(F32), piece(BF), piece(BF)],
        scratch_shapes=[pltpu.VMEM((tokens, feature // 2), BF)],
        input_output_aliases={given + i: i for i in range(len(done))},
        compiler_params=pltpu.CompilerParams(vmem_limit_bytes=VMEM),
        cost_estimate=pl.CostEstimate(
            flops=6 * tokens * band * feature, bytes_accessed=0, transcendentals=0
        ),
        name="attend_backward",
    )(q, *keys, *values, p, att, near, *cots, *weights, *done)


def place(s):
    return s // (RING * RING), (s // RING) % RING, s % RING


def index(y, x, z):
    return (y * RING + x) * RING + z


FAR, EVEN, ODD, OWN, PART, SHARE, WEIGHT, AUDIO = 0, 1, 2, 3, 4, 8, 12, 16


def table(shards, per_shard):
    rows = []
    for s in range(shards):
        y, x, z = place(s)
        step = 1 - 2 * (s % 2)
        for a in range(4):
            row = [(x + 2) % RING, x ^ 1, odd_swap(x, RING), x]
            row += [y ^ j ^ a for j in range(RING)] + [z ^ j for j in range(RING)]
            row += [a ^ j for j in range(4)]
            for shard in (s, s + step, s - step, s + 2 * step, s - 2 * step):
                row += [shard * per_shard + i for i in range(per_shard)]
            rows.append(row)
    return np.array(rows, np.int32)


def odd_swap(i, n):
    return (((i + 1) % n ^ 1) - 1) % n


def pick(array, i):
    return lax.dynamic_index_in_dim(array, i, 0, keepdims=False, allow_negative_indices=False)


def after(value, *earlier):
    return lax.optimization_barrier((value, *earlier))[0]


def add_half(own, got):
    return (own.astype(F32) + got.astype(F32)).astype(BF)


def local(video_query, audio_key, audio_value, window_first, window_count, out_weight, cotangent):
    tokens, feature = video_query.shape
    audio_rows = audio_key.shape[0]
    shards = lax.axis_size("vseq")
    device = lax.axis_index("vseq") * 4 + lax.axis_index("aseq")
    pos = pick(jnp.asarray(table(shards, audio_rows // ABLK)), device)
    each = range(shards)
    pa = [(i, i ^ 1) for i in each]
    pb = [(i, odd_swap(i, shards)) for i in each]

    def along(change):
        return [(i, index(*change(*place(i)))) for i in each]

    x_even = along(lambda y, x, z: (y, x ^ 1, z))
    x_odd = along(lambda y, x, z: (y, odd_swap(x, RING), z))

    def exchange(send, even, odd):
        return lax.ppermute(send[0], "vseq", even), lax.ppermute(send[1], "vseq", odd)

    def direct(sends, change):
        return [
            lax.ppermute(send, "vseq", along(functools.partial(change, j + 1)))
            for j, send in enumerate(sends)
        ]

    key_block = pos[AUDIO:]
    first = jnp.repeat(window_first, VBLK)
    end = jnp.repeat(window_first + window_count, VBLK)
    allowed = (key_block[:, None] >= first[None, :]) & (key_block[:, None] < end[None, :])
    bias = jnp.where(allowed, 0.0, -1e30).astype(F32)

    weight_parts = out_weight.reshape(4, feature, feature)
    w0, w1, w2, w3 = [
        pick(weight_parts, pos[WEIGHT + j]) for j in range(4)
    ]
    w_core = jnp.concatenate([w3, w1], 0)
    cot_core = lax.ppermute(cotangent, "aseq", CORE)
    grad_near = dot(cot_core, w1, NN) + dot(cotangent, w0, NN)

    def halo(own, *first):
        by_a = lax.ppermute(own, "vseq", pa)
        by_b = lax.ppermute(own, "vseq", pb)
        by_a, by_b = after((by_a, by_b), *first)
        return own, by_a, by_b, lax.ppermute(by_b, "vseq", pa), lax.ppermute(by_a, "vseq", pb)

    keys = halo(after(audio_key, pos), bias)
    values = halo(audio_value, grad_near, w_core)

    cot_pair = lax.ppermute(after(cotangent, *keys[3:], *values[3:]), "aseq", PAIR)
    att, p, far_core, near, *near_far = forward_call(
        pos, video_query, keys, values, after(bias, grad_near, w2, w3), w_core, (cotangent, cot_core)
    )

    near_got = exchange(near_far, x_even, x_odd)
    cot_pair = after(cot_pair, *near_got)
    cot_both = lax.ppermute(cot_pair, "aseq", CORE)
    got_core = lax.ppermute(after(far_core, cot_pair), "aseq", CORE)
    near_send = beside(pos, near, near_got)
    near_got = exchange(near_send, x_even, x_odd)
    far_pair = (dot(after(att, *near_send), w2, NT) + got_core[:, :feature].astype(F32)).astype(BF)
    got_pair = lax.ppermute(far_pair, "aseq", PAIR)
    more, *more_far = weight_far(pos, cot_pair, after(cot_both, far_pair), att)
    more_got = exchange(more_far, x_even, x_odd)

    def backward(half, cot_both, done):
        return backward_call(
            video_query, keys, values, p, att, grad_near, (cot_pair, cot_both), (w2, w3), half, done
        )

    left = backward(0, after(cot_both, *more_far), ())
    more_send = beside(pos, more, after(more_got, left[0], *near_got))
    more_got = exchange(more_send, x_even, x_odd)
    mixed_video = (
        dot(after(att, *more_send), w0, NT) + got_core[:, feature:].astype(F32) + got_pair.astype(F32)
    ).astype(BF)
    grad_query, g_own, g_a, g_b, g_aa, g_bb = backward(1, after(cot_both, mixed_video), left)
    back_a = lax.ppermute(g_aa, "vseq", pa)
    back_b = lax.ppermute(g_bb, "vseq", pb)

    keep, *sends = rows_of(pos, near, near_got, more, more_got)
    y_got = direct(sends, lambda j, y, x, z: (y ^ j, x, z))

    back_a, back_b = after((back_a, back_b), keep)
    send_b = add_half(g_b, back_a)
    send_a = add_half(g_a, back_b)
    sum_b = lax.ppermute(send_b, "vseq", pb)
    sum_a = lax.ppermute(send_a, "vseq", pa)

    grad_weight, *sends = plane_of(pos, after(keep, send_a, send_b), y_got)
    for got in direct(sends, lambda j, y, x, z: (y, x, z ^ j)):
        grad_weight = grad_weight + got.astype(F32)

    grad_key = g_own[0] + sum_a[0].astype(F32) + sum_b[0].astype(F32)
    grad_value = g_own[1] + sum_a[1].astype(F32) + sum_b[1].astype(F32)
    return mixed_video, grad_query, grad_key, grad_value, grad_weight


def solution(mesh):
    both = P("vseq", "aseq")
    in_specs = (both, both, both, P("vseq"), P("vseq"), P(None, "aseq"), both)
    return jax.shard_map(
        local, mesh=mesh, in_specs=in_specs, out_specs=(both,) * 5, check_vma=False
    )
```

time: 188 us -> 165 us (0.88)
  Pallas kernels: 17.5 us -> 29.8 us
  waiting for transfers between devices: 79 us -> 67 us
  starting transfers between devices: 61.8 us -> 51.1 us
  matrix products: 11.8 us -> 4.49 us
  local copies, waits for them, and re-layouts: 11.3 us -> 7.99 us
    pallas_call x2 -> x8, Pallas kernels: 17.5 us -> 29.8 us  [the longest x2 13.9 us: backward_call(): pl.pallas_call(functools.partial(attend_backward, len(done)), grid=(heads...]
    ppermute x28 -> x27, waiting for transfers between devices: 64.6 us -> 53.1 us  [the longest x4 13.4 us: exchange(): lax.ppermute(send[0], 'vseq', even)]
    dot_general x6 -> x4, matrix products: 11.8 us -> 4.49 us  [dot(): return lax.dot_general(a, b, dims, preferred_element_type=F32)]
    ppermute x28 -> x27, starting transfers between devices: 54.5 us -> 48.6 us  [the longest x2 12 us: halo(): by_b = lax.ppermute(own, 'vseq', pb)]
    ppermute x1, starting transfers between devices: 7.21 us -> 2.02 us  [local(): back_b = lax.ppermute(g_bb, 'vseq', pb)]
    ppermute x1, waiting for transfers between devices: 10.6 us -> 6.3 us  [local(): back_b = lax.ppermute(g_bb, 'vseq', pb)]
    ppermute x1, waiting for transfers between devices: 3.84 us -> 7.61 us  [local(): back_a = lax.ppermute(g_aa, 'vseq', pa)]
    squeeze x2 -> x1, local copies, waits for them, and re-layouts: 5.59 us -> 4.7 us  [pick(): lax.dynamic_index_in_dim(array, i, 0, keepdims=False, allow_negative_indi...]
  transfers between devices with their start and end apart: 32 -> 31, of which waited for: 16 -> 22; matrix products, arithmetic and copies ran while one was open for 14% -> 8% of each run, Pallas kernels for 9% -> 18%
where the time goes in v2:
time: 165 us
  waiting for transfers between devices  67 us (41%)
  starting transfers between devices  51.1 us (31%)
  Pallas kernels  29.8 us (18%)
  local copies, waits for them, and re-layouts  7.99 us (5%)
  matrix products  4.49 us (3%)
  other arithmetic  3.93 us (2%)
    pallas_call x2, Pallas kernels, backward_call(): pl.pallas_call(functools.partial(attend_backward, len(done)), grid=(heads...  13.9 us
    ppermute x4, waiting for transfers between devices, exchange(): lax.ppermute(send[0], 'vseq', even)  13.4 us
    ppermute x2, starting transfers between devices, halo(): by_b = lax.ppermute(own, 'vseq', pb)  12 us
    ppermute x6, starting transfers between devices, direct(): lax.ppermute(send, 'vseq', along(functools.partial(change, j + 1)))  11.3 us
    ppermute x6, waiting for transfers between devices, direct(): lax.ppermute(send, 'vseq', along(functools.partial(change, j + 1)))  11.2 us
    pallas_call x1, Pallas kernels, forward_call(): call(attend_forward, (heads,), (pos,), [by_head] + [kv_head] * 10 + [whol...  10.2 us
    ppermute x2, starting transfers between devices, halo(): lax.ppermute(by_a, 'vseq', pb)  9.46 us
    ppermute x1, waiting for transfers between devices, local(): sum_b = lax.ppermute(send_b, 'vseq', pb)  8.45 us
  transfers between devices with their start and end apart: 31, of which 22 were waited for; matrix products, arithmetic and copies ran while one was open for 8% of the time, Pallas kernels for 18%

profile of v2, /device:TPU:32, one launch (start us, length us, event | category | flops | bytes accessed | tf_op | source)
XLA Modules:
  0.0 165.2 jit_solution(12073254266566923609)
XLA Ops:
  1.3 10.0 %collective-permute-start.1 = (bf16[128,768]{1,0:T(8,128)(2,1)}, bf16[128,768]{1,0:T(8,128)(2,1)S(1)}, u32[]{:S(2)}, u32[]{:S(2)}) collective-permute-start(bf16[128,768]{1,0:T(8,128)(2,1)} %k0.2), channel_id=1, source_target_pairs={{0,252},{4,8},{8,4},{12,16},{16,12},{20,24},{24,20},{28,32},{32,28... | collective-permute-start | bytes 589832 | tf_op jit(solution)/shard_map/ppermute | solution.py:369
  11.4 2.0 %collective-permute-start.5 = (bf16[128,768]{1,0:T(8,128)(2,1)}, bf16[128,768]{1,0:T(8,128)(2,1)S(1)}, u32[]{:S(2)}, u32[]{:S(2)}) collective-permute-start(bf16[128,768]{1,0:T(8,128)(2,1)} %v0.5), channel_id=1, source_target_pairs={{0,252},{4,8},{8,4},{12,16},{16,12},{20,24},{24,20},{28,32},{32,28... | collective-permute-start | bytes 589832 | tf_op jit(solution)/shard_map/ppermute | solution.py:369
  16.4 4.7 %dynamic-slice_bitcast_fusion = (bf16[768,768]{1,0:T(8,128)(2,1)S(1)}, bf16[768,768]{1,0:T(8,128)(2,1)S(1)}, bf16[768,768]{1,0:T(8,128)(2,1)S(1)}) fusion(bf16[4,768,768]{2,1,0:T(8,128)(2,1)} %bitcast.36, s32[]{:T(128)} %bitcast.12, s32[]{:T(128)} %bitcast.10, s32[]{:T(128)} %bitcast.5), kind=kLoop, calls=%fused_computation.8 | loop fusion | bytes 7077900 | tf_op jit(solution)/shard_map/jit(dynamic_index_in_dim)/squeeze | solution.py:317
  21.1 1.4 fusion.2
  23.5 1.7 %collective-permute-done.k1 = bf16[128,768]{1,0:T(8,128)(2,1)S(1)} collective-permute-done((bf16[128,768]{1,0:T(8,128)(2,1)}, bf16[128,768]{1,0:T(8,128)(2,1)S(1)}, u32[]{:S(2)}, u32[]{:S(2)}) %collective-permute-start) | collective-permute-done | bytes 196640 | tf_op jit(solution)/shard_map/ppermute | solution.py:368
  25.2 7.2 %collective-permute-start.3 = (bf16[128,768]{1,0:T(8,128)(2,1)S(1)}, bf16[128,768]{1,0:T(8,128)(2,1)S(1)}, u32[]{:S(2)}, u32[]{:S(2)}) collective-permute-start(bf16[128,768]{1,0:T(8,128)(2,1)S(1)} %collective-permute-done.k1), channel_id=1, source_target_pairs={{0,252},{4,8},{8,4},{12,16},{16,12},{20,24},{24,20},{28,32},{32,28... | collective-permute-start | bytes 589832 | tf_op jit(solution)/shard_map/ppermute | solution.py:371
  33.2 2.3 %collective-permute-start.8 = (bf16[128,768]{1,0:T(8,128)(2,1)S(1)}, bf16[128,768]{1,0:T(8,128)(2,1)S(1)}, u32[]{:S(2)}, u32[]{:S(2)}) collective-permute-start(bf16[128,768]{1,0:T(8,128)(2,1)S(1)} %collective-permute-done.4.v1), channel_id=1, source_target_pairs={{0,252},{4,8},{8,4},{12,16},{16,12},{20,24},{24,20},{28,32},{32,28... | collective-permute-start | bytes 589832 | tf_op jit(solution)/shard_map/ppermute | solution.py:371
  36.3 5.3 %collective-permute-done.3.k4 = bf16[128,768]{1,0:T(8,128)(2,1)S(1)} collective-permute-done((bf16[128,768]{1,0:T(8,128)(2,1)S(1)}, bf16[128,768]{1,0:T(8,128)(2,1)S(1)}, u32[]{:S(2)}, u32[]{:S(2)}) %collective-permute-start.3) | collective-permute-done | bytes 196640 | tf_op jit(solution)/shard_map/ppermute | solution.py:371
  41.5 2.6 %collective-permute-done.2.k3 = bf16[128,768]{1,0:T(8,128)(2,1)S(1)} collective-permute-done((bf16[128,768]{1,0:T(8,128)(2,1)S(1)}, bf16[128,768]{1,0:T(8,128)(2,1)S(1)}, u32[]{:S(2)}, u32[]{:S(2)}) %collective-permute-start.2) | collective-permute-done | bytes 196640 | tf_op jit(solution)/shard_map/ppermute | solution.py:371
  44.1 1.6 collective-permute-done.8.v4
  46.9 5.9 %collective-permute-start.9 = (bf16[512,768]{1,0:T(8,128)(2,1)S(1)}, bf16[512,768]{1,0:T(8,128)(2,1)S(1)}, u32[]{:S(2)}, u32[]{:S(2)}) collective-permute-start(bf16[512,768]{1,0:T(8,128)(2,1)S(1)} %copy-done.3), channel_id=1, source_target_pairs={{0,2},{1,3},{2,0},{3,1},{4,6},{5,7},{6,4},{7,5},{8,10},{9,11},{10,... | collective-permute-start | bytes 2359304 | tf_op jit(solution)/shard_map/ppermute | solution.py:376
  52.8 10.2 %attend_forward.1 = (bf16[512,768]{1,0:T(8,128)(2,1)S(1)}, bf16[6,640,512]{2,1,0:T(8,128)(2,1)S(1)}, bf16[512,1536]{1,0:T(8,128)(2,1)S(1)}, bf16[2,4,192,768]{3,...) custom-call(s32[36]{0:T(128)S(1)} %get-tuple-element.115.pos, ...), custom_call_target="tpu_custom_call" | custom-call | flops 2013265920 | tf_op jit(solution)/shard_map/attend_forward/pallas_call | solution.py:233
  63.2 8.5 %collective-permute-done.10.got_even = bf16[192,768]{1,0:T(8,128)(2,1)S(1)} collective-permute-done((bf16[192,768]{1,0:T(8,128)(2,1)S(1)}, bf16[192,768]{1,0:T(8,128)(2,1)S(1)}, u32[]{:S(2)}, u32[]{:S(2)}) %collective-permute-start.10) | collective-permute-done | bytes 294944 | tf_op jit(solution)/shard_map/ppermute | solution.py:345
  78.8 2.0 %weight_far.1 = (bf16[2,4,192,768]{3,2,1,0:T(8,128)(2,1)S(1)}, bf16[192,768]{1,0:T(8,128)(2,1)S(1)}, bf16[192,768]{1,0:T(8,128)(2,1)S(1)}) custom-call(s32[36]{0:T(128)S(1)} %get-tuple-element.115.pos, bf16[512,768]{1,0:T(8,128)(2,1)S(1)} %collective-permute-done.9.l0.c0, bf16[512,768]{1,0:T(8,128)(2,1)S(1)} %collective-permute-done.12.l1.c1, ...), custom_call_target="tpu_custom_call" | custom-call | tf_op jit(solution)/shard_map/weight_far/pallas_call | solution.py:135
  81.3 2.1 %collective-permute-start.15 = (bf16[192,768]{1,0:T(8,128)(2,1)S(1)}, bf16[192,768]{1,0:T(8,128)(2,1)S(1)}, u32[]{:S(2)}, u32[]{:S(2)}) collective-permute-start(bf16[192,768]{1,0:T(8,128)(2,1)S(1)} %get-tuple-element.77), channel_id=1, source_target_pairs={{0,48},{4,52},{8,56},{12,60},{16,32},{20,36},{24,40},{28,44},{32,1... | collective-permute-start | bytes 884744 | tf_op jit(solution)/shard_map/ppermute | solution.py:345
  83.5 7.0 %attend_backward.2 = (f32[512,768]{1,0:T(8,128)}, f32[2,128,768]{2,1,0:T(8,128)S(1)}, f32[2,128,768]{2,1,0:T(8,128)S(1)}, f32[2,128,768]{2,1,0:T(8,128)S(1)}, bf...) custom-call(bf16[512,768]{1,0:T(8,128)(2,1)S(1)} %copy-done, bf16[128,768]{1,0:T(8,128)(2,1)S(1)} %copy-done.1, ...), custom_call_target="tpu_custom_call" | custom-call | flops 1509949440 | tf_op jit(solution)/shard_map/attend_backward/pallas_call | solution.py:264
  90.5 1.7 %collective-permute-done.17.near_odd = bf16[2,192,768]{2,1,0:T(8,128)(2,1)S(1)} collective-permute-done((bf16[2,192,768]{2,1,0:T(8,128)(2,1)S(1)}, bf16[2,192,768]{2,1,0:T(8,128)(2,1)S(1)}, u32[]{:S(2)}, u32[]{:S(2)}) %collective-permute-start.17) | collective-permute-done | bytes 589856 | tf_op jit(solution)/shard_map/ppermute | solution.py:345
  92.2 3.7 %collective-permute-done.14.got_even = bf16[192,768]{1,0:T(8,128)(2,1)S(1)} collective-permute-done((bf16[192,768]{1,0:T(8,128)(2,1)S(1)}, bf16[192,768]{1,0:T(8,128)(2,1)S(1)}, u32[]{:S(2)}, u32[]{:S(2)}) %collective-permute-start.14) | collective-permute-done | bytes 294944 | tf_op jit(solution)/shard_map/ppermute | solution.py:345
  99.3 1.5 fusion
  102.0 6.9 %attend_backward.3 = (f32[512,768]{1,0:T(8,128)}, f32[2,128,768]{2,1,0:T(8,128)S(1)}, f32[2,128,768]{2,1,0:T(8,128)S(1)}, f32[2,128,768]{2,1,0:T(8,128)S(1)}, bf...) custom-call(bf16[512,768]{1,0:T(8,128)(2,1)S(1)} %copy-done, ...), custom_call_target="tpu_custom_call", output_to_operand_aliasing={{0}: (18, {}), {1}: (19, {}), {2}: (20, {}), {3}: (21, {}),... | custom-call | flops 1509949440 | tf_op jit(solution)/shard_map/attend_backward/pallas_call | solution.py:264
  108.9 2.0 %collective-permute-start.20 = (bf16[2,128,768]{2,1,0:T(8,128)(2,1)S(1)}, bf16[2,128,768]{2,1,0:T(8,128)(2,1)S(1)}, u32[]{:S(2)}, u32[]{:S(2)}) collective-permute-start(bf16[2,128,768]{2,1,0:T(8,128)(2,1)S(1)} %get-tuple-element.96), channel_id=1, source_target_pairs={{0,252},{4,8},{8,4},{12,16},{16,12},{20,24},{24,20},{28,32},{32,28... | collective-permute-start | bytes 1179656 | tf_op jit(solution)/shard_map/ppermute | solution.py:405
  112.1 2.0 %collective-permute-done.22.more_odd = bf16[2,192,768]{2,1,0:T(8,128)(2,1)S(1)} collective-permute-done((bf16[2,192,768]{2,1,0:T(8,128)(2,1)S(1)}, bf16[2,192,768]{2,1,0:T(8,128)(2,1)S(1)}, u32[]{:S(2)}, u32[]{:S(2)}) %collective-permute-start.22) | collective-permute-done | bytes 589856 | tf_op jit(solution)/shard_map/ppermute | solution.py:345
  114.1 1.4 rows.1
  115.7 4.6 %collective-permute-start.27 = (bf16[192,768]{1,0:T(8,128)(2,1)S(1)}, bf16[192,768]{1,0:T(8,128)(2,1)S(1)}, u32[]{:S(2)}, u32[]{:S(2)}) collective-permute-start(bf16[192,768]{1,0:T(8,128)(2,1)S(1)} %get-tuple-element.104), channel_id=1, source_target_pairs={{0,192},{4,196},{8,200},{12,204},{16,208},{20,212},{24,216},{28,22... | collective-permute-start | bytes 884744 | tf_op jit(solution)/shard_map/ppermute | solution.py:349
  120.3 7.6 %collective-permute-done.19 = bf16[2,128,768]{2,1,0:T(8,128)(2,1)S(1)} collective-permute-done((bf16[2,128,768]{2,1,0:T(8,128)(2,1)S(1)}, bf16[2,128,768]{2,1,0:T(8,128)(2,1)S(1)}, u32[]{:S(2)}, u32[]{:S(2)}) %collective-permute-start.19) | collective-permute-done | bytes 393248 | tf_op jit(solution)/shard_map/ppermute | solution.py:404
  127.9 6.3 %collective-permute-done.20 = bf16[2,128,768]{2,1,0:T(8,128)(2,1)S(1)} collective-permute-done((bf16[2,128,768]{2,1,0:T(8,128)(2,1)S(1)}, bf16[2,128,768]{2,1,0:T(8,128)(2,1)S(1)}, u32[]{:S(2)}, u32[]{:S(2)}) %collective-permute-start.20) | collective-permute-done | bytes 393248 | tf_op jit(solution)/shard_map/ppermute | solution.py:405
  135.0 1.4 collective-permute-start.24
  136.6 2.4 %collective-permute-done.27.g3 = bf16[192,768]{1,0:T(8,128)(2,1)S(1)} collective-permute-done((bf16[192,768]{1,0:T(8,128)(2,1)S(1)}, bf16[192,768]{1,0:T(8,128)(2,1)S(1)}, u32[]{:S(2)}, u32[]{:S(2)}) %collective-permute-start.27) | collective-permute-done | bytes 294944 | tf_op jit(solution)/shard_map/ppermute | solution.py:349
  139.9 2.1 %collective-permute-start.29 = (bf16[48,768]{1,0:T(8,128)(2,1)S(1)}, bf16[48,768]{1,0:T(8,128)(2,1)S(1)}, u32[]{:S(2)}, u32[]{:S(2)}) collective-permute-start(bf16[48,768]{1,0:T(8,128)(2,1)S(1)} %get-tuple-element.107), channel_id=1, source_target_pairs={{0,8},{4,12},{8,0},{12,4},{16,24},{20,28},{24,16},{28,20},{32,40},... | collective-permute-start | bytes 221192 | tf_op jit(solution)/shard_map/ppermute | solution.py:349
  142.0 4.4 %collective-permute-start.30 = (bf16[48,768]{1,0:T(8,128)(2,1)S(1)}, bf16[48,768]{1,0:T(8,128)(2,1)S(1)}, u32[]{:S(2)}, u32[]{:S(2)}) collective-permute-start(bf16[48,768]{1,0:T(8,128)(2,1)S(1)} %get-tuple-element.108), channel_id=1, source_target_pairs={{0,12},{4,8},{8,4},{12,0},{16,28},{20,24},{24,20},{28,16},{32,44},... | collective-permute-start | bytes 221192 | tf_op jit(solution)/shard_map/ppermute | solution.py:349
  146.4 7.9 %collective-permute-done.28 = bf16[48,768]{1,0:T(8,128)(2,1)S(1)} collective-permute-done((bf16[48,768]{1,0:T(8,128)(2,1)S(1)}, bf16[48,768]{1,0:T(8,128)(2,1)S(1)}, u32[]{:S(2)}, u32[]{:S(2)}) %collective-permute-start.28) | collective-permute-done | bytes 73760 | tf_op jit(solution)/shard_map/ppermute | solution.py:349
  155.7 8.4 %collective-permute-done.24 = bf16[2,128,768]{2,1,0:T(8,128)(2,1)S(1)} collective-permute-done((bf16[2,128,768]{2,1,0:T(8,128)(2,1)S(1)}, bf16[2,128,768]{2,1,0:T(8,128)(2,1)S(1)}, u32[]{:S(2)}, u32[]{:S(2)}) %collective-permute-start.24) | collective-permute-done | bytes 393248 | tf_op jit(solution)/shard_map/ppermute | solution.py:413
  (69 shorter events, 25.5 us)
Async XLA Ops:
  1.3 22.1 %collective-permute-start.1 = (bf16[128,768]{1,0:T(8,128)(2,1)}, bf16[128,768]{1,0:T(8,128)(2,1)S(1)}, u32[]{:S(2)}, u32[]{:S(2)}) collective-permute-start(bf16[128,768]{1,0:T(8,128)(2,1)} %k0.2), channel_id=1, source_target_pairs={{0,252},{4,8},{8,4},{12,16},{16,12},{20,24},{24,20},{28,32},{32,28... | collective-permute-start | bytes 589832 | tf_op jit(solution)/shard_map/ppermute | solution.py:369
  11.4 13.8 %collective-permute-start = (bf16[128,768]{1,0:T(8,128)(2,1)}, bf16[128,768]{1,0:T(8,128)(2,1)S(1)}, u32[]{:S(2)}, u32[]{:S(2)}) collective-permute-start(bf16[128,768]{1,0:T(8,128)(2,1)} %k0.2), channel_id=1, source_target_pairs={{0,4},{4,0},{8,12},{12,8},{16,20},{20,16},{24,28},{28,24},{32,36},... | collective-permute-start | bytes 589832 | tf_op jit(solution)/shard_map/ppermute | solution.py:368
  11.4 21.8 %collective-permute-start.5 = (bf16[128,768]{1,0:T(8,128)(2,1)}, bf16[128,768]{1,0:T(8,128)(2,1)S(1)}, u32[]{:S(2)}, u32[]{:S(2)}) collective-permute-start(bf16[128,768]{1,0:T(8,128)(2,1)} %v0.5), channel_id=1, source_target_pairs={{0,252},{4,8},{8,4},{12,16},{16,12},{20,24},{24,20},{28,32},{32,28... | collective-permute-start | bytes 589832 | tf_op jit(solution)/shard_map/ppermute | solution.py:369
  13.4 19.8 %collective-permute-start.4 = (bf16[128,768]{1,0:T(8,128)(2,1)}, bf16[128,768]{1,0:T(8,128)(2,1)S(1)}, u32[]{:S(2)}, u32[]{:S(2)}) collective-permute-start(bf16[128,768]{1,0:T(8,128)(2,1)} %v0.5), channel_id=1, source_target_pairs={{0,4},{4,0},{8,12},{12,8},{16,20},{20,16},{24,28},{28,24},{32,36},... | collective-permute-start | bytes 589832 | tf_op jit(solution)/shard_map/ppermute | solution.py:368
  14.3 18.0 %collective-permute-start.6 = (bf16[512,768]{1,0:T(8,128)(2,1)}, bf16[512,768]{1,0:T(8,128)(2,1)S(1)}, u32[]{:S(2)}, u32[]{:S(2)}) collective-permute-start(bf16[512,768]{1,0:T(8,128)(2,1)} %l0.1), channel_id=1, source_target_pairs={{0,1},{1,0},{2,3},{3,2},{4,5},{5,4},{6,7},{7,6},{8,9},{9,8},{10,11... | collective-permute-start | bytes 2359304 | tf_op jit(solution)/shard_map/ppermute | solution.py:364
  22.8 30.0 %copy-start = (bf16[512,768]{1,0:T(8,128)(2,1)S(1)}, bf16[512,768]{1,0:T(8,128)(2,1)}, u32[]{:S(2)}) copy-start(bf16[512,768]{1,0:T(8,128)(2,1)} %q_ref.5) | copy-start | bytes 2359300
  25.2 16.4 %collective-permute-start.3 = (bf16[128,768]{1,0:T(8,128)(2,1)S(1)}, bf16[128,768]{1,0:T(8,128)(2,1)S(1)}, u32[]{:S(2)}, u32[]{:S(2)}) collective-permute-start(bf16[128,768]{1,0:T(8,128)(2,1)S(1)} %collective-permute-done.k1), channel_id=1, source_target_pairs={{0,252},{4,8},{8,4},{12,16},{16,12},{20,24},{24,20},{28,32},{32,28... | collective-permute-start | bytes 589832 | tf_op jit(solution)/shard_map/ppermute | solution.py:371
  32.3 11.8 %collective-permute-start.2 = (bf16[128,768]{1,0:T(8,128)(2,1)S(1)}, bf16[128,768]{1,0:T(8,128)(2,1)S(1)}, u32[]{:S(2)}, u32[]{:S(2)}) collective-permute-start(bf16[128,768]{1,0:T(8,128)(2,1)S(1)} %collective-permute-done.1.k2), channel_id=1, source_target_pairs={{0,4},{4,0},{8,12},{12,8},{16,20},{20,16},{24,28},{28,24},{32,36},... | collective-permute-start | bytes 589832 | tf_op jit(solution)/shard_map/ppermute | solution.py:371
  33.2 12.6 %collective-permute-start.8 = (bf16[128,768]{1,0:T(8,128)(2,1)S(1)}, bf16[128,768]{1,0:T(8,128)(2,1)S(1)}, u32[]{:S(2)}, u32[]{:S(2)}) collective-permute-start(bf16[128,768]{1,0:T(8,128)(2,1)S(1)} %collective-permute-done.4.v1), channel_id=1, source_target_pairs={{0,252},{4,8},{8,4},{12,16},{16,12},{20,24},{24,20},{28,32},{32,28... | collective-permute-start | bytes 589832 | tf_op jit(solution)/shard_map/ppermute | solution.py:371
  35.4 11.4 %collective-permute-start.7 = (bf16[128,768]{1,0:T(8,128)(2,1)S(1)}, bf16[128,768]{1,0:T(8,128)(2,1)S(1)}, u32[]{:S(2)}, u32[]{:S(2)}) collective-permute-start(bf16[128,768]{1,0:T(8,128)(2,1)S(1)} %collective-permute-done.5.v2), channel_id=1, source_target_pairs={{0,4},{4,0},{8,12},{12,8},{16,20},{20,16},{24,28},{28,24},{32,36},... | collective-permute-start | bytes 589832 | tf_op jit(solution)/shard_map/ppermute | solution.py:371
  46.9 26.1 %collective-permute-start.9 = (bf16[512,768]{1,0:T(8,128)(2,1)S(1)}, bf16[512,768]{1,0:T(8,128)(2,1)S(1)}, u32[]{:S(2)}, u32[]{:S(2)}) collective-permute-start(bf16[512,768]{1,0:T(8,128)(2,1)S(1)} %copy-done.3), channel_id=1, source_target_pairs={{0,2},{1,3},{2,0},{3,1},{4,6},{5,7},{6,4},{7,5},{8,10},{9,11},{10,... | collective-permute-start | bytes 2359304 | tf_op jit(solution)/shard_map/ppermute | solution.py:376
  63.0 8.7 %collective-permute-start.10 = (bf16[192,768]{1,0:T(8,128)(2,1)S(1)}, bf16[192,768]{1,0:T(8,128)(2,1)S(1)}, u32[]{:S(2)}, u32[]{:S(2)}) collective-permute-start(bf16[192,768]{1,0:T(8,128)(2,1)S(1)} %get-tuple-element.65), channel_id=1, source_target_pairs={{0,16},{4,20},{8,24},{12,28},{16,0},{20,4},{24,8},{28,12},{32,48},... | collective-permute-start | bytes 884744 | tf_op jit(solution)/shard_map/ppermute | solution.py:345
  63.1 9.9 %collective-permute-start.11 = (bf16[192,768]{1,0:T(8,128)(2,1)S(1)}, bf16[192,768]{1,0:T(8,128)(2,1)S(1)}, u32[]{:S(2)}, u32[]{:S(2)}) collective-permute-start(bf16[192,768]{1,0:T(8,128)(2,1)S(1)} %get-tuple-element.66), channel_id=1, source_target_pairs={{0,48},{4,52},{8,56},{12,60},{16,32},{20,36},{24,40},{28,44},{32,1... | collective-permute-start | bytes 884744 | tf_op jit(solution)/shard_map/ppermute | solution.py:345
  73.0 3.4 %collective-permute-start.13 = (bf16[512,1536]{1,0:T(8,128)(2,1)S(1)}, bf16[512,1536]{1,0:T(8,128)(2,1)S(1)}, u32[]{:S(2)}, u32[]{:S(2)}) collective-permute-start(bf16[512,1536]{1,0:T(8,128)(2,1)S(1)} %get-tuple-element.73), channel_id=1, source_target_pairs={{0,1},{1,0},{2,3},{3,2},{4,5},{5,4},{6,7},{7,6},{8,9},{9,8},{10,11... | collective-permute-start | bytes 4718600 | tf_op jit(solution)/shard_map/ppermute | solution.py:384
  73.0 5.8 %collective-permute-start.12 = (bf16[512,768]{1,0:T(8,128)(2,1)S(1)}, bf16[512,768]{1,0:T(8,128)(2,1)S(1)}, u32[]{:S(2)}, u32[]{:S(2)}) collective-permute-start(bf16[512,768]{1,0:T(8,128)(2,1)S(1)} %collective-permute-done.9.l0.c0), channel_id=1, source_target_pairs={{0,1},{1,0},{2,3},{3,2},{4,5},{5,4},{6,7},{7,6},{8,9},{9,8},{10,11... | collective-permute-start | bytes 2359304 | tf_op jit(solution)/shard_map/ppermute | solution.py:383
  74.2 16.3 %collective-permute-start.16 = (bf16[2,192,768]{2,1,0:T(8,128)(2,1)S(1)}, bf16[2,192,768]{2,1,0:T(8,128)(2,1)S(1)}, u32[]{:S(2)}, u32[]{:S(2)}) collective-permute-start(bf16[2,192,768]{2,1,0:T(8,128)(2,1)S(1)} %get-tuple-element.69), channel_id=1, source_target_pairs={{0,16},{4,20},{8,24},{12,28},{16,0},{20,4},{24,8},{28,12},{32,48},... | collective-permute-start | bytes 1769480 | tf_op jit(solution)/shard_map/ppermute | solution.py:345
  74.8 17.4 %collective-permute-start.17 = (bf16[2,192,768]{2,1,0:T(8,128)(2,1)S(1)}, bf16[2,192,768]{2,1,0:T(8,128)(2,1)S(1)}, u32[]{:S(2)}, u32[]{:S(2)}) collective-permute-start(bf16[2,192,768]{2,1,0:T(8,128)(2,1)S(1)} %get-tuple-element.70), channel_id=1, source_target_pairs={{0,48},{4,52},{8,56},{12,60},{16,32},{20,36},{24,40},{28,44},{32,1... | collective-permute-start | bytes 1769480 | tf_op jit(solution)/shard_map/ppermute | solution.py:345
  78.4 22.4 %collective-permute-start.18 = (bf16[512,768]{1,0:T(8,128)(2,1)S(1)}, bf16[512,768]{1,0:T(8,128)(2,1)S(1)}, u32[]{:S(2)}, u32[]{:S(2)}) collective-permute-start(bf16[512,768]{1,0:T(8,128)(2,1)S(1)} %add_convert_fusion.1), channel_id=1, source_target_pairs={{0,2},{1,3},{2,0},{3,1},{4,6},{5,7},{6,4},{7,5},{8,10},{9,11},{10,... | collective-permute-start | bytes 2359304 | tf_op jit(solution)/shard_map/ppermute | solution.py:388
  80.8 15.1 %collective-permute-start.14 = (bf16[192,768]{1,0:T(8,128)(2,1)S(1)}, bf16[192,768]{1,0:T(8,128)(2,1)S(1)}, u32[]{:S(2)}, u32[]{:S(2)}) collective-permute-start(bf16[192,768]{1,0:T(8,128)(2,1)S(1)} %get-tuple-element.76), channel_id=1, source_target_pairs={{0,16},{4,20},{8,24},{12,28},{16,0},{20,4},{24,8},{28,12},{32,48},... | collective-permute-start | bytes 884744 | tf_op jit(solution)/shard_map/ppermute | solution.py:345
  81.3 15.9 %collective-permute-start.15 = (bf16[192,768]{1,0:T(8,128)(2,1)S(1)}, bf16[192,768]{1,0:T(8,128)(2,1)S(1)}, u32[]{:S(2)}, u32[]{:S(2)}) collective-permute-start(bf16[192,768]{1,0:T(8,128)(2,1)S(1)} %get-tuple-element.77), channel_id=1, source_target_pairs={{0,48},{4,52},{8,56},{12,60},{16,32},{20,36},{24,40},{28,44},{32,1... | collective-permute-start | bytes 884744 | tf_op jit(solution)/shard_map/ppermute | solution.py:345
  98.0 14.2 %collective-permute-start.21 = (bf16[2,192,768]{2,1,0:T(8,128)(2,1)S(1)}, bf16[2,192,768]{2,1,0:T(8,128)(2,1)S(1)}, u32[]{:S(2)}, u32[]{:S(2)}) collective-permute-start(bf16[2,192,768]{2,1,0:T(8,128)(2,1)S(1)} %get-tuple-element.83), channel_id=1, source_target_pairs={{0,16},{4,20},{8,24},{12,28},{16,0},{20,4},{24,8},{28,12},{32,48},... | collective-permute-start | bytes 1769480 | tf_op jit(solution)/shard_map/ppermute | solution.py:345
  98.4 15.6 %collective-permute-start.22 = (bf16[2,192,768]{2,1,0:T(8,128)(2,1)S(1)}, bf16[2,192,768]{2,1,0:T(8,128)(2,1)S(1)}, u32[]{:S(2)}, u32[]{:S(2)}) collective-permute-start(bf16[2,192,768]{2,1,0:T(8,128)(2,1)S(1)} %get-tuple-element.84), channel_id=1, source_target_pairs={{0,48},{4,52},{8,56},{12,60},{16,32},{20,36},{24,40},{28,44},{32,1... | collective-permute-start | bytes 1769480 | tf_op jit(solution)/shard_map/ppermute | solution.py:345
  108.9 19.0 %collective-permute-start.19 = (bf16[2,128,768]{2,1,0:T(8,128)(2,1)S(1)}, bf16[2,128,768]{2,1,0:T(8,128)(2,1)S(1)}, u32[]{:S(2)}, u32[]{:S(2)}) collective-permute-start(bf16[2,128,768]{2,1,0:T(8,128)(2,1)S(1)} %get-tuple-element.95), channel_id=1, source_target_pairs={{0,4},{4,0},{8,12},{12,8},{16,20},{20,16},{24,28},{28,24},{32,36},... | collective-permute-start | bytes 1179656 | tf_op jit(solution)/shard_map/ppermute | solution.py:404
  108.9 25.3 %collective-permute-start.20 = (bf16[2,128,768]{2,1,0:T(8,128)(2,1)S(1)}, bf16[2,128,768]{2,1,0:T(8,128)(2,1)S(1)}, u32[]{:S(2)}, u32[]{:S(2)}) collective-permute-start(bf16[2,128,768]{2,1,0:T(8,128)(2,1)S(1)} %get-tuple-element.96), channel_id=1, source_target_pairs={{0,252},{4,8},{8,4},{12,16},{16,12},{20,24},{24,20},{28,32},{32,28... | collective-permute-start | bytes 1179656 | tf_op jit(solution)/shard_map/ppermute | solution.py:405
  115.5 20.9 %collective-permute-start.25 = (bf16[192,768]{1,0:T(8,128)(2,1)S(1)}, bf16[192,768]{1,0:T(8,128)(2,1)S(1)}, u32[]{:S(2)}, u32[]{:S(2)}) collective-permute-start(bf16[192,768]{1,0:T(8,128)(2,1)S(1)} %get-tuple-element.102), channel_id=1, source_target_pairs={{0,64},{4,68},{8,72},{12,76},{16,80},{20,84},{24,88},{28,92},{32,9... | collective-permute-start | bytes 884744 | tf_op jit(solution)/shard_map/ppermute | solution.py:349
  115.6 21.0 %collective-permute-start.26 = (bf16[192,768]{1,0:T(8,128)(2,1)S(1)}, bf16[192,768]{1,0:T(8,128)(2,1)S(1)}, u32[]{:S(2)}, u32[]{:S(2)}) collective-permute-start(bf16[192,768]{1,0:T(8,128)(2,1)S(1)} %get-tuple-element.103), channel_id=1, source_target_pairs={{0,128},{4,132},{8,136},{12,140},{16,144},{20,148},{24,152},{28,15... | collective-permute-start | bytes 884744 | tf_op jit(solution)/shard_map/ppermute | solution.py:349
  115.7 23.3 %collective-permute-start.27 = (bf16[192,768]{1,0:T(8,128)(2,1)S(1)}, bf16[192,768]{1,0:T(8,128)(2,1)S(1)}, u32[]{:S(2)}, u32[]{:S(2)}) collective-permute-start(bf16[192,768]{1,0:T(8,128)(2,1)S(1)} %get-tuple-element.104), channel_id=1, source_target_pairs={{0,192},{4,196},{8,200},{12,204},{16,208},{20,212},{24,216},{28,22... | collective-permute-start | bytes 884744 | tf_op jit(solution)/shard_map/ppermute | solution.py:349
  134.3 21.5 %collective-permute-start.23 = (bf16[2,128,768]{2,1,0:T(8,128)(2,1)S(1)}, bf16[2,128,768]{2,1,0:T(8,128)(2,1)S(1)}, u32[]{:S(2)}, u32[]{:S(2)}) collective-permute-start(bf16[2,128,768]{2,1,0:T(8,128)(2,1)S(1)} %add_convert_fusion.3), channel_id=1, source_target_pairs={{0,4},{4,0},{8,12},{12,8},{16,20},{20,16},{24,28},{28,24},{32,36},... | collective-permute-start | bytes 1179656 | tf_op jit(solution)/shard_map/ppermute | solution.py:414
  135.0 29.2 %collective-permute-start.24 = (bf16[2,128,768]{2,1,0:T(8,128)(2,1)S(1)}, bf16[2,128,768]{2,1,0:T(8,128)(2,1)S(1)}, u32[]{:S(2)}, u32[]{:S(2)}) collective-permute-start(bf16[2,128,768]{2,1,0:T(8,128)(2,1)S(1)} %add_convert_fusion.2), channel_id=1, source_target_pairs={{0,252},{4,8},{8,4},{12,16},{16,12},{20,24},{24,20},{28,32},{32,28... | collective-permute-start | bytes 1179656 | tf_op jit(solution)/shard_map/ppermute | solution.py:413
  139.8 14.5 %collective-permute-start.28 = (bf16[48,768]{1,0:T(8,128)(2,1)S(1)}, bf16[48,768]{1,0:T(8,128)(2,1)S(1)}, u32[]{:S(2)}, u32[]{:S(2)}) collective-permute-start(bf16[48,768]{1,0:T(8,128)(2,1)S(1)} %get-tuple-element.106), channel_id=1, source_target_pairs={{0,4},{4,0},{8,12},{12,8},{16,20},{20,16},{24,28},{28,24},{32,36},... | collective-permute-start | bytes 221192 | tf_op jit(solution)/shard_map/ppermute | solution.py:349
  139.9 15.1 %collective-permute-start.29 = (bf16[48,768]{1,0:T(8,128)(2,1)S(1)}, bf16[48,768]{1,0:T(8,128)(2,1)S(1)}, u32[]{:S(2)}, u32[]{:S(2)}) collective-permute-start(bf16[48,768]{1,0:T(8,128)(2,1)S(1)} %get-tuple-element.107), channel_id=1, source_target_pairs={{0,8},{4,12},{8,0},{12,4},{16,24},{20,28},{24,16},{28,20},{32,40},... | collective-permute-start | bytes 221192 | tf_op jit(solution)/shard_map/ppermute | solution.py:349
  142.0 13.0 %collective-permute-start.30 = (bf16[48,768]{1,0:T(8,128)(2,1)S(1)}, bf16[48,768]{1,0:T(8,128)(2,1)S(1)}, u32[]{:S(2)}, u32[]{:S(2)}) collective-permute-start(bf16[48,768]{1,0:T(8,128)(2,1)S(1)} %get-tuple-element.108), channel_id=1, source_target_pairs={{0,12},{4,8},{8,4},{12,0},{16,28},{20,24},{24,20},{28,16},{32,44},... | collective-permute-start | bytes 221192 | tf_op jit(solution)/shard_map/ppermute | solution.py:349
  (6 other events, 72.9 us)

commit v3 on v2

--- a/solution.py
+++ b/solution.py
@@ -13,6 +13,7 @@
 VBLK = 128
 ABLK = 32
 RING = 4
+PAIRED = 2
 SCALE = 1.0 / math.sqrt(HEAD)
 LOG2E = math.log2(math.e)
 NT = (((1,), (1,)), ((), ()))
@@ -20,7 +21,7 @@
 NN = (((1,), (0,)), ((), ()))
 F32 = jnp.float32
 BF = jnp.bfloat16
-VMEM = 32 << 20
+VMEM = 24 << 20
 CORE = [(a, a ^ 1) for a in range(4)]
 PAIR = [(a, a ^ 2) for a in range(4)]
 
@@ -33,26 +34,27 @@
     pos, q_ref, k0, k1, k2, k3, k4, v0, v1, v2, v3, v4, bias_ref, w_ref, l0, l1,
     att_ref, p_ref, out_ref, gw_ref, far0, far1, all_ref,
 ):
-    q = q_ref[...]
-    tokens = q.shape[0]
+    tokens = q_ref.shape[0]
     rows = k0.shape[0]
     blocks = rows // ABLK
-    scores = []
-    for i, k in enumerate((k0, k1, k2, k3, k4)):
-        tile = dot(k[...], q, NT).reshape(blocks, ABLK, tokens)
-        tile = tile + bias_ref[blocks * i : blocks * (i + 1), :][:, None, :]
-        scores.append(tile.reshape(rows, tokens))
-    top = jnp.max(functools.reduce(jnp.maximum, scores), axis=0, keepdims=True)
-    exponent = [jnp.exp2((tile - top) * (SCALE * LOG2E)) for tile in scores]
-    total = jnp.sum(functools.reduce(jnp.add, exponent), axis=0, keepdims=True)
-    share = 1.0 / total
-    for i, tile in enumerate(exponent):
-        p_ref[0, rows * i : rows * (i + 1), :] = (tile * share).astype(BF)
-    values = jnp.concatenate([v[...] for v in (v0, v1, v2, v3, v4)], axis=0)
-    att = dot(values, p_ref[0], TN).T.astype(BF)
-    att_ref[...] = att
     head = pl.program_id(0)
-    all_ref[:, pl.ds(pl.multiple_of(head * HEAD, HEAD), HEAD)] = att
+    for u in range(PAIRED):
+        own = slice(u * HEAD, (u + 1) * HEAD)
+        q = q_ref[:, own]
+        scores = []
+        for i, k in enumerate((k0, k1, k2, k3, k4)):
+            tile = dot(k[:, own], q, NT).reshape(blocks, ABLK, tokens)
+            tile = tile + bias_ref[blocks * i : blocks * (i + 1), :][:, None, :]
+            scores.append(tile.reshape(rows, tokens))
+        top = jnp.max(functools.reduce(jnp.maximum, scores), axis=0, keepdims=True)
+        exponent = [jnp.exp2((tile - top) * (SCALE * LOG2E)) for tile in scores]
+        total = jnp.sum(functools.reduce(jnp.add, exponent), axis=0, keepdims=True)
+        share = 1.0 / total
+        for i, tile in enumerate(exponent):
+            p_ref[u, rows * i : rows * (i + 1), :] = (tile * share).astype(BF)
+        values = jnp.concatenate([v[:, own] for v in (v0, v1, v2, v3, v4)], axis=0)
+        att_ref[:, own] = dot(values, p_ref[u], TN).T.astype(BF)
+    all_ref[:, pl.ds(pl.multiple_of(head * PAIRED * HEAD, PAIRED * HEAD), PAIRED * HEAD)] = att_ref[...]
 
     @pl.when(head == pl.num_programs(0) - 1)
     def _():
@@ -71,9 +73,9 @@
 
 
 def attend_backward(
-    given, q_ref, k0, k1, k2, k3, k4, v0, v1, v2, v3, v4, p_ref, att_ref, near_ref, c0, c1, w0, w1, *refs
+    q_ref, k0, k1, k2, k3, k4, v0, v1, v2, v3, v4, p_ref, att_ref, near_ref, c0, c1, w0, w1,
+    dq_ref, g0, g1, g2, g3, g4, all_ref,
 ):
-    dq_ref, g0, g1, g2, g3, g4, all_ref = refs[given:]
     head = pl.program_id(0)
 
     @pl.when(head == 0)
@@ -82,23 +84,26 @@
         all_ref[...] = total.astype(BF)
 
     grads = (g0, g1, g2, g3, g4)
-    q = q_ref[...]
-    do = all_ref[:, pl.ds(pl.multiple_of(head * HEAD, HEAD), HEAD)]
     rows = k0.shape[0]
-    do_t = do.T
-    delta = jnp.sum(
-        do_t.astype(F32) * att_ref[...].T.astype(F32), axis=0, keepdims=True
-    )
-    score_grads = []
-    for i, v in enumerate((v0, v1, v2, v3, v4)):
-        p = p_ref[0, rows * i : rows * (i + 1), :]
-        prob_grad = dot(v[...], do_t, NN)
-        ds = (p.astype(F32) * (prob_grad - delta)).astype(BF)
-        score_grads.append(ds)
-        grads[i][0] = (dot(ds, q, NN) * SCALE).astype(grads[i].dtype)
-        grads[i][1] = dot(p, do, NN).astype(grads[i].dtype)
-    keys = jnp.concatenate([k[...] for k in (k0, k1, k2, k3, k4)], axis=0)
-    dq_ref[...] = (dot(keys, jnp.concatenate(score_grads, axis=0), TN) * SCALE).T
+    wide = all_ref[:, pl.ds(pl.multiple_of(head * PAIRED * HEAD, PAIRED * HEAD), PAIRED * HEAD)]
+    for u in range(PAIRED):
+        own = slice(u * HEAD, (u + 1) * HEAD)
+        q = q_ref[:, own]
+        do = wide[:, own]
+        do_t = do.T
+        delta = jnp.sum(
+            do_t.astype(F32) * att_ref[:, own].T.astype(F32), axis=0, keepdims=True
+        )
+        values = jnp.concatenate([v[:, own] for v in (v0, v1, v2, v3, v4)], axis=0)
+        keys = jnp.concatenate([k[:, own] for k in (k0, k1, k2, k3, k4)], axis=0)
+        p = p_ref[u]
+        ds = (p.astype(F32) * (dot(values, do_t, NN) - delta)).astype(BF)
+        dk = dot(ds, q, NN) * SCALE
+        dv = dot(p, do, NN)
+        for i, out in enumerate((g0, g1, g2, g3, g4)):
+            out[0, :, own] = dk[rows * i : rows * (i + 1)].astype(out.dtype)
+            out[1, :, own] = dv[rows * i : rows * (i + 1)].astype(out.dtype)
+        dq_ref[:, own] = (dot(keys, ds, TN) * SCALE).T
 
 
 def call(kernel, grid, scalars, in_specs, out_specs, out_shape, scratch=(), name=None, cost=None):
@@ -222,8 +227,8 @@
     rows = keys[0].shape[0]
     band = rows * len(keys)
     part = feature // RING
-    by_head = pl.BlockSpec((tokens, HEAD), lambda h, pos: (0, h))
-    kv_head = pl.BlockSpec((rows, HEAD), lambda h, pos: (0, h))
+    by_head = pl.BlockSpec((tokens, PAIRED * HEAD), lambda h, pos: (0, h))
+    kv_head = pl.BlockSpec((rows, PAIRED * HEAD), lambda h, pos: (0, h))
     once = [
         jax.ShapeDtypeStruct((tokens, weight.shape[0]), BF),
         jax.ShapeDtypeStruct((2, RING, part, feature), BF),
@@ -232,10 +237,10 @@
     ]
     return call(
         attend_forward,
-        (heads,),
+        (heads // PAIRED,),
         (pos,),
         [by_head] + [kv_head] * 10 + [whole(v) for v in (bias, weight, *lefts)],
-        [by_head, pl.BlockSpec((1, band, tokens), lambda h, pos: (h, 0, 0))] + [whole(v) for v in once],
+        [by_head, pl.BlockSpec((PAIRED, band, tokens), lambda h, pos: (h, 0, 0))] + [whole(v) for v in once],
         [
             jax.ShapeDtypeStruct((tokens, feature), BF),
             jax.ShapeDtypeStruct((heads, band, tokens), BF),
@@ -249,38 +254,32 @@
     )(pos, q, *keys, *values, bias, weight, *lefts)
 
 
-def backward_call(q, keys, values, p, att, near, cots, weights, half, done):
+def backward_call(q, keys, values, p, att, near, cots, weights):
     tokens, feature = q.shape
-    heads = feature // HEAD // 2
-    first = half * heads
+    heads = feature // HEAD
     rows = keys[0].shape[0]
     band = rows * len(keys)
-    by_head = pl.BlockSpec((tokens, HEAD), lambda h: (0, first + h))
-    kv_head = pl.BlockSpec((rows, HEAD), lambda h: (0, first + h))
-    both_head = pl.BlockSpec((2, rows, HEAD), lambda h: (0, 0, first + h))
-    columns = lambda v: pl.BlockSpec((v.shape[0], feature // 2), lambda h: (0, half))
+    by_head = pl.BlockSpec((tokens, PAIRED * HEAD), lambda h: (0, h))
+    kv_head = pl.BlockSpec((rows, PAIRED * HEAD), lambda h: (0, h))
+    both_head = pl.BlockSpec((2, rows, PAIRED * HEAD), lambda h: (0, 0, h))
     piece = lambda kind: jax.ShapeDtypeStruct((2, rows, feature), kind)
-    given = 18
-    return pl.pallas_call(
-        functools.partial(attend_backward, len(done)),
-        grid=(heads,),
-        in_specs=[by_head]
+    return call(
+        attend_backward,
+        (heads // PAIRED,),
+        (),
+        [by_head]
         + [kv_head] * 10
-        + [pl.BlockSpec((1, band, tokens), lambda h: (first + h, 0, 0)), by_head, columns(near)]
-        + [whole(v) for v in cots]
-        + [columns(v) for v in weights]
-        + [pl.BlockSpec(memory_space=pl.ANY)] * len(done),
-        out_specs=[by_head] + [both_head] * 5,
-        out_shape=[jax.ShapeDtypeStruct((tokens, feature), F32)]
+        + [pl.BlockSpec((PAIRED, band, tokens), lambda h: (h, 0, 0)), by_head]
+        + [whole(v) for v in (near, *cots, *weights)],
+        [by_head] + [both_head] * 5,
+        [jax.ShapeDtypeStruct((tokens, feature), F32)]
         + [piece(F32), piece(F32), piece(F32), piece(BF), piece(BF)],
-        scratch_shapes=[pltpu.VMEM((tokens, feature // 2), BF)],
-        input_output_aliases={given + i: i for i in range(len(done))},
-        compiler_params=pltpu.CompilerParams(vmem_limit_bytes=VMEM),
-        cost_estimate=pl.CostEstimate(
-            flops=6 * tokens * band * feature, bytes_accessed=0, transcendentals=0
+        scratch=[pltpu.VMEM((tokens, feature), BF)],
+        name="attend_backward",
+        cost=pl.CostEstimate(
+            flops=12 * tokens * band * feature, bytes_accessed=0, transcendentals=0
         ),
-        name="attend_backward",
-    )(q, *keys, *values, p, att, near, *cots, *weights, *done)
+    )(q, *keys, *values, p, att, near, *cots, *weights)
 
 
 def place(s):
@@ -389,22 +388,18 @@
     more, *more_far = weight_far(pos, cot_pair, after(cot_both, far_pair), att)
     more_got = exchange(more_far, x_even, x_odd)
 
-    def backward(half, cot_both, done):
-        return backward_call(
-            video_query, keys, values, p, att, grad_near, (cot_pair, cot_both), (w2, w3), half, done
-        )
-
-    left = backward(0, after(cot_both, *more_far), ())
-    more_send = beside(pos, more, after(more_got, left[0], *near_got))
+    grad_query, g_own, g_a, g_b, g_aa, g_bb = backward_call(
+        video_query, keys, values, p, att, grad_near, (cot_pair, after(cot_both, *more_far)), (w2, w3)
+    )
+    back_a = lax.ppermute(g_aa, "vseq", pa)
+    back_b = lax.ppermute(g_bb, "vseq", pb)
+
+    more_send = beside(pos, more, after(more_got, g_aa, g_bb, *near_got))
     more_got = exchange(more_send, x_even, x_odd)
     mixed_video = (
         dot(after(att, *more_send), w0, NT) + got_core[:, feature:].astype(F32) + got_pair.astype(F32)
     ).astype(BF)
-    grad_query, g_own, g_a, g_b, g_aa, g_bb = backward(1, after(cot_both, mixed_video), left)
-    back_a = lax.ppermute(g_aa, "vseq", pa)
-    back_b = lax.ppermute(g_bb, "vseq", pb)
-
-    keep, *sends = rows_of(pos, near, near_got, more, more_got)
+    keep, *sends = rows_of(pos, near, near_got, more, after(more_got, mixed_video))
     y_got = direct(sends, lambda j, y, x, z: (y ^ j, x, z))
 
     back_a, back_b = after((back_a, back_b), keep)

time: 165 us -> 157 us (0.952)
  Pallas kernels: 29.8 us -> 22.2 us
  starting transfers between devices: 51.1 us -> 49 us
    ppermute x4, waiting for transfers between devices: 13.4 us -> 24.9 us  [exchange(): lax.ppermute(send[0], 'vseq', even)]
    ppermute x1, waiting for transfers between devices: 8.45 us -> 0.01 us  [local(): sum_b = lax.ppermute(send_b, 'vseq', pb)]
    ppermute x1, waiting for transfers between devices: 7.61 us -> 0.01 us  [local(): back_a = lax.ppermute(g_aa, 'vseq', pa)]
    pallas_call x3 -> x2, Pallas kernels: 24.2 us -> 16.6 us  [the longest x1 9.03 us: forward_call(): call(attend_forward, (heads // PAIRED,), (pos,), [by_head] + [kv_head] *...]
    ppermute x4, waiting for transfers between devices: 6.32 us -> 12.8 us  [exchange(): lax.ppermute(send[1], 'vseq', odd)]
    ppermute x1, waiting for transfers between devices: 6.3 us -> 0.01 us  [local(): back_b = lax.ppermute(g_bb, 'vseq', pb)]
    ppermute x6, waiting for transfers between devices: 11.2 us -> 17 us  [direct(): lax.ppermute(send, 'vseq', along(functools.partial(change, j + 1)))]
    ppermute x1, starting transfers between devices: 2.02 us -> 0.01 us  [local(): back_b = lax.ppermute(g_bb, 'vseq', pb)]
  transfers between devices with their start and end apart: 31 -> 31, of which waited for: 22 -> 20; matrix products, arithmetic and copies ran while one was open for 8% -> 9% of each run, Pallas kernels for 18% -> 14%
where the time goes in v3:
time: 157 us; the launch traced here: 156 us
  waiting for transfers between devices  68.6 us (44%)
  starting transfers between devices  49 us (31%)
  Pallas kernels  22.2 us (14%)
  local copies, waits for them, and re-layouts  6.81 us (4%)
  matrix products  4.49 us (3%)
  other arithmetic  3.96 us (3%)
    ppermute x4, waiting for transfers between devices, exchange(): lax.ppermute(send[0], 'vseq', even)  24.9 us
    ppermute x6, waiting for transfers between devices, direct(): lax.ppermute(send, 'vseq', along(functools.partial(change, j + 1)))  17 us
    ppermute x4, waiting for transfers between devices, exchange(): lax.ppermute(send[1], 'vseq', odd)  12.8 us
    ppermute x2, starting transfers between devices, halo(): by_b = lax.ppermute(own, 'vseq', pb)  12 us
    ppermute x6, starting transfers between devices, direct(): lax.ppermute(send, 'vseq', along(functools.partial(change, j + 1)))  11.3 us
    ppermute x2, starting transfers between devices, halo(): lax.ppermute(by_a, 'vseq', pb)  9.46 us
    pallas_call x1, Pallas kernels, forward_call(): call(attend_forward, (heads // PAIRED,), (pos,), [by_head] + [kv_head] *...  9.03 us
    pallas_call x1, Pallas kernels, backward_call(): call(attend_backward, (heads // PAIRED,), (), [by_head] + [kv_head] * 10...  7.52 us
  transfers between devices with their start and end apart: 31, of which 20 were waited for; matrix products, arithmetic and copies ran while one was open for 9% of the time, Pallas kernels for 14%

profile of v3, /device:TPU:32, one launch (start us, length us, event | category | flops | bytes accessed | tf_op | source)
XLA Modules:
  0.0 155.9 jit_solution(17348372130944852202)
XLA Ops:
  1.3 10.0 %collective-permute-start.1 = (bf16[128,768]{1,0:T(8,128)(2,1)}, bf16[128,768]{1,0:T(8,128)(2,1)S(1)}, u32[]{:S(2)}, u32[]{:S(2)}) collective-permute-start(bf16[128,768]{1,0:T(8,128)(2,1)} %k0.1), channel_id=1, source_target_pairs={{0,252},{4,8},{8,4},{12,16},{16,12},{20,24},{24,20},{28,32},{32,28... | collective-permute-start | bytes 589832 | tf_op jit(solution)/shard_map/ppermute | solution.py:368
  11.4 2.0 %collective-permute-start.5 = (bf16[128,768]{1,0:T(8,128)(2,1)}, bf16[128,768]{1,0:T(8,128)(2,1)S(1)}, u32[]{:S(2)}, u32[]{:S(2)}) collective-permute-start(bf16[128,768]{1,0:T(8,128)(2,1)} %v0.3), channel_id=1, source_target_pairs={{0,252},{4,8},{8,4},{12,16},{16,12},{20,24},{24,20},{28,32},{32,28... | collective-permute-start | bytes 589832 | tf_op jit(solution)/shard_map/ppermute | solution.py:368
  16.4 4.7 %dynamic-slice_bitcast_fusion = (bf16[768,768]{1,0:T(8,128)(2,1)S(1)}, bf16[768,768]{1,0:T(8,128)(2,1)S(1)}, bf16[768,768]{1,0:T(8,128)(2,1)S(1)}) fusion(bf16[4,768,768]{2,1,0:T(8,128)(2,1)} %bitcast.36, s32[]{:T(128)} %bitcast.12, s32[]{:T(128)} %bitcast.10, s32[]{:T(128)} %bitcast.5), kind=kLoop, calls=%fused_computation.8 | loop fusion | bytes 7077900 | tf_op jit(solution)/shard_map/jit(dynamic_index_in_dim)/squeeze | solution.py:316
  21.1 1.4 fusion.2
  23.5 1.7 %collective-permute-done.k1 = bf16[128,768]{1,0:T(8,128)(2,1)S(1)} collective-permute-done((bf16[128,768]{1,0:T(8,128)(2,1)}, bf16[128,768]{1,0:T(8,128)(2,1)S(1)}, u32[]{:S(2)}, u32[]{:S(2)}) %collective-permute-start) | collective-permute-done | bytes 196640 | tf_op jit(solution)/shard_map/ppermute | solution.py:367
  25.2 7.2 %collective-permute-start.3 = (bf16[128,768]{1,0:T(8,128)(2,1)S(1)}, bf16[128,768]{1,0:T(8,128)(2,1)S(1)}, u32[]{:S(2)}, u32[]{:S(2)}) collective-permute-start(bf16[128,768]{1,0:T(8,128)(2,1)S(1)} %collective-permute-done.k1), channel_id=1, source_target_pairs={{0,252},{4,8},{8,4},{12,16},{16,12},{20,24},{24,20},{28,32},{32,28... | collective-permute-start | bytes 589832 | tf_op jit(solution)/shard_map/ppermute | solution.py:370
  33.2 2.3 %collective-permute-start.8 = (bf16[128,768]{1,0:T(8,128)(2,1)S(1)}, bf16[128,768]{1,0:T(8,128)(2,1)S(1)}, u32[]{:S(2)}, u32[]{:S(2)}) collective-permute-start(bf16[128,768]{1,0:T(8,128)(2,1)S(1)} %collective-permute-done.4.v1), channel_id=1, source_target_pairs={{0,252},{4,8},{8,4},{12,16},{16,12},{20,24},{24,20},{28,32},{32,28... | collective-permute-start | bytes 589832 | tf_op jit(solution)/shard_map/ppermute | solution.py:370
  36.3 5.3 %collective-permute-done.3.k4 = bf16[128,768]{1,0:T(8,128)(2,1)S(1)} collective-permute-done((bf16[128,768]{1,0:T(8,128)(2,1)S(1)}, bf16[128,768]{1,0:T(8,128)(2,1)S(1)}, u32[]{:S(2)}, u32[]{:S(2)}) %collective-permute-start.3) | collective-permute-done | bytes 196640 | tf_op jit(solution)/shard_map/ppermute | solution.py:370
  41.5 2.6 %collective-permute-done.2.k3 = bf16[128,768]{1,0:T(8,128)(2,1)S(1)} collective-permute-done((bf16[128,768]{1,0:T(8,128)(2,1)S(1)}, bf16[128,768]{1,0:T(8,128)(2,1)S(1)}, u32[]{:S(2)}, u32[]{:S(2)}) %collective-permute-start.2) | collective-permute-done | bytes 196640 | tf_op jit(solution)/shard_map/ppermute | solution.py:370
  44.1 1.6 %collective-permute-done.8.v4 = bf16[128,768]{1,0:T(8,128)(2,1)S(1)} collective-permute-done((bf16[128,768]{1,0:T(8,128)(2,1)S(1)}, bf16[128,768]{1,0:T(8,128)(2,1)S(1)}, u32[]{:S(2)}, u32[]{:S(2)}) %collective-permute-start.8) | collective-permute-done | bytes 196640 | tf_op jit(solution)/shard_map/ppermute | solution.py:370
  46.9 5.9 %collective-permute-start.9 = (bf16[512,768]{1,0:T(8,128)(2,1)S(1)}, bf16[512,768]{1,0:T(8,128)(2,1)S(1)}, u32[]{:S(2)}, u32[]{:S(2)}) collective-permute-start(bf16[512,768]{1,0:T(8,128)(2,1)S(1)} %copy-done.3), channel_id=1, source_target_pairs={{0,2},{1,3},{2,0},{3,1},{4,6},{5,7},{6,4},{7,5},{8,10},{9,11},{10,... | collective-permute-start | bytes 2359304 | tf_op jit(solution)/shard_map/ppermute | solution.py:375
  52.8 9.0 %attend_forward.1 = (bf16[512,768]{1,0:T(8,128)(2,1)S(1)}, bf16[6,640,512]{2,1,0:T(8,128)(2,1)S(1)}, bf16[512,1536]{1,0:T(8,128)(2,1)S(1)}, bf16[2,4,192,768]{3,...) custom-call(s32[36]{0:T(128)S(1)} %get-tuple-element.105.pos, ...), custom_call_target="tpu_custom_call" | custom-call | flops 2013265920 | tf_op jit(solution)/shard_map/attend_forward/pallas_call | solution.py:238
  62.2 8.3 %collective-permute-done.10.got_even = bf16[192,768]{1,0:T(8,128)(2,1)S(1)} collective-permute-done((bf16[192,768]{1,0:T(8,128)(2,1)S(1)}, bf16[192,768]{1,0:T(8,128)(2,1)S(1)}, u32[]{:S(2)}, u32[]{:S(2)}) %collective-permute-start.10) | collective-permute-done | bytes 294944 | tf_op jit(solution)/shard_map/ppermute | solution.py:344
  70.5 1.5 collective-permute-done.11.got_odd
  76.6 2.0 %weight_far.1 = (bf16[2,4,192,768]{3,2,1,0:T(8,128)(2,1)S(1)}, bf16[192,768]{1,0:T(8,128)(2,1)S(1)}, bf16[192,768]{1,0:T(8,128)(2,1)S(1)}) custom-call(s32[36]{0:T(128)S(1)} %get-tuple-element.105.pos, bf16[512,768]{1,0:T(8,128)(2,1)S(1)} %collective-permute-done.9.l0.c0, bf16[512,768]{1,0:T(8,128)(2,1)S(1)} %collective-permute-done.12.l1.c1, ...), custom_call_target="tpu_custom_call" | custom-call | tf_op jit(solution)/shard_map/weight_far/pallas_call | solution.py:140
  78.9 2.3 %collective-permute-start.15 = (bf16[192,768]{1,0:T(8,128)(2,1)S(1)}, bf16[192,768]{1,0:T(8,128)(2,1)S(1)}, u32[]{:S(2)}, u32[]{:S(2)}) collective-permute-start(bf16[192,768]{1,0:T(8,128)(2,1)S(1)} %get-tuple-element.72), channel_id=1, source_target_pairs={{0,48},{4,52},{8,56},{12,60},{16,32},{20,36},{24,40},{28,44},{32,1... | collective-permute-start | bytes 884744 | tf_op jit(solution)/shard_map/ppermute | solution.py:344
  81.3 7.5 %attend_backward.1 = (f32[512,768]{1,0:T(8,128)}, f32[2,128,768]{2,1,0:T(8,128)S(1)}, f32[2,128,768]{2,1,0:T(8,128)S(1)}, f32[2,128,768]{2,1,0:T(8,128)S(1)}, bf...) custom-call(bf16[512,768]{1,0:T(8,128)(2,1)S(1)} %copy-done, bf16[128,768]{1,0:T(8,128)(2,1)S(1)} %copy-done.1, ...), custom_call_target="tpu_custom_call" | custom-call | flops 3019898880 | tf_op jit(solution)/shard_map/attend_backward/pallas_call | solution.py:266
  89.5 5.7 %collective-permute-done.17.near_odd = bf16[2,192,768]{2,1,0:T(8,128)(2,1)S(1)} collective-permute-done((bf16[2,192,768]{2,1,0:T(8,128)(2,1)S(1)}, bf16[2,192,768]{2,1,0:T(8,128)(2,1)S(1)}, u32[]{:S(2)}, u32[]{:S(2)}) %collective-permute-start.17) | collective-permute-done | bytes 589856 | tf_op jit(solution)/shard_map/ppermute | solution.py:344
  95.2 5.3 %collective-permute-done.14.got_even = bf16[192,768]{1,0:T(8,128)(2,1)S(1)} collective-permute-done((bf16[192,768]{1,0:T(8,128)(2,1)S(1)}, bf16[192,768]{1,0:T(8,128)(2,1)S(1)}, u32[]{:S(2)}, u32[]{:S(2)}) %collective-permute-start.14) | collective-permute-done | bytes 294944 | tf_op jit(solution)/shard_map/ppermute | solution.py:344
  100.6 4.0 %collective-permute-done.15.got_odd = bf16[192,768]{1,0:T(8,128)(2,1)S(1)} collective-permute-done((bf16[192,768]{1,0:T(8,128)(2,1)S(1)}, bf16[192,768]{1,0:T(8,128)(2,1)S(1)}, u32[]{:S(2)}, u32[]{:S(2)}) %collective-permute-start.15) | collective-permute-done | bytes 294944 | tf_op jit(solution)/shard_map/ppermute | solution.py:344
  106.4 1.5 fusion
  109.1 10.6 %collective-permute-done.21.more_even = bf16[2,192,768]{2,1,0:T(8,128)(2,1)S(1)} collective-permute-done((bf16[2,192,768]{2,1,0:T(8,128)(2,1)S(1)}, bf16[2,192,768]{2,1,0:T(8,128)(2,1)S(1)}, u32[]{:S(2)}, u32[]{:S(2)}) %collective-permute-start.21) | collective-permute-done | bytes 589856 | tf_op jit(solution)/shard_map/ppermute | solution.py:344
  119.6 1.5 collective-permute-done.22.more_odd
  121.1 1.4 rows.1
  122.7 2.0 %collective-permute-start.26 = (bf16[192,768]{1,0:T(8,128)(2,1)S(1)}, bf16[192,768]{1,0:T(8,128)(2,1)S(1)}, u32[]{:S(2)}, u32[]{:S(2)}) collective-permute-start(bf16[192,768]{1,0:T(8,128)(2,1)S(1)} %get-tuple-element.93), channel_id=1, source_target_pairs={{0,128},{4,132},{8,136},{12,140},{16,144},{20,148},{24,152},{28,15... | collective-permute-start | bytes 884744 | tf_op jit(solution)/shard_map/ppermute | solution.py:348
  124.7 2.7 %collective-permute-start.27 = (bf16[192,768]{1,0:T(8,128)(2,1)S(1)}, bf16[192,768]{1,0:T(8,128)(2,1)S(1)}, u32[]{:S(2)}, u32[]{:S(2)}) collective-permute-start(bf16[192,768]{1,0:T(8,128)(2,1)S(1)} %get-tuple-element.94), channel_id=1, source_target_pairs={{0,192},{4,196},{8,200},{12,204},{16,208},{20,212},{24,216},{28,22... | collective-permute-start | bytes 884744 | tf_op jit(solution)/shard_map/ppermute | solution.py:348
  127.7 2.1 %collective-permute-start.24 = (bf16[2,128,768]{2,1,0:T(8,128)(2,1)S(1)}, bf16[2,128,768]{2,1,0:T(8,128)(2,1)S(1)}, u32[]{:S(2)}, u32[]{:S(2)}) collective-permute-start(bf16[2,128,768]{2,1,0:T(8,128)(2,1)S(1)} %add_convert_fusion.2), channel_id=1, source_target_pairs={{0,252},{4,8},{8,4},{12,16},{16,12},{20,24},{24,20},{28,32},{32,28... | collective-permute-start | bytes 1179656 | tf_op jit(solution)/shard_map/ppermute | solution.py:408
  129.8 2.8 %collective-permute-done.25.g1 = bf16[192,768]{1,0:T(8,128)(2,1)S(1)} collective-permute-done((bf16[192,768]{1,0:T(8,128)(2,1)S(1)}, bf16[192,768]{1,0:T(8,128)(2,1)S(1)}, u32[]{:S(2)}, u32[]{:S(2)}) %collective-permute-start.25) | collective-permute-done | bytes 294944 | tf_op jit(solution)/shard_map/ppermute | solution.py:348
  132.6 3.5 %collective-permute-done.26.g2 = bf16[192,768]{1,0:T(8,128)(2,1)S(1)} collective-permute-done((bf16[192,768]{1,0:T(8,128)(2,1)S(1)}, bf16[192,768]{1,0:T(8,128)(2,1)S(1)}, u32[]{:S(2)}, u32[]{:S(2)}) %collective-permute-start.26) | collective-permute-done | bytes 294944 | tf_op jit(solution)/shard_map/ppermute | solution.py:348
  136.2 7.4 %collective-permute-done.27.g3 = bf16[192,768]{1,0:T(8,128)(2,1)S(1)} collective-permute-done((bf16[192,768]{1,0:T(8,128)(2,1)S(1)}, bf16[192,768]{1,0:T(8,128)(2,1)S(1)}, u32[]{:S(2)}, u32[]{:S(2)}) %collective-permute-start.27) | collective-permute-done | bytes 294944 | tf_op jit(solution)/shard_map/ppermute | solution.py:348
  144.6 6.4 %collective-permute-start.30 = (bf16[48,768]{1,0:T(8,128)(2,1)S(1)}, bf16[48,768]{1,0:T(8,128)(2,1)S(1)}, u32[]{:S(2)}, u32[]{:S(2)}) collective-permute-start(bf16[48,768]{1,0:T(8,128)(2,1)S(1)} %get-tuple-element.98), channel_id=1, source_target_pairs={{0,12},{4,8},{8,4},{12,0},{16,28},{20,24},{24,20},{28,16},{32,44},... | collective-permute-start | bytes 221192 | tf_op jit(solution)/shard_map/ppermute | solution.py:348
  151.0 1.9 %collective-permute-done.29 = bf16[48,768]{1,0:T(8,128)(2,1)S(1)} collective-permute-done((bf16[48,768]{1,0:T(8,128)(2,1)S(1)}, bf16[48,768]{1,0:T(8,128)(2,1)S(1)}, u32[]{:S(2)}, u32[]{:S(2)}) %collective-permute-start.29) | collective-permute-done | bytes 73760 | tf_op jit(solution)/shard_map/ppermute | solution.py:348
  (64 shorter events, 20.8 us)
Async XLA Ops:
  1.3 22.1 %collective-permute-start.1 = (bf16[128,768]{1,0:T(8,128)(2,1)}, bf16[128,768]{1,0:T(8,128)(2,1)S(1)}, u32[]{:S(2)}, u32[]{:S(2)}) collective-permute-start(bf16[128,768]{1,0:T(8,128)(2,1)} %k0.1), channel_id=1, source_target_pairs={{0,252},{4,8},{8,4},{12,16},{16,12},{20,24},{24,20},{28,32},{32,28... | collective-permute-start | bytes 589832 | tf_op jit(solution)/shard_map/ppermute | solution.py:368
  11.4 13.8 %collective-permute-start = (bf16[128,768]{1,0:T(8,128)(2,1)}, bf16[128,768]{1,0:T(8,128)(2,1)S(1)}, u32[]{:S(2)}, u32[]{:S(2)}) collective-permute-start(bf16[128,768]{1,0:T(8,128)(2,1)} %k0.1), channel_id=1, source_target_pairs={{0,4},{4,0},{8,12},{12,8},{16,20},{20,16},{24,28},{28,24},{32,36},... | collective-permute-start | bytes 589832 | tf_op jit(solution)/shard_map/ppermute | solution.py:367
  11.4 21.8 %collective-permute-start.5 = (bf16[128,768]{1,0:T(8,128)(2,1)}, bf16[128,768]{1,0:T(8,128)(2,1)S(1)}, u32[]{:S(2)}, u32[]{:S(2)}) collective-permute-start(bf16[128,768]{1,0:T(8,128)(2,1)} %v0.3), channel_id=1, source_target_pairs={{0,252},{4,8},{8,4},{12,16},{16,12},{20,24},{24,20},{28,32},{32,28... | collective-permute-start | bytes 589832 | tf_op jit(solution)/shard_map/ppermute | solution.py:368
  13.4 19.8 %collective-permute-start.4 = (bf16[128,768]{1,0:T(8,128)(2,1)}, bf16[128,768]{1,0:T(8,128)(2,1)S(1)}, u32[]{:S(2)}, u32[]{:S(2)}) collective-permute-start(bf16[128,768]{1,0:T(8,128)(2,1)} %v0.3), channel_id=1, source_target_pairs={{0,4},{4,0},{8,12},{12,8},{16,20},{20,16},{24,28},{28,24},{32,36},... | collective-permute-start | bytes 589832 | tf_op jit(solution)/shard_map/ppermute | solution.py:367
  14.3 18.0 %collective-permute-start.6 = (bf16[512,768]{1,0:T(8,128)(2,1)}, bf16[512,768]{1,0:T(8,128)(2,1)S(1)}, u32[]{:S(2)}, u32[]{:S(2)}) collective-permute-start(bf16[512,768]{1,0:T(8,128)(2,1)} %l0.1), channel_id=1, source_target_pairs={{0,1},{1,0},{2,3},{3,2},{4,5},{5,4},{6,7},{7,6},{8,9},{9,8},{10,11... | collective-permute-start | bytes 2359304 | tf_op jit(solution)/shard_map/ppermute | solution.py:363
  22.8 30.0 %copy-start = (bf16[512,768]{1,0:T(8,128)(2,1)S(1)}, bf16[512,768]{1,0:T(8,128)(2,1)}, u32[]{:S(2)}) copy-start(bf16[512,768]{1,0:T(8,128)(2,1)} %q_ref.3) | copy-start | bytes 2359300
  25.2 16.4 %collective-permute-start.3 = (bf16[128,768]{1,0:T(8,128)(2,1)S(1)}, bf16[128,768]{1,0:T(8,128)(2,1)S(1)}, u32[]{:S(2)}, u32[]{:S(2)}) collective-permute-start(bf16[128,768]{1,0:T(8,128)(2,1)S(1)} %collective-permute-done.k1), channel_id=1, source_target_pairs={{0,252},{4,8},{8,4},{12,16},{16,12},{20,24},{24,20},{28,32},{32,28... | collective-permute-start | bytes 589832 | tf_op jit(solution)/shard_map/ppermute | solution.py:370
  32.3 11.8 %collective-permute-start.2 = (bf16[128,768]{1,0:T(8,128)(2,1)S(1)}, bf16[128,768]{1,0:T(8,128)(2,1)S(1)}, u32[]{:S(2)}, u32[]{:S(2)}) collective-permute-start(bf16[128,768]{1,0:T(8,128)(2,1)S(1)} %collective-permute-done.1.k2), channel_id=1, source_target_pairs={{0,4},{4,0},{8,12},{12,8},{16,20},{20,16},{24,28},{28,24},{32,36},... | collective-permute-start | bytes 589832 | tf_op jit(solution)/shard_map/ppermute | solution.py:370
  33.2 12.6 %collective-permute-start.8 = (bf16[128,768]{1,0:T(8,128)(2,1)S(1)}, bf16[128,768]{1,0:T(8,128)(2,1)S(1)}, u32[]{:S(2)}, u32[]{:S(2)}) collective-permute-start(bf16[128,768]{1,0:T(8,128)(2,1)S(1)} %collective-permute-done.4.v1), channel_id=1, source_target_pairs={{0,252},{4,8},{8,4},{12,16},{16,12},{20,24},{24,20},{28,32},{32,28... | collective-permute-start | bytes 589832 | tf_op jit(solution)/shard_map/ppermute | solution.py:370
  35.4 11.4 %collective-permute-start.7 = (bf16[128,768]{1,0:T(8,128)(2,1)S(1)}, bf16[128,768]{1,0:T(8,128)(2,1)S(1)}, u32[]{:S(2)}, u32[]{:S(2)}) collective-permute-start(bf16[128,768]{1,0:T(8,128)(2,1)S(1)} %collective-permute-done.5.v2), channel_id=1, source_target_pairs={{0,4},{4,0},{8,12},{12,8},{16,20},{20,16},{24,28},{28,24},{32,36},... | collective-permute-start | bytes 589832 | tf_op jit(solution)/shard_map/ppermute | solution.py:370
  46.9 25.1 %collective-permute-start.9 = (bf16[512,768]{1,0:T(8,128)(2,1)S(1)}, bf16[512,768]{1,0:T(8,128)(2,1)S(1)}, u32[]{:S(2)}, u32[]{:S(2)}) collective-permute-start(bf16[512,768]{1,0:T(8,128)(2,1)S(1)} %copy-done.3), channel_id=1, source_target_pairs={{0,2},{1,3},{2,0},{3,1},{4,6},{5,7},{6,4},{7,5},{8,10},{9,11},{10,... | collective-permute-start | bytes 2359304 | tf_op jit(solution)/shard_map/ppermute | solution.py:375
  61.8 8.7 %collective-permute-start.10 = (bf16[192,768]{1,0:T(8,128)(2,1)S(1)}, bf16[192,768]{1,0:T(8,128)(2,1)S(1)}, u32[]{:S(2)}, u32[]{:S(2)}) collective-permute-start(bf16[192,768]{1,0:T(8,128)(2,1)S(1)} %get-tuple-element.60), channel_id=1, source_target_pairs={{0,16},{4,20},{8,24},{12,28},{16,0},{20,4},{24,8},{28,12},{32,48},... | collective-permute-start | bytes 884744 | tf_op jit(solution)/shard_map/ppermute | solution.py:344
  61.9 10.1 %collective-permute-start.11 = (bf16[192,768]{1,0:T(8,128)(2,1)S(1)}, bf16[192,768]{1,0:T(8,128)(2,1)S(1)}, u32[]{:S(2)}, u32[]{:S(2)}) collective-permute-start(bf16[192,768]{1,0:T(8,128)(2,1)S(1)} %get-tuple-element.61), channel_id=1, source_target_pairs={{0,48},{4,52},{8,56},{12,60},{16,32},{20,36},{24,40},{28,44},{32,1... | collective-permute-start | bytes 884744 | tf_op jit(solution)/shard_map/ppermute | solution.py:344
  72.0 3.4 %collective-permute-start.13 = (bf16[512,1536]{1,0:T(8,128)(2,1)S(1)}, bf16[512,1536]{1,0:T(8,128)(2,1)S(1)}, u32[]{:S(2)}, u32[]{:S(2)}) collective-permute-start(bf16[512,1536]{1,0:T(8,128)(2,1)S(1)} %get-tuple-element.68), channel_id=1, source_target_pairs={{0,1},{1,0},{2,3},{3,2},{4,5},{5,4},{6,7},{7,6},{8,9},{9,8},{10,11... | collective-permute-start | bytes 4718600 | tf_op jit(solution)/shard_map/ppermute | solution.py:383
  72.0 4.6 %collective-permute-start.12 = (bf16[512,768]{1,0:T(8,128)(2,1)S(1)}, bf16[512,768]{1,0:T(8,128)(2,1)S(1)}, u32[]{:S(2)}, u32[]{:S(2)}) collective-permute-start(bf16[512,768]{1,0:T(8,128)(2,1)S(1)} %collective-permute-done.9.l0.c0), channel_id=1, source_target_pairs={{0,1},{1,0},{2,3},{3,2},{4,5},{5,4},{6,7},{7,6},{8,9},{9,8},{10,11... | collective-permute-start | bytes 2359304 | tf_op jit(solution)/shard_map/ppermute | solution.py:382
  73.2 16.3 %collective-permute-start.16 = (bf16[2,192,768]{2,1,0:T(8,128)(2,1)S(1)}, bf16[2,192,768]{2,1,0:T(8,128)(2,1)S(1)}, u32[]{:S(2)}, u32[]{:S(2)}) collective-permute-start(bf16[2,192,768]{2,1,0:T(8,128)(2,1)S(1)} %get-tuple-element.64), channel_id=1, source_target_pairs={{0,16},{4,20},{8,24},{12,28},{16,0},{20,4},{24,8},{28,12},{32,48},... | collective-permute-start | bytes 1769480 | tf_op jit(solution)/shard_map/ppermute | solution.py:344
  73.5 21.7 %collective-permute-start.17 = (bf16[2,192,768]{2,1,0:T(8,128)(2,1)S(1)}, bf16[2,192,768]{2,1,0:T(8,128)(2,1)S(1)}, u32[]{:S(2)}, u32[]{:S(2)}) collective-permute-start(bf16[2,192,768]{2,1,0:T(8,128)(2,1)S(1)} %get-tuple-element.65), channel_id=1, source_target_pairs={{0,48},{4,52},{8,56},{12,60},{16,32},{20,36},{24,40},{28,44},{32,1... | collective-permute-start | bytes 1769480 | tf_op jit(solution)/shard_map/ppermute | solution.py:344
  76.2 31.7 %collective-permute-start.18 = (bf16[512,768]{1,0:T(8,128)(2,1)S(1)}, bf16[512,768]{1,0:T(8,128)(2,1)S(1)}, u32[]{:S(2)}, u32[]{:S(2)}) collective-permute-start(bf16[512,768]{1,0:T(8,128)(2,1)S(1)} %add_convert_fusion.1), channel_id=1, source_target_pairs={{0,2},{1,3},{2,0},{3,1},{4,6},{5,7},{6,4},{7,5},{8,10},{9,11},{10,... | collective-permute-start | bytes 2359304 | tf_op jit(solution)/shard_map/ppermute | solution.py:387
  78.6 22.0 %collective-permute-start.14 = (bf16[192,768]{1,0:T(8,128)(2,1)S(1)}, bf16[192,768]{1,0:T(8,128)(2,1)S(1)}, u32[]{:S(2)}, u32[]{:S(2)}) collective-permute-start(bf16[192,768]{1,0:T(8,128)(2,1)S(1)} %get-tuple-element.71), channel_id=1, source_target_pairs={{0,16},{4,20},{8,24},{12,28},{16,0},{20,4},{24,8},{28,12},{32,48},... | collective-permute-start | bytes 884744 | tf_op jit(solution)/shard_map/ppermute | solution.py:344
  78.9 25.6 %collective-permute-start.15 = (bf16[192,768]{1,0:T(8,128)(2,1)S(1)}, bf16[192,768]{1,0:T(8,128)(2,1)S(1)}, u32[]{:S(2)}, u32[]{:S(2)}) collective-permute-start(bf16[192,768]{1,0:T(8,128)(2,1)S(1)} %get-tuple-element.72), channel_id=1, source_target_pairs={{0,48},{4,52},{8,56},{12,60},{16,32},{20,36},{24,40},{28,44},{32,1... | collective-permute-start | bytes 884744 | tf_op jit(solution)/shard_map/ppermute | solution.py:344
  89.5 33.1 %collective-permute-start.19 = (bf16[2,128,768]{2,1,0:T(8,128)(2,1)S(1)}, bf16[2,128,768]{2,1,0:T(8,128)(2,1)S(1)}, u32[]{:S(2)}, u32[]{:S(2)}) collective-permute-start(bf16[2,128,768]{2,1,0:T(8,128)(2,1)S(1)} %get-tuple-element.75), channel_id=1, source_target_pairs={{0,4},{4,0},{8,12},{12,8},{16,20},{20,16},{24,28},{28,24},{32,36},... | collective-permute-start | bytes 1179656 | tf_op jit(solution)/shard_map/ppermute | solution.py:394
  95.2 27.3 %collective-permute-start.20 = (bf16[2,128,768]{2,1,0:T(8,128)(2,1)S(1)}, bf16[2,128,768]{2,1,0:T(8,128)(2,1)S(1)}, u32[]{:S(2)}, u32[]{:S(2)}) collective-permute-start(bf16[2,128,768]{2,1,0:T(8,128)(2,1)S(1)} %get-tuple-element.76), channel_id=1, source_target_pairs={{0,252},{4,8},{8,4},{12,16},{16,12},{20,24},{24,20},{28,32},{32,28... | collective-permute-start | bytes 1179656 | tf_op jit(solution)/shard_map/ppermute | solution.py:395
  105.3 14.3 %collective-permute-start.21 = (bf16[2,192,768]{2,1,0:T(8,128)(2,1)S(1)}, bf16[2,192,768]{2,1,0:T(8,128)(2,1)S(1)}, u32[]{:S(2)}, u32[]{:S(2)}) collective-permute-start(bf16[2,192,768]{2,1,0:T(8,128)(2,1)S(1)} %get-tuple-element.79), channel_id=1, source_target_pairs={{0,16},{4,20},{8,24},{12,28},{16,0},{20,4},{24,8},{28,12},{32,48},... | collective-permute-start | bytes 1769480 | tf_op jit(solution)/shard_map/ppermute | solution.py:344
  105.4 15.7 %collective-permute-start.22 = (bf16[2,192,768]{2,1,0:T(8,128)(2,1)S(1)}, bf16[2,192,768]{2,1,0:T(8,128)(2,1)S(1)}, u32[]{:S(2)}, u32[]{:S(2)}) collective-permute-start(bf16[2,192,768]{2,1,0:T(8,128)(2,1)S(1)} %get-tuple-element.80), channel_id=1, source_target_pairs={{0,48},{4,52},{8,56},{12,60},{16,32},{20,36},{24,40},{28,44},{32,1... | collective-permute-start | bytes 1769480 | tf_op jit(solution)/shard_map/ppermute | solution.py:344
  122.6 10.0 %collective-permute-start.25 = (bf16[192,768]{1,0:T(8,128)(2,1)S(1)}, bf16[192,768]{1,0:T(8,128)(2,1)S(1)}, u32[]{:S(2)}, u32[]{:S(2)}) collective-permute-start(bf16[192,768]{1,0:T(8,128)(2,1)S(1)} %get-tuple-element.92), channel_id=1, source_target_pairs={{0,64},{4,68},{8,72},{12,76},{16,80},{20,84},{24,88},{28,92},{32,9... | collective-permute-start | bytes 884744 | tf_op jit(solution)/shard_map/ppermute | solution.py:348
  122.7 13.5 %collective-permute-start.26 = (bf16[192,768]{1,0:T(8,128)(2,1)S(1)}, bf16[192,768]{1,0:T(8,128)(2,1)S(1)}, u32[]{:S(2)}, u32[]{:S(2)}) collective-permute-start(bf16[192,768]{1,0:T(8,128)(2,1)S(1)} %get-tuple-element.93), channel_id=1, source_target_pairs={{0,128},{4,132},{8,136},{12,140},{16,144},{20,148},{24,152},{28,15... | collective-permute-start | bytes 884744 | tf_op jit(solution)/shard_map/ppermute | solution.py:348
  124.7 18.9 %collective-permute-start.27 = (bf16[192,768]{1,0:T(8,128)(2,1)S(1)}, bf16[192,768]{1,0:T(8,128)(2,1)S(1)}, u32[]{:S(2)}, u32[]{:S(2)}) collective-permute-start(bf16[192,768]{1,0:T(8,128)(2,1)S(1)} %get-tuple-element.94), channel_id=1, source_target_pairs={{0,192},{4,196},{8,200},{12,204},{16,208},{20,212},{24,216},{28,22... | collective-permute-start | bytes 884744 | tf_op jit(solution)/shard_map/ppermute | solution.py:348
  127.5 27.4 %collective-permute-start.23 = (bf16[2,128,768]{2,1,0:T(8,128)(2,1)S(1)}, bf16[2,128,768]{2,1,0:T(8,128)(2,1)S(1)}, u32[]{:S(2)}, u32[]{:S(2)}) collective-permute-start(bf16[2,128,768]{2,1,0:T(8,128)(2,1)S(1)} %add_convert_fusion.3), channel_id=1, source_target_pairs={{0,4},{4,0},{8,12},{12,8},{16,20},{20,16},{24,28},{28,24},{32,36},... | collective-permute-start | bytes 1179656 | tf_op jit(solution)/shard_map/ppermute | solution.py:409
  127.7 27.2 %collective-permute-start.24 = (bf16[2,128,768]{2,1,0:T(8,128)(2,1)S(1)}, bf16[2,128,768]{2,1,0:T(8,128)(2,1)S(1)}, u32[]{:S(2)}, u32[]{:S(2)}) collective-permute-start(bf16[2,128,768]{2,1,0:T(8,128)(2,1)S(1)} %add_convert_fusion.2), channel_id=1, source_target_pairs={{0,252},{4,8},{8,4},{12,16},{16,12},{20,24},{24,20},{28,32},{32,28... | collective-permute-start | bytes 1179656 | tf_op jit(solution)/shard_map/ppermute | solution.py:408
  144.4 6.6 %collective-permute-start.28 = (bf16[48,768]{1,0:T(8,128)(2,1)S(1)}, bf16[48,768]{1,0:T(8,128)(2,1)S(1)}, u32[]{:S(2)}, u32[]{:S(2)}) collective-permute-start(bf16[48,768]{1,0:T(8,128)(2,1)S(1)} %get-tuple-element.96), channel_id=1, source_target_pairs={{0,4},{4,0},{8,12},{12,8},{16,20},{20,16},{24,28},{28,24},{32,36},... | collective-permute-start | bytes 221192 | tf_op jit(solution)/shard_map/ppermute | solution.py:348
  144.5 8.4 %collective-permute-start.29 = (bf16[48,768]{1,0:T(8,128)(2,1)S(1)}, bf16[48,768]{1,0:T(8,128)(2,1)S(1)}, u32[]{:S(2)}, u32[]{:S(2)}) collective-permute-start(bf16[48,768]{1,0:T(8,128)(2,1)S(1)} %get-tuple-element.97), channel_id=1, source_target_pairs={{0,8},{4,12},{8,0},{12,4},{16,24},{20,28},{24,16},{28,20},{32,40},... | collective-permute-start | bytes 221192 | tf_op jit(solution)/shard_map/ppermute | solution.py:348
  144.6 9.5 %collective-permute-start.30 = (bf16[48,768]{1,0:T(8,128)(2,1)S(1)}, bf16[48,768]{1,0:T(8,128)(2,1)S(1)}, u32[]{:S(2)}, u32[]{:S(2)}) collective-permute-start(bf16[48,768]{1,0:T(8,128)(2,1)S(1)} %get-tuple-element.98), channel_id=1, source_target_pairs={{0,12},{4,8},{8,4},{12,0},{16,28},{20,24},{24,20},{28,16},{32,44},... | collective-permute-start | bytes 221192 | tf_op jit(solution)/shard_map/ppermute | solution.py:348
  (4 other events, 69.4 us)

commit v4 on v3

--- a/solution.py
+++ b/solution.py
@@ -170,17 +170,19 @@
     )(pos, chunks, chunks, *got)
 
 
-def rows_kernel(pos, near, near_even, near_odd, more, more_even, more_odd, keep, s1, s2, s3, rows):
+def rows_kernel(pos, near, near_even, near_odd, more, more_even, more_odd, rows, s_even, s_odd):
     for j, (own, even, odd) in enumerate(((near, near_even, near_odd), (more, more_even, more_odd))):
         total = own[:, 0].astype(F32) + even[...].astype(F32) + odd[...].astype(F32)
         rows[2 * j : 2 * j + 2] = total.astype(BF)
-    for k, out in enumerate((keep, s1, s2, s3)):
-        out[...] = rows[pos[PART + k]]
+    half = s_even.shape[0]
+    s_even[...] = rows[pos[PART + 2], :half]
+    s_odd[...] = rows[pos[PART + 2], half:]
 
 
 def rows_of(pos, near, near_got, more, more_got):
     _, _, part, feature = near.shape
-    send = jax.ShapeDtypeStruct((part, feature), BF)
+    half = jax.ShapeDtypeStruct((part // 2, feature), BF)
+    shapes = [jax.ShapeDtypeStruct((RING, part, feature), BF), half, half]
     own = pl.BlockSpec((2, 1, part, feature), lambda i, pos: (0, pos[OWN], 0, 0))
     got = whole(near_got[0])
     return call(
@@ -188,16 +190,36 @@
         (1,),
         (pos,),
         [own, got, got] * 2,
-        [whole(send)] * 4,
-        [send] * 4,
-        scratch=[pltpu.VMEM((RING, part, feature), BF)],
+        [whole(v) for v in shapes],
+        shapes,
         name="rows",
     )(pos, near, *near_got, more, *more_got)
 
 
-def plane_kernel(pos, own, g1, g2, g3, keep, s1, s2, s3, rows):
-    each = own.shape[0] // RING
-    total = own[...].astype(F32) + g1[...].astype(F32) + g2[...].astype(F32) + g3[...].astype(F32)
+def pass_kernel(pos, rows, got_even, got_odd, to_even, to_odd):
+    half = got_even.shape[0]
+    to_even[:half] = rows[pos[PART + 1], :half]
+    to_even[half:] = (rows[pos[PART + 1], half:].astype(F32) + got_odd[...].astype(F32)).astype(BF)
+    to_odd[:half] = (rows[pos[PART + 3], :half].astype(F32) + got_even[...].astype(F32)).astype(BF)
+    to_odd[half:] = rows[pos[PART + 3], half:]
+
+
+def pass_on(pos, rows, got):
+    send = jax.ShapeDtypeStruct(rows.shape[1:], BF)
+    return call(
+        pass_kernel,
+        (1,),
+        (pos,),
+        [whole(v) for v in (rows, *got)],
+        [whole(send)] * 2,
+        [send] * 2,
+        name="pass_on",
+    )(pos, rows, *got)
+
+
+def plane_kernel(pos, own, g1, g2, keep, s1, s2, s3, rows):
+    each = own.shape[1] // RING
+    total = own[pos[PART]].astype(F32) + g1[...].astype(F32) + g2[...].astype(F32)
     for i in range(RING):
         rows[i] = total[i * each : (i + 1) * each]
     keep[...] = rows[pos[SHARE]]
@@ -206,7 +228,7 @@
 
 
 def plane_of(pos, own, got):
-    part, feature = own.shape
+    _, part, feature = own.shape
     each = part // RING
     shapes = [jax.ShapeDtypeStruct((each, feature), F32)] + [jax.ShapeDtypeStruct((each, feature), BF)] * 3
     return call(
@@ -339,6 +361,8 @@
 
     x_even = along(lambda y, x, z: (y, x ^ 1, z))
     x_odd = along(lambda y, x, z: (y, odd_swap(x, RING), z))
+    y_even = along(lambda y, x, z: (y ^ 1, x, z))
+    y_odd = along(lambda y, x, z: (odd_swap(y, RING), x, z))
 
     def exchange(send, even, odd):
         return lax.ppermute(send[0], "vseq", even), lax.ppermute(send[1], "vseq", odd)
@@ -399,16 +423,16 @@
     mixed_video = (
         dot(after(att, *more_send), w0, NT) + got_core[:, feature:].astype(F32) + got_pair.astype(F32)
     ).astype(BF)
-    keep, *sends = rows_of(pos, near, near_got, more, after(more_got, mixed_video))
-    y_got = direct(sends, lambda j, y, x, z: (y ^ j, x, z))
-
-    back_a, back_b = after((back_a, back_b), keep)
+    back_a, back_b = after((back_a, back_b), mixed_video)
     send_b = add_half(g_b, back_a)
     send_a = add_half(g_a, back_b)
     sum_b = lax.ppermute(send_b, "vseq", pb)
     sum_a = lax.ppermute(send_a, "vseq", pa)
 
-    grad_weight, *sends = plane_of(pos, after(keep, send_a, send_b), y_got)
+    rows, *sends = rows_of(pos, near, near_got, more, after(more_got, send_a, send_b))
+    y_got = exchange(sends, y_even, y_odd)
+    y_got = exchange(pass_on(pos, rows, y_got), y_even, y_odd)
+    grad_weight, *sends = plane_of(pos, rows, y_got)
     for got in direct(sends, lambda j, y, x, z: (y, x, z ^ j)):
         grad_weight = grad_weight + got.astype(F32)
 

time: 157 us -> 155 us (0.987)
  starting transfers between devices: 49 us -> 45.8 us
    ppermute x6 -> x3, waiting for transfers between devices: 17 us -> 1.34 us  [direct(): lax.ppermute(send, 'vseq', along(functools.partial(change, j + 1)))]
    ppermute x1, waiting for transfers between devices: 0.01 us -> 8.75 us  [local(): back_b = lax.ppermute(g_bb, 'vseq', pb)]
    ppermute x4 -> x6, waiting for transfers between devices: 12.8 us -> 18.4 us  [exchange(): lax.ppermute(send[1], 'vseq', odd)]
    ppermute x6 -> x3, starting transfers between devices: 11.3 us -> 6.57 us  [direct(): lax.ppermute(send, 'vseq', along(functools.partial(change, j + 1)))]
    ppermute x4 -> x6, waiting for transfers between devices: 24.9 us -> 27.5 us  [exchange(): lax.ppermute(send[0], 'vseq', even)]
    ppermute x4 -> x6, starting transfers between devices: 4.47 us -> 5.73 us  [exchange(): lax.ppermute(send[1], 'vseq', odd)]
  transfers between devices with their start and end apart: 31 -> 32, of which waited for: 20 -> 22; matrix products, arithmetic and copies ran while one was open for 9% -> 9% of each run, Pallas kernels for 14% -> 14%
where the time goes in v4:
time: 155 us; the launch traced here: 154 us
  waiting for transfers between devices  69.9 us (45%)
  starting transfers between devices  45.8 us (30%)
  Pallas kernels  22.7 us (15%)
  local copies, waits for them, and re-layouts  6.81 us (4%)
  matrix products  4.49 us (3%)
  other arithmetic  3.91 us (3%)
    ppermute x6, waiting for transfers between devices, exchange(): lax.ppermute(send[0], 'vseq', even)  27.5 us
    ppermute x6, waiting for transfers between devices, exchange(): lax.ppermute(send[1], 'vseq', odd)  18.4 us
    ppermute x2, starting transfers between devices, halo(): by_b = lax.ppermute(own, 'vseq', pb)  12 us
    ppermute x2, starting transfers between devices, halo(): lax.ppermute(by_a, 'vseq', pb)  9.46 us
    pallas_call x1, Pallas kernels, forward_call(): call(attend_forward, (heads // PAIRED,), (pos,), [by_head] + [kv_head] *...  9.03 us
    ppermute x1, waiting for transfers between devices, local(): back_b = lax.ppermute(g_bb, 'vseq', pb)  8.75 us
    pallas_call x1, Pallas kernels, backward_call(): call(attend_backward, (heads // PAIRED,), (), [by_head] + [kv_head] * 10...  7.52 us
    ppermute x2, waiting for transfers between devices, halo(): lax.ppermute(by_a, 'vseq', pb)  6.91 us
  transfers between devices with their start and end apart: 32, of which 22 were waited for; matrix products, arithmetic and copies ran while one was open for 9% of the time, Pallas kernels for 14%

profile of v4, /device:TPU:32, one launch (start us, length us, event | category | flops | bytes accessed | tf_op | source)
XLA Modules:
  0.0 154.5 jit_solution(13015884944083236757)
XLA Ops:
  1.3 10.0 %collective-permute-start.1 = (bf16[128,768]{1,0:T(8,128)(2,1)}, bf16[128,768]{1,0:T(8,128)(2,1)S(1)}, u32[]{:S(2)}, u32[]{:S(2)}) collective-permute-start(bf16[128,768]{1,0:T(8,128)(2,1)} %k0.1), channel_id=1, source_target_pairs={{0,252},{4,8},{8,4},{12,16},{16,12},{20,24},{24,20},{28,32},{32,28... | collective-permute-start | bytes 589832 | tf_op jit(solution)/shard_map/ppermute | solution.py:392
  11.4 2.0 %collective-permute-start.5 = (bf16[128,768]{1,0:T(8,128)(2,1)}, bf16[128,768]{1,0:T(8,128)(2,1)S(1)}, u32[]{:S(2)}, u32[]{:S(2)}) collective-permute-start(bf16[128,768]{1,0:T(8,128)(2,1)} %v0.3), channel_id=1, source_target_pairs={{0,252},{4,8},{8,4},{12,16},{16,12},{20,24},{24,20},{28,32},{32,28... | collective-permute-start | bytes 589832 | tf_op jit(solution)/shard_map/ppermute | solution.py:392
  16.4 4.7 %dynamic-slice_bitcast_fusion = (bf16[768,768]{1,0:T(8,128)(2,1)S(1)}, bf16[768,768]{1,0:T(8,128)(2,1)S(1)}, bf16[768,768]{1,0:T(8,128)(2,1)S(1)}) fusion(bf16[4,768,768]{2,1,0:T(8,128)(2,1)} %bitcast.36, s32[]{:T(128)} %bitcast.12, s32[]{:T(128)} %bitcast.10, s32[]{:T(128)} %bitcast.5), kind=kLoop, calls=%fused_computation.8 | loop fusion | bytes 7077900 | tf_op jit(solution)/shard_map/jit(dynamic_index_in_dim)/squeeze | solution.py:338
  21.1 1.4 fusion.2
  23.5 1.7 %collective-permute-done.k1 = bf16[128,768]{1,0:T(8,128)(2,1)S(1)} collective-permute-done((bf16[128,768]{1,0:T(8,128)(2,1)}, bf16[128,768]{1,0:T(8,128)(2,1)S(1)}, u32[]{:S(2)}, u32[]{:S(2)}) %collective-permute-start) | collective-permute-done | bytes 196640 | tf_op jit(solution)/shard_map/ppermute | solution.py:391
  25.2 7.2 %collective-permute-start.3 = (bf16[128,768]{1,0:T(8,128)(2,1)S(1)}, bf16[128,768]{1,0:T(8,128)(2,1)S(1)}, u32[]{:S(2)}, u32[]{:S(2)}) collective-permute-start(bf16[128,768]{1,0:T(8,128)(2,1)S(1)} %collective-permute-done.k1), channel_id=1, source_target_pairs={{0,252},{4,8},{8,4},{12,16},{16,12},{20,24},{24,20},{28,32},{32,28... | collective-permute-start | bytes 589832 | tf_op jit(solution)/shard_map/ppermute | solution.py:394
  33.2 2.3 %collective-permute-start.8 = (bf16[128,768]{1,0:T(8,128)(2,1)S(1)}, bf16[128,768]{1,0:T(8,128)(2,1)S(1)}, u32[]{:S(2)}, u32[]{:S(2)}) collective-permute-start(bf16[128,768]{1,0:T(8,128)(2,1)S(1)} %collective-permute-done.4.v1), channel_id=1, source_target_pairs={{0,252},{4,8},{8,4},{12,16},{16,12},{20,24},{24,20},{28,32},{32,28... | collective-permute-start | bytes 589832 | tf_op jit(solution)/shard_map/ppermute | solution.py:394
  36.3 5.3 %collective-permute-done.3.k4 = bf16[128,768]{1,0:T(8,128)(2,1)S(1)} collective-permute-done((bf16[128,768]{1,0:T(8,128)(2,1)S(1)}, bf16[128,768]{1,0:T(8,128)(2,1)S(1)}, u32[]{:S(2)}, u32[]{:S(2)}) %collective-permute-start.3) | collective-permute-done | bytes 196640 | tf_op jit(solution)/shard_map/ppermute | solution.py:394
  41.5 2.6 %collective-permute-done.2.k3 = bf16[128,768]{1,0:T(8,128)(2,1)S(1)} collective-permute-done((bf16[128,768]{1,0:T(8,128)(2,1)S(1)}, bf16[128,768]{1,0:T(8,128)(2,1)S(1)}, u32[]{:S(2)}, u32[]{:S(2)}) %collective-permute-start.2) | collective-permute-done | bytes 196640 | tf_op jit(solution)/shard_map/ppermute | solution.py:394
  44.1 1.6 %collective-permute-done.8.v4 = bf16[128,768]{1,0:T(8,128)(2,1)S(1)} collective-permute-done((bf16[128,768]{1,0:T(8,128)(2,1)S(1)}, bf16[128,768]{1,0:T(8,128)(2,1)S(1)}, u32[]{:S(2)}, u32[]{:S(2)}) %collective-permute-start.8) | collective-permute-done | bytes 196640 | tf_op jit(solution)/shard_map/ppermute | solution.py:394
  46.9 5.9 %collective-permute-start.9 = (bf16[512,768]{1,0:T(8,128)(2,1)S(1)}, bf16[512,768]{1,0:T(8,128)(2,1)S(1)}, u32[]{:S(2)}, u32[]{:S(2)}) collective-permute-start(bf16[512,768]{1,0:T(8,128)(2,1)S(1)} %copy-done.3), channel_id=1, source_target_pairs={{0,2},{1,3},{2,0},{3,1},{4,6},{5,7},{6,4},{7,5},{8,10},{9,11},{10,... | collective-permute-start | bytes 2359304 | tf_op jit(solution)/shard_map/ppermute | solution.py:399
  52.8 9.0 %attend_forward.1 = (bf16[512,768]{1,0:T(8,128)(2,1)S(1)}, bf16[6,640,512]{2,1,0:T(8,128)(2,1)S(1)}, bf16[512,1536]{1,0:T(8,128)(2,1)S(1)}, bf16[2,4,192,768]{3,...) custom-call(s32[36]{0:T(128)S(1)} %get-tuple-element.105.pos, ...), custom_call_target="tpu_custom_call" | custom-call | flops 2013265920 | tf_op jit(solution)/shard_map/attend_forward/pallas_call | solution.py:260
  62.2 8.3 %collective-permute-done.10.got_even = bf16[192,768]{1,0:T(8,128)(2,1)S(1)} collective-permute-done((bf16[192,768]{1,0:T(8,128)(2,1)S(1)}, bf16[192,768]{1,0:T(8,128)(2,1)S(1)}, u32[]{:S(2)}, u32[]{:S(2)}) %collective-permute-start.10) | collective-permute-done | bytes 294944 | tf_op jit(solution)/shard_map/ppermute | solution.py:368
  70.5 1.5 collective-permute-done.11.got_odd
  76.6 2.0 %weight_far.1 = (bf16[2,4,192,768]{3,2,1,0:T(8,128)(2,1)S(1)}, bf16[192,768]{1,0:T(8,128)(2,1)S(1)}, bf16[192,768]{1,0:T(8,128)(2,1)S(1)}) custom-call(s32[36]{0:T(128)S(1)} %get-tuple-element.105.pos, bf16[512,768]{1,0:T(8,128)(2,1)S(1)} %collective-permute-done.9.l0.c0, bf16[512,768]{1,0:T(8,128)(2,1)S(1)} %collective-permute-done.12.l1.c1, ...), custom_call_target="tpu_custom_call" | custom-call | tf_op jit(solution)/shard_map/weight_far/pallas_call | solution.py:140
  78.9 2.3 %collective-permute-start.15 = (bf16[192,768]{1,0:T(8,128)(2,1)S(1)}, bf16[192,768]{1,0:T(8,128)(2,1)S(1)}, u32[]{:S(2)}, u32[]{:S(2)}) collective-permute-start(bf16[192,768]{1,0:T(8,128)(2,1)S(1)} %get-tuple-element.72), channel_id=1, source_target_pairs={{0,48},{4,52},{8,56},{12,60},{16,32},{20,36},{24,40},{28,44},{32,1... | collective-permute-start | bytes 884744 | tf_op jit(solution)/shard_map/ppermute | solution.py:368
  81.3 7.5 %attend_backward.1 = (f32[512,768]{1,0:T(8,128)}, f32[2,128,768]{2,1,0:T(8,128)S(1)}, f32[2,128,768]{2,1,0:T(8,128)S(1)}, f32[2,128,768]{2,1,0:T(8,128)S(1)}, bf...) custom-call(bf16[512,768]{1,0:T(8,128)(2,1)S(1)} %copy-done, bf16[128,768]{1,0:T(8,128)(2,1)S(1)} %copy-done.1, ...), custom_call_target="tpu_custom_call" | custom-call | flops 3019898880 | tf_op jit(solution)/shard_map/attend_backward/pallas_call | solution.py:288
  89.5 5.7 %collective-permute-done.17.near_odd = bf16[2,192,768]{2,1,0:T(8,128)(2,1)S(1)} collective-permute-done((bf16[2,192,768]{2,1,0:T(8,128)(2,1)S(1)}, bf16[2,192,768]{2,1,0:T(8,128)(2,1)S(1)}, u32[]{:S(2)}, u32[]{:S(2)}) %collective-permute-start.17) | collective-permute-done | bytes 589856 | tf_op jit(solution)/shard_map/ppermute | solution.py:368
  95.2 5.3 %collective-permute-done.14.got_even = bf16[192,768]{1,0:T(8,128)(2,1)S(1)} collective-permute-done((bf16[192,768]{1,0:T(8,128)(2,1)S(1)}, bf16[192,768]{1,0:T(8,128)(2,1)S(1)}, u32[]{:S(2)}, u32[]{:S(2)}) %collective-permute-start.14) | collective-permute-done | bytes 294944 | tf_op jit(solution)/shard_map/ppermute | solution.py:368
  100.6 4.0 %collective-permute-done.15.got_odd = bf16[192,768]{1,0:T(8,128)(2,1)S(1)} collective-permute-done((bf16[192,768]{1,0:T(8,128)(2,1)S(1)}, bf16[192,768]{1,0:T(8,128)(2,1)S(1)}, u32[]{:S(2)}, u32[]{:S(2)}) %collective-permute-start.15) | collective-permute-done | bytes 294944 | tf_op jit(solution)/shard_map/ppermute | solution.py:368
  106.4 1.5 fusion
  107.9 1.1 add_convert_fusion
  109.0 8.7 %collective-permute-done.20 = bf16[2,128,768]{2,1,0:T(8,128)(2,1)S(1)} collective-permute-done((bf16[2,128,768]{2,1,0:T(8,128)(2,1)S(1)}, bf16[2,128,768]{2,1,0:T(8,128)(2,1)S(1)}, u32[]{:S(2)}, u32[]{:S(2)}) %collective-permute-start.20) | collective-permute-done | bytes 393248 | tf_op jit(solution)/shard_map/ppermute | solution.py:419
  118.0 1.6 %collective-permute-done.23.more_even = bf16[2,192,768]{2,1,0:T(8,128)(2,1)S(1)} collective-permute-done((bf16[2,192,768]{2,1,0:T(8,128)(2,1)S(1)}, bf16[2,192,768]{2,1,0:T(8,128)(2,1)S(1)}, u32[]{:S(2)}, u32[]{:S(2)}) %collective-permute-start.23) | collective-permute-done | bytes 589856 | tf_op jit(solution)/shard_map/ppermute | solution.py:368
  119.6 1.5 collective-permute-done.24.more_odd
  121.1 1.4 rows.1
  123.3 1.7 %collective-permute-start.22 = (bf16[2,128,768]{2,1,0:T(8,128)(2,1)S(1)}, bf16[2,128,768]{2,1,0:T(8,128)(2,1)S(1)}, u32[]{:S(2)}, u32[]{:S(2)}) collective-permute-start(bf16[2,128,768]{2,1,0:T(8,128)(2,1)S(1)} %add_convert_fusion.2), channel_id=1, source_target_pairs={{0,252},{4,8},{8,4},{12,16},{16,12},{20,24},{24,20},{28,32},{32,28... | collective-permute-start | bytes 1179656 | tf_op jit(solution)/shard_map/ppermute | solution.py:429
  124.9 2.8 %collective-permute-done.25.got_even = bf16[96,768]{1,0:T(8,128)(2,1)S(1)} collective-permute-done((bf16[96,768]{1,0:T(8,128)(2,1)S(1)}, bf16[96,768]{1,0:T(8,128)(2,1)S(1)}, u32[]{:S(2)}, u32[]{:S(2)}) %collective-permute-start.25) | collective-permute-done | bytes 147488 | tf_op jit(solution)/shard_map/ppermute | solution.py:368
  127.7 1.3 collective-permute-done.26.got_odd
  131.1 8.7 %collective-permute-done.27.g1 = bf16[192,768]{1,0:T(8,128)(2,1)S(1)} collective-permute-done((bf16[192,768]{1,0:T(8,128)(2,1)S(1)}, bf16[192,768]{1,0:T(8,128)(2,1)S(1)}, u32[]{:S(2)}, u32[]{:S(2)}) %collective-permute-start.27) | collective-permute-done | bytes 294944 | tf_op jit(solution)/shard_map/ppermute | solution.py:368
  139.8 4.3 %collective-permute-done.28.g2 = bf16[192,768]{1,0:T(8,128)(2,1)S(1)} collective-permute-done((bf16[192,768]{1,0:T(8,128)(2,1)S(1)}, bf16[192,768]{1,0:T(8,128)(2,1)S(1)}, u32[]{:S(2)}, u32[]{:S(2)}) %collective-permute-start.28) | collective-permute-done | bytes 294944 | tf_op jit(solution)/shard_map/ppermute | solution.py:368
  145.1 6.4 %collective-permute-start.31 = (bf16[48,768]{1,0:T(8,128)(2,1)S(1)}, bf16[48,768]{1,0:T(8,128)(2,1)S(1)}, u32[]{:S(2)}, u32[]{:S(2)}) collective-permute-start(bf16[48,768]{1,0:T(8,128)(2,1)S(1)} %get-tuple-element.98), channel_id=1, source_target_pairs={{0,12},{4,8},{8,4},{12,0},{16,28},{20,24},{24,20},{28,16},{32,44},... | collective-permute-start | bytes 221192 | tf_op jit(solution)/shard_map/ppermute | solution.py:372
  (67 shorter events, 22.1 us)
Async XLA Ops:
  1.3 22.1 %collective-permute-start.1 = (bf16[128,768]{1,0:T(8,128)(2,1)}, bf16[128,768]{1,0:T(8,128)(2,1)S(1)}, u32[]{:S(2)}, u32[]{:S(2)}) collective-permute-start(bf16[128,768]{1,0:T(8,128)(2,1)} %k0.1), channel_id=1, source_target_pairs={{0,252},{4,8},{8,4},{12,16},{16,12},{20,24},{24,20},{28,32},{32,28... | collective-permute-start | bytes 589832 | tf_op jit(solution)/shard_map/ppermute | solution.py:392
  11.4 13.8 %collective-permute-start = (bf16[128,768]{1,0:T(8,128)(2,1)}, bf16[128,768]{1,0:T(8,128)(2,1)S(1)}, u32[]{:S(2)}, u32[]{:S(2)}) collective-permute-start(bf16[128,768]{1,0:T(8,128)(2,1)} %k0.1), channel_id=1, source_target_pairs={{0,4},{4,0},{8,12},{12,8},{16,20},{20,16},{24,28},{28,24},{32,36},... | collective-permute-start | bytes 589832 | tf_op jit(solution)/shard_map/ppermute | solution.py:391
  11.4 21.8 %collective-permute-start.5 = (bf16[128,768]{1,0:T(8,128)(2,1)}, bf16[128,768]{1,0:T(8,128)(2,1)S(1)}, u32[]{:S(2)}, u32[]{:S(2)}) collective-permute-start(bf16[128,768]{1,0:T(8,128)(2,1)} %v0.3), channel_id=1, source_target_pairs={{0,252},{4,8},{8,4},{12,16},{16,12},{20,24},{24,20},{28,32},{32,28... | collective-permute-start | bytes 589832 | tf_op jit(solution)/shard_map/ppermute | solution.py:392
  13.4 19.8 %collective-permute-start.4 = (bf16[128,768]{1,0:T(8,128)(2,1)}, bf16[128,768]{1,0:T(8,128)(2,1)S(1)}, u32[]{:S(2)}, u32[]{:S(2)}) collective-permute-start(bf16[128,768]{1,0:T(8,128)(2,1)} %v0.3), channel_id=1, source_target_pairs={{0,4},{4,0},{8,12},{12,8},{16,20},{20,16},{24,28},{28,24},{32,36},... | collective-permute-start | bytes 589832 | tf_op jit(solution)/shard_map/ppermute | solution.py:391
  14.3 18.0 %collective-permute-start.6 = (bf16[512,768]{1,0:T(8,128)(2,1)}, bf16[512,768]{1,0:T(8,128)(2,1)S(1)}, u32[]{:S(2)}, u32[]{:S(2)}) collective-permute-start(bf16[512,768]{1,0:T(8,128)(2,1)} %l0.1), channel_id=1, source_target_pairs={{0,1},{1,0},{2,3},{3,2},{4,5},{5,4},{6,7},{7,6},{8,9},{9,8},{10,11... | collective-permute-start | bytes 2359304 | tf_op jit(solution)/shard_map/ppermute | solution.py:387
  25.2 16.4 %collective-permute-start.3 = (bf16[128,768]{1,0:T(8,128)(2,1)S(1)}, bf16[128,768]{1,0:T(8,128)(2,1)S(1)}, u32[]{:S(2)}, u32[]{:S(2)}) collective-permute-start(bf16[128,768]{1,0:T(8,128)(2,1)S(1)} %collective-permute-done.k1), channel_id=1, source_target_pairs={{0,252},{4,8},{8,4},{12,16},{16,12},{20,24},{24,20},{28,32},{32,28... | collective-permute-start | bytes 589832 | tf_op jit(solution)/shard_map/ppermute | solution.py:394
  32.3 11.8 %collective-permute-start.2 = (bf16[128,768]{1,0:T(8,128)(2,1)S(1)}, bf16[128,768]{1,0:T(8,128)(2,1)S(1)}, u32[]{:S(2)}, u32[]{:S(2)}) collective-permute-start(bf16[128,768]{1,0:T(8,128)(2,1)S(1)} %collective-permute-done.1.k2), channel_id=1, source_target_pairs={{0,4},{4,0},{8,12},{12,8},{16,20},{20,16},{24,28},{28,24},{32,36},... | collective-permute-start | bytes 589832 | tf_op jit(solution)/shard_map/ppermute | solution.py:394
  33.2 12.6 %collective-permute-start.8 = (bf16[128,768]{1,0:T(8,128)(2,1)S(1)}, bf16[128,768]{1,0:T(8,128)(2,1)S(1)}, u32[]{:S(2)}, u32[]{:S(2)}) collective-permute-start(bf16[128,768]{1,0:T(8,128)(2,1)S(1)} %collective-permute-done.4.v1), channel_id=1, source_target_pairs={{0,252},{4,8},{8,4},{12,16},{16,12},{20,24},{24,20},{28,32},{32,28... | collective-permute-start | bytes 589832 | tf_op jit(solution)/shard_map/ppermute | solution.py:394
  35.4 11.4 %collective-permute-start.7 = (bf16[128,768]{1,0:T(8,128)(2,1)S(1)}, bf16[128,768]{1,0:T(8,128)(2,1)S(1)}, u32[]{:S(2)}, u32[]{:S(2)}) collective-permute-start(bf16[128,768]{1,0:T(8,128)(2,1)S(1)} %collective-permute-done.5.v2), channel_id=1, source_target_pairs={{0,4},{4,0},{8,12},{12,8},{16,20},{20,16},{24,28},{28,24},{32,36},... | collective-permute-start | bytes 589832 | tf_op jit(solution)/shard_map/ppermute | solution.py:394
  46.9 25.1 %collective-permute-start.9 = (bf16[512,768]{1,0:T(8,128)(2,1)S(1)}, bf16[512,768]{1,0:T(8,128)(2,1)S(1)}, u32[]{:S(2)}, u32[]{:S(2)}) collective-permute-start(bf16[512,768]{1,0:T(8,128)(2,1)S(1)} %copy-done.3), channel_id=1, source_target_pairs={{0,2},{1,3},{2,0},{3,1},{4,6},{5,7},{6,4},{7,5},{8,10},{9,11},{10,... | collective-permute-start | bytes 2359304 | tf_op jit(solution)/shard_map/ppermute | solution.py:399
  61.8 8.7 %collective-permute-start.10 = (bf16[192,768]{1,0:T(8,128)(2,1)S(1)}, bf16[192,768]{1,0:T(8,128)(2,1)S(1)}, u32[]{:S(2)}, u32[]{:S(2)}) collective-permute-start(bf16[192,768]{1,0:T(8,128)(2,1)S(1)} %get-tuple-element.60), channel_id=1, source_target_pairs={{0,16},{4,20},{8,24},{12,28},{16,0},{20,4},{24,8},{28,12},{32,48},... | collective-permute-start | bytes 884744 | tf_op jit(solution)/shard_map/ppermute | solution.py:368
  61.9 10.1 %collective-permute-start.11 = (bf16[192,768]{1,0:T(8,128)(2,1)S(1)}, bf16[192,768]{1,0:T(8,128)(2,1)S(1)}, u32[]{:S(2)}, u32[]{:S(2)}) collective-permute-start(bf16[192,768]{1,0:T(8,128)(2,1)S(1)} %get-tuple-element.61), channel_id=1, source_target_pairs={{0,48},{4,52},{8,56},{12,60},{16,32},{20,36},{24,40},{28,44},{32,1... | collective-permute-start | bytes 884744 | tf_op jit(solution)/shard_map/ppermute | solution.py:368
  72.0 3.4 %collective-permute-start.13 = (bf16[512,1536]{1,0:T(8,128)(2,1)S(1)}, bf16[512,1536]{1,0:T(8,128)(2,1)S(1)}, u32[]{:S(2)}, u32[]{:S(2)}) collective-permute-start(bf16[512,1536]{1,0:T(8,128)(2,1)S(1)} %get-tuple-element.68), channel_id=1, source_target_pairs={{0,1},{1,0},{2,3},{3,2},{4,5},{5,4},{6,7},{7,6},{8,9},{9,8},{10,11... | collective-permute-start | bytes 4718600 | tf_op jit(solution)/shard_map/ppermute | solution.py:407
  72.0 4.6 %collective-permute-start.12 = (bf16[512,768]{1,0:T(8,128)(2,1)S(1)}, bf16[512,768]{1,0:T(8,128)(2,1)S(1)}, u32[]{:S(2)}, u32[]{:S(2)}) collective-permute-start(bf16[512,768]{1,0:T(8,128)(2,1)S(1)} %collective-permute-done.9.l0.c0), channel_id=1, source_target_pairs={{0,1},{1,0},{2,3},{3,2},{4,5},{5,4},{6,7},{7,6},{8,9},{9,8},{10,11... | collective-permute-start | bytes 2359304 | tf_op jit(solution)/shard_map/ppermute | solution.py:406
  73.2 16.3 %collective-permute-start.16 = (bf16[2,192,768]{2,1,0:T(8,128)(2,1)S(1)}, bf16[2,192,768]{2,1,0:T(8,128)(2,1)S(1)}, u32[]{:S(2)}, u32[]{:S(2)}) collective-permute-start(bf16[2,192,768]{2,1,0:T(8,128)(2,1)S(1)} %get-tuple-element.64), channel_id=1, source_target_pairs={{0,16},{4,20},{8,24},{12,28},{16,0},{20,4},{24,8},{28,12},{32,48},... | collective-permute-start | bytes 1769480 | tf_op jit(solution)/shard_map/ppermute | solution.py:368
  73.5 21.7 %collective-permute-start.17 = (bf16[2,192,768]{2,1,0:T(8,128)(2,1)S(1)}, bf16[2,192,768]{2,1,0:T(8,128)(2,1)S(1)}, u32[]{:S(2)}, u32[]{:S(2)}) collective-permute-start(bf16[2,192,768]{2,1,0:T(8,128)(2,1)S(1)} %get-tuple-element.65), channel_id=1, source_target_pairs={{0,48},{4,52},{8,56},{12,60},{16,32},{20,36},{24,40},{28,44},{32,1... | collective-permute-start | bytes 1769480 | tf_op jit(solution)/shard_map/ppermute | solution.py:368
  76.2 31.7 %collective-permute-start.18 = (bf16[512,768]{1,0:T(8,128)(2,1)S(1)}, bf16[512,768]{1,0:T(8,128)(2,1)S(1)}, u32[]{:S(2)}, u32[]{:S(2)}) collective-permute-start(bf16[512,768]{1,0:T(8,128)(2,1)S(1)} %add_convert_fusion.1), channel_id=1, source_target_pairs={{0,2},{1,3},{2,0},{3,1},{4,6},{5,7},{6,4},{7,5},{8,10},{9,11},{10,... | collective-permute-start | bytes 2359304 | tf_op jit(solution)/shard_map/ppermute | solution.py:411
  78.6 22.0 %collective-permute-start.14 = (bf16[192,768]{1,0:T(8,128)(2,1)S(1)}, bf16[192,768]{1,0:T(8,128)(2,1)S(1)}, u32[]{:S(2)}, u32[]{:S(2)}) collective-permute-start(bf16[192,768]{1,0:T(8,128)(2,1)S(1)} %get-tuple-element.71), channel_id=1, source_target_pairs={{0,16},{4,20},{8,24},{12,28},{16,0},{20,4},{24,8},{28,12},{32,48},... | collective-permute-start | bytes 884744 | tf_op jit(solution)/shard_map/ppermute | solution.py:368
  78.9 25.6 %collective-permute-start.15 = (bf16[192,768]{1,0:T(8,128)(2,1)S(1)}, bf16[192,768]{1,0:T(8,128)(2,1)S(1)}, u32[]{:S(2)}, u32[]{:S(2)}) collective-permute-start(bf16[192,768]{1,0:T(8,128)(2,1)S(1)} %get-tuple-element.72), channel_id=1, source_target_pairs={{0,48},{4,52},{8,56},{12,60},{16,32},{20,36},{24,40},{28,44},{32,1... | collective-permute-start | bytes 884744 | tf_op jit(solution)/shard_map/ppermute | solution.py:368
  89.5 19.5 %collective-permute-start.19 = (bf16[2,128,768]{2,1,0:T(8,128)(2,1)S(1)}, bf16[2,128,768]{2,1,0:T(8,128)(2,1)S(1)}, u32[]{:S(2)}, u32[]{:S(2)}) collective-permute-start(bf16[2,128,768]{2,1,0:T(8,128)(2,1)S(1)} %get-tuple-element.75), channel_id=1, source_target_pairs={{0,4},{4,0},{8,12},{12,8},{16,20},{20,16},{24,28},{28,24},{32,36},... | collective-permute-start | bytes 1179656 | tf_op jit(solution)/shard_map/ppermute | solution.py:418
  95.2 22.6 %collective-permute-start.20 = (bf16[2,128,768]{2,1,0:T(8,128)(2,1)S(1)}, bf16[2,128,768]{2,1,0:T(8,128)(2,1)S(1)}, u32[]{:S(2)}, u32[]{:S(2)}) collective-permute-start(bf16[2,128,768]{2,1,0:T(8,128)(2,1)S(1)} %get-tuple-element.76), channel_id=1, source_target_pairs={{0,252},{4,8},{8,4},{12,16},{16,12},{20,24},{24,20},{28,32},{32,28... | collective-permute-start | bytes 1179656 | tf_op jit(solution)/shard_map/ppermute | solution.py:419
  105.3 14.3 %collective-permute-start.23 = (bf16[2,192,768]{2,1,0:T(8,128)(2,1)S(1)}, bf16[2,192,768]{2,1,0:T(8,128)(2,1)S(1)}, u32[]{:S(2)}, u32[]{:S(2)}) collective-permute-start(bf16[2,192,768]{2,1,0:T(8,128)(2,1)S(1)} %get-tuple-element.79), channel_id=1, source_target_pairs={{0,16},{4,20},{8,24},{12,28},{16,0},{20,4},{24,8},{28,12},{32,48},... | collective-permute-start | bytes 1769480 | tf_op jit(solution)/shard_map/ppermute | solution.py:368
  105.4 15.7 %collective-permute-start.24 = (bf16[2,192,768]{2,1,0:T(8,128)(2,1)S(1)}, bf16[2,192,768]{2,1,0:T(8,128)(2,1)S(1)}, u32[]{:S(2)}, u32[]{:S(2)}) collective-permute-start(bf16[2,192,768]{2,1,0:T(8,128)(2,1)S(1)} %get-tuple-element.80), channel_id=1, source_target_pairs={{0,48},{4,52},{8,56},{12,60},{16,32},{20,36},{24,40},{28,44},{32,1... | collective-permute-start | bytes 1769480 | tf_op jit(solution)/shard_map/ppermute | solution.py:368
  122.5 5.2 %collective-permute-start.25 = (bf16[96,768]{1,0:T(8,128)(2,1)S(1)}, bf16[96,768]{1,0:T(8,128)(2,1)S(1)}, u32[]{:S(2)}, u32[]{:S(2)}) collective-permute-start(bf16[96,768]{1,0:T(8,128)(2,1)S(1)} %get-tuple-element.91), channel_id=1, source_target_pairs={{0,64},{4,68},{8,72},{12,76},{16,80},{20,84},{24,88},{28,92},{32,9... | collective-permute-start | bytes 442376 | tf_op jit(solution)/shard_map/ppermute | solution.py:368
  122.6 6.4 %collective-permute-start.26 = (bf16[96,768]{1,0:T(8,128)(2,1)S(1)}, bf16[96,768]{1,0:T(8,128)(2,1)S(1)}, u32[]{:S(2)}, u32[]{:S(2)}) collective-permute-start(bf16[96,768]{1,0:T(8,128)(2,1)S(1)} %get-tuple-element.92), channel_id=1, source_target_pairs={{0,192},{4,196},{8,200},{12,204},{16,208},{20,212},{24,216},{28,22... | collective-permute-start | bytes 442376 | tf_op jit(solution)/shard_map/ppermute | solution.py:368
  123.3 28.2 %collective-permute-start.21 = (bf16[2,128,768]{2,1,0:T(8,128)(2,1)S(1)}, bf16[2,128,768]{2,1,0:T(8,128)(2,1)S(1)}, u32[]{:S(2)}, u32[]{:S(2)}) collective-permute-start(bf16[2,128,768]{2,1,0:T(8,128)(2,1)S(1)} %add_convert_fusion.3), channel_id=1, source_target_pairs={{0,4},{4,0},{8,12},{12,8},{16,20},{20,16},{24,28},{28,24},{32,36},... | collective-permute-start | bytes 1179656 | tf_op jit(solution)/shard_map/ppermute | solution.py:430
  123.3 28.2 %collective-permute-start.22 = (bf16[2,128,768]{2,1,0:T(8,128)(2,1)S(1)}, bf16[2,128,768]{2,1,0:T(8,128)(2,1)S(1)}, u32[]{:S(2)}, u32[]{:S(2)}) collective-permute-start(bf16[2,128,768]{2,1,0:T(8,128)(2,1)S(1)} %add_convert_fusion.2), channel_id=1, source_target_pairs={{0,252},{4,8},{8,4},{12,16},{16,12},{20,24},{24,20},{28,32},{32,28... | collective-permute-start | bytes 1179656 | tf_op jit(solution)/shard_map/ppermute | solution.py:429
  129.7 10.1 %collective-permute-start.27 = (bf16[192,768]{1,0:T(8,128)(2,1)S(1)}, bf16[192,768]{1,0:T(8,128)(2,1)S(1)}, u32[]{:S(2)}, u32[]{:S(2)}) collective-permute-start(bf16[192,768]{1,0:T(8,128)(2,1)S(1)} %get-tuple-element.93), channel_id=1, source_target_pairs={{0,64},{4,68},{8,72},{12,76},{16,80},{20,84},{24,88},{28,92},{32,9... | collective-permute-start | bytes 884744 | tf_op jit(solution)/shard_map/ppermute | solution.py:368
  130.5 13.6 %collective-permute-start.28 = (bf16[192,768]{1,0:T(8,128)(2,1)S(1)}, bf16[192,768]{1,0:T(8,128)(2,1)S(1)}, u32[]{:S(2)}, u32[]{:S(2)}) collective-permute-start(bf16[192,768]{1,0:T(8,128)(2,1)S(1)} %get-tuple-element.94), channel_id=1, source_target_pairs={{0,192},{4,196},{8,200},{12,204},{16,208},{20,212},{24,216},{28,22... | collective-permute-start | bytes 884744 | tf_op jit(solution)/shard_map/ppermute | solution.py:368
  144.9 7.6 %collective-permute-start.29 = (bf16[48,768]{1,0:T(8,128)(2,1)S(1)}, bf16[48,768]{1,0:T(8,128)(2,1)S(1)}, u32[]{:S(2)}, u32[]{:S(2)}) collective-permute-start(bf16[48,768]{1,0:T(8,128)(2,1)S(1)} %get-tuple-element.96), channel_id=1, source_target_pairs={{0,4},{4,0},{8,12},{12,8},{16,20},{20,16},{24,28},{28,24},{32,36},... | collective-permute-start | bytes 221192 | tf_op jit(solution)/shard_map/ppermute | solution.py:372
  145.0 8.3 %collective-permute-start.30 = (bf16[48,768]{1,0:T(8,128)(2,1)S(1)}, bf16[48,768]{1,0:T(8,128)(2,1)S(1)}, u32[]{:S(2)}, u32[]{:S(2)}) collective-permute-start(bf16[48,768]{1,0:T(8,128)(2,1)S(1)} %get-tuple-element.97), channel_id=1, source_target_pairs={{0,8},{4,12},{8,0},{12,4},{16,24},{20,28},{24,16},{28,20},{32,40},... | collective-permute-start | bytes 221192 | tf_op jit(solution)/shard_map/ppermute | solution.py:372
  145.1 8.7 %collective-permute-start.31 = (bf16[48,768]{1,0:T(8,128)(2,1)S(1)}, bf16[48,768]{1,0:T(8,128)(2,1)S(1)}, u32[]{:S(2)}, u32[]{:S(2)}) collective-permute-start(bf16[48,768]{1,0:T(8,128)(2,1)S(1)} %get-tuple-element.98), channel_id=1, source_target_pairs={{0,12},{4,8},{8,4},{12,0},{16,28},{20,24},{24,20},{28,16},{32,44},... | collective-permute-start | bytes 221192 | tf_op jit(solution)/shard_map/ppermute | solution.py:372
  (5 other events, 99.3 us)

commit v5 on v4

--- a/solution.py
+++ b/solution.py
@@ -74,18 +74,10 @@
 
 def attend_backward(
     q_ref, k0, k1, k2, k3, k4, v0, v1, v2, v3, v4, p_ref, att_ref, near_ref, c0, c1, w0, w1,
-    dq_ref, g0, g1, g2, g3, g4, all_ref,
+    dq_ref, g0, g1, g2, g3, g4,
 ):
-    head = pl.program_id(0)
-
-    @pl.when(head == 0)
-    def _():
-        total = near_ref[...] + dot(c0[...], w0[...], NN) + dot(c1[...], w1[...], NN)
-        all_ref[...] = total.astype(BF)
-
-    grads = (g0, g1, g2, g3, g4)
     rows = k0.shape[0]
-    wide = all_ref[:, pl.ds(pl.multiple_of(head * PAIRED * HEAD, PAIRED * HEAD), PAIRED * HEAD)]
+    wide = (near_ref[...] + dot(c0[...], w0[...], NN) + dot(c1[...], w1[...], NN)).astype(BF)
     for u in range(PAIRED):
         own = slice(u * HEAD, (u + 1) * HEAD)
         q = q_ref[:, own]
@@ -291,12 +283,12 @@
         (),
         [by_head]
         + [kv_head] * 10
-        + [pl.BlockSpec((PAIRED, band, tokens), lambda h: (h, 0, 0)), by_head]
-        + [whole(v) for v in (near, *cots, *weights)],
+        + [pl.BlockSpec((PAIRED, band, tokens), lambda h: (h, 0, 0)), by_head, by_head]
+        + [whole(v) for v in cots]
+        + [pl.BlockSpec((feature, PAIRED * HEAD), lambda h: (0, h))] * len(weights),
         [by_head] + [both_head] * 5,
         [jax.ShapeDtypeStruct((tokens, feature), F32)]
         + [piece(F32), piece(F32), piece(F32), piece(BF), piece(BF)],
-        scratch=[pltpu.VMEM((tokens, feature), BF)],
         name="attend_backward",
         cost=pl.CostEstimate(
             flops=12 * tokens * band * feature, bytes_accessed=0, transcendentals=0

time: 155 us -> 155 us (level)
  waiting for transfers between devices: 69.9 us -> 61.3 us
  starting transfers between devices: 45.8 us -> 52.4 us
  Pallas kernels: 22.7 us -> 25.3 us
    ppermute x6, waiting for transfers between devices: 18.4 us -> 9.61 us  [exchange(): lax.ppermute(send[1], 'vseq', odd)]
    ppermute x6, waiting for transfers between devices: 27.5 us -> 21.5 us  [exchange(): lax.ppermute(send[0], 'vseq', even)]
    ppermute x1, waiting for transfers between devices: 0.01 us -> 4.5 us  [local(): got_pair = lax.ppermute(far_pair, 'aseq', PAIR)]
    ppermute x1, starting transfers between devices: 1.66 us -> 4.58 us  [local(): sum_b = lax.ppermute(send_b, 'vseq', pb)]
    pallas_call x1, Pallas kernels: 7.52 us -> 10.1 us  [backward_call(): call(attend_backward, (heads // PAIRED,), (), [by_head] + [kv_head] * 10...]
    ppermute x1, starting transfers between devices: 0.01 us -> 2.11 us  [local(): back_b = lax.ppermute(g_bb, 'vseq', pb)]
  transfers between devices with their start and end apart: 32 -> 32, of which waited for: 22 -> 19; matrix products, arithmetic and copies ran while one was open for 9% -> 9% of each run, Pallas kernels for 14% -> 15%
where the time goes in v5:
time: 155 us
  waiting for transfers between devices  61.3 us (40%)
  starting transfers between devices  52.4 us (34%)
  Pallas kernels  25.3 us (16%)
  local copies, waits for them, and re-layouts  6.81 us (4%)
  matrix products  4.49 us (3%)
  other arithmetic  3.91 us (3%)
    ppermute x6, waiting for transfers between devices, exchange(): lax.ppermute(send[0], 'vseq', even)  21.5 us
    ppermute x2, starting transfers between devices, halo(): by_b = lax.ppermute(own, 'vseq', pb)  12 us
    pallas_call x1, Pallas kernels, backward_call(): call(attend_backward, (heads // PAIRED,), (), [by_head] + [kv_head] * 10...  10.1 us
    ppermute x1, waiting for transfers between devices, local(): back_b = lax.ppermute(g_bb, 'vseq', pb)  9.95 us
    ppermute x6, waiting for transfers between devices, exchange(): lax.ppermute(send[1], 'vseq', odd)  9.61 us
    ppermute x2, starting transfers between devices, halo(): lax.ppermute(by_a, 'vseq', pb)  9.46 us
    pallas_call x1, Pallas kernels, forward_call(): call(attend_forward, (heads // PAIRED,), (pos,), [by_head] + [kv_head] *...  9.03 us
    ppermute x6, starting transfers between devices, exchange(): lax.ppermute(send[1], 'vseq', odd)  7.28 us
  transfers between devices with their start and end apart: 32, of which 19 were waited for; matrix products, arithmetic and copies ran while one was open for 9% of the time, Pallas kernels for 15%

profile of v5, /device:TPU:32, one launch (start us, length us, event | category | flops | bytes accessed | tf_op | source)
XLA Modules:
  0.0 155.1 jit_solution(4633804219501017309)
XLA Ops:
  1.3 10.0 %collective-permute-start.1 = (bf16[128,768]{1,0:T(8,128)(2,1)}, bf16[128,768]{1,0:T(8,128)(2,1)S(1)}, u32[]{:S(2)}, u32[]{:S(2)}) collective-permute-start(bf16[128,768]{1,0:T(8,128)(2,1)} %k0.1), channel_id=1, source_target_pairs={{0,252},{4,8},{8,4},{12,16},{16,12},{20,24},{24,20},{28,32},{32,28... | collective-permute-start | bytes 589832 | tf_op jit(solution)/shard_map/ppermute | solution.py:384
  11.4 2.0 %collective-permute-start.5 = (bf16[128,768]{1,0:T(8,128)(2,1)}, bf16[128,768]{1,0:T(8,128)(2,1)S(1)}, u32[]{:S(2)}, u32[]{:S(2)}) collective-permute-start(bf16[128,768]{1,0:T(8,128)(2,1)} %v0.3), channel_id=1, source_target_pairs={{0,252},{4,8},{8,4},{12,16},{16,12},{20,24},{24,20},{28,32},{32,28... | collective-permute-start | bytes 589832 | tf_op jit(solution)/shard_map/ppermute | solution.py:384
  16.4 4.7 %dynamic-slice_bitcast_fusion = (bf16[768,768]{1,0:T(8,128)(2,1)S(1)}, bf16[768,768]{1,0:T(8,128)(2,1)S(1)}, bf16[768,768]{1,0:T(8,128)(2,1)S(1)}) fusion(bf16[4,768,768]{2,1,0:T(8,128)(2,1)} %bitcast.36, s32[]{:T(128)} %bitcast.12, s32[]{:T(128)} %bitcast.10, s32[]{:T(128)} %bitcast.5), kind=kLoop, calls=%fused_computation.8 | loop fusion | bytes 7077900 | tf_op jit(solution)/shard_map/jit(dynamic_index_in_dim)/squeeze | solution.py:330
  21.1 1.4 fusion.2
  23.5 1.7 %collective-permute-done.k1 = bf16[128,768]{1,0:T(8,128)(2,1)S(1)} collective-permute-done((bf16[128,768]{1,0:T(8,128)(2,1)}, bf16[128,768]{1,0:T(8,128)(2,1)S(1)}, u32[]{:S(2)}, u32[]{:S(2)}) %collective-permute-start) | collective-permute-done | bytes 196640 | tf_op jit(solution)/shard_map/ppermute | solution.py:383
  25.2 7.2 %collective-permute-start.3 = (bf16[128,768]{1,0:T(8,128)(2,1)S(1)}, bf16[128,768]{1,0:T(8,128)(2,1)S(1)}, u32[]{:S(2)}, u32[]{:S(2)}) collective-permute-start(bf16[128,768]{1,0:T(8,128)(2,1)S(1)} %collective-permute-done.k1), channel_id=1, source_target_pairs={{0,252},{4,8},{8,4},{12,16},{16,12},{20,24},{24,20},{28,32},{32,28... | collective-permute-start | bytes 589832 | tf_op jit(solution)/shard_map/ppermute | solution.py:386
  33.2 2.3 %collective-permute-start.8 = (bf16[128,768]{1,0:T(8,128)(2,1)S(1)}, bf16[128,768]{1,0:T(8,128)(2,1)S(1)}, u32[]{:S(2)}, u32[]{:S(2)}) collective-permute-start(bf16[128,768]{1,0:T(8,128)(2,1)S(1)} %collective-permute-done.4.v1), channel_id=1, source_target_pairs={{0,252},{4,8},{8,4},{12,16},{16,12},{20,24},{24,20},{28,32},{32,28... | collective-permute-start | bytes 589832 | tf_op jit(solution)/shard_map/ppermute | solution.py:386
  36.3 5.3 %collective-permute-done.3.k4 = bf16[128,768]{1,0:T(8,128)(2,1)S(1)} collective-permute-done((bf16[128,768]{1,0:T(8,128)(2,1)S(1)}, bf16[128,768]{1,0:T(8,128)(2,1)S(1)}, u32[]{:S(2)}, u32[]{:S(2)}) %collective-permute-start.3) | collective-permute-done | bytes 196640 | tf_op jit(solution)/shard_map/ppermute | solution.py:386
  41.5 2.6 %collective-permute-done.2.k3 = bf16[128,768]{1,0:T(8,128)(2,1)S(1)} collective-permute-done((bf16[128,768]{1,0:T(8,128)(2,1)S(1)}, bf16[128,768]{1,0:T(8,128)(2,1)S(1)}, u32[]{:S(2)}, u32[]{:S(2)}) %collective-permute-start.2) | collective-permute-done | bytes 196640 | tf_op jit(solution)/shard_map/ppermute | solution.py:386
  44.1 1.6 %collective-permute-done.8.v4 = bf16[128,768]{1,0:T(8,128)(2,1)S(1)} collective-permute-done((bf16[128,768]{1,0:T(8,128)(2,1)S(1)}, bf16[128,768]{1,0:T(8,128)(2,1)S(1)}, u32[]{:S(2)}, u32[]{:S(2)}) %collective-permute-start.8) | collective-permute-done | bytes 196640 | tf_op jit(solution)/shard_map/ppermute | solution.py:386
  46.9 5.9 %collective-permute-start.9 = (bf16[512,768]{1,0:T(8,128)(2,1)S(1)}, bf16[512,768]{1,0:T(8,128)(2,1)S(1)}, u32[]{:S(2)}, u32[]{:S(2)}) collective-permute-start(bf16[512,768]{1,0:T(8,128)(2,1)S(1)} %copy-done.3), channel_id=1, source_target_pairs={{0,2},{1,3},{2,0},{3,1},{4,6},{5,7},{6,4},{7,5},{8,10},{9,11},{10,... | collective-permute-start | bytes 2359304 | tf_op jit(solution)/shard_map/ppermute | solution.py:391
  52.8 9.0 %attend_forward.1 = (bf16[512,768]{1,0:T(8,128)(2,1)S(1)}, bf16[6,640,512]{2,1,0:T(8,128)(2,1)S(1)}, bf16[512,1536]{1,0:T(8,128)(2,1)S(1)}, bf16[2,4,192,768]{3,...) custom-call(s32[36]{0:T(128)S(1)} %get-tuple-element.105.pos, ...), custom_call_target="tpu_custom_call" | custom-call | flops 2013265920 | tf_op jit(solution)/shard_map/attend_forward/pallas_call | solution.py:252
  62.2 8.3 %collective-permute-done.10.got_even = bf16[192,768]{1,0:T(8,128)(2,1)S(1)} collective-permute-done((bf16[192,768]{1,0:T(8,128)(2,1)S(1)}, bf16[192,768]{1,0:T(8,128)(2,1)S(1)}, u32[]{:S(2)}, u32[]{:S(2)}) %collective-permute-start.10) | collective-permute-done | bytes 294944 | tf_op jit(solution)/shard_map/ppermute | solution.py:360
  70.5 1.5 collective-permute-done.11.got_odd
  76.6 2.0 %weight_far.1 = (bf16[2,4,192,768]{3,2,1,0:T(8,128)(2,1)S(1)}, bf16[192,768]{1,0:T(8,128)(2,1)S(1)}, bf16[192,768]{1,0:T(8,128)(2,1)S(1)}) custom-call(s32[36]{0:T(128)S(1)} %get-tuple-element.105.pos, bf16[512,768]{1,0:T(8,128)(2,1)S(1)} %collective-permute-done.9.l0.c0, bf16[512,768]{1,0:T(8,128)(2,1)S(1)} %collective-permute-done.12.l1.c1, ...), custom_call_target="tpu_custom_call" | custom-call | tf_op jit(solution)/shard_map/weight_far/pallas_call | solution.py:132
  78.9 2.3 %collective-permute-start.15 = (bf16[192,768]{1,0:T(8,128)(2,1)S(1)}, bf16[192,768]{1,0:T(8,128)(2,1)S(1)}, u32[]{:S(2)}, u32[]{:S(2)}) collective-permute-start(bf16[192,768]{1,0:T(8,128)(2,1)S(1)} %get-tuple-element.72), channel_id=1, source_target_pairs={{0,48},{4,52},{8,56},{12,60},{16,32},{20,36},{24,40},{28,44},{32,1... | collective-permute-start | bytes 884744 | tf_op jit(solution)/shard_map/ppermute | solution.py:360
  81.3 10.1 %attend_backward.1 = (f32[512,768]{1,0:T(8,128)}, f32[2,128,768]{2,1,0:T(8,128)S(1)}, f32[2,128,768]{2,1,0:T(8,128)S(1)}, f32[2,128,768]{2,1,0:T(8,128)S(1)}, bf...) custom-call(bf16[512,768]{1,0:T(8,128)(2,1)S(1)} %copy-done, bf16[128,768]{1,0:T(8,128)(2,1)S(1)} %copy-done.1, ...), custom_call_target="tpu_custom_call" | custom-call | flops 3019898880 | tf_op jit(solution)/shard_map/attend_backward/pallas_call | solution.py:280
  91.4 2.1 %collective-permute-start.20 = (bf16[2,128,768]{2,1,0:T(8,128)(2,1)S(1)}, bf16[2,128,768]{2,1,0:T(8,128)(2,1)S(1)}, u32[]{:S(2)}, u32[]{:S(2)}) collective-permute-start(bf16[2,128,768]{2,1,0:T(8,128)(2,1)S(1)} %get-tuple-element.76), channel_id=1, source_target_pairs={{0,252},{4,8},{8,4},{12,16},{16,12},{20,24},{24,20},{28,32},{32,28... | collective-permute-start | bytes 1179656 | tf_op jit(solution)/shard_map/ppermute | solution.py:411
  93.5 1.3 collective-permute-done.14.got_even
  94.8 2.9 %collective-permute-done.15.got_odd = bf16[192,768]{1,0:T(8,128)(2,1)S(1)} collective-permute-done((bf16[192,768]{1,0:T(8,128)(2,1)S(1)}, bf16[192,768]{1,0:T(8,128)(2,1)S(1)}, u32[]{:S(2)}, u32[]{:S(2)}) %collective-permute-start.15) | collective-permute-done | bytes 294944 | tf_op jit(solution)/shard_map/ppermute | solution.py:360
  98.9 1.5 fusion
  100.4 4.5 %collective-permute-done.18 = bf16[512,768]{1,0:T(8,128)(2,1)S(1)} collective-permute-done((bf16[512,768]{1,0:T(8,128)(2,1)S(1)}, bf16[512,768]{1,0:T(8,128)(2,1)S(1)}, u32[]{:S(2)}, u32[]{:S(2)}) %collective-permute-start.18) | collective-permute-done | bytes 786464 | tf_op jit(solution)/shard_map/ppermute | solution.py:403
  104.9 1.1 add_convert_fusion
  106.0 9.9 %collective-permute-done.20 = bf16[2,128,768]{2,1,0:T(8,128)(2,1)S(1)} collective-permute-done((bf16[2,128,768]{2,1,0:T(8,128)(2,1)S(1)}, bf16[2,128,768]{2,1,0:T(8,128)(2,1)S(1)}, u32[]{:S(2)}, u32[]{:S(2)}) %collective-permute-start.20) | collective-permute-done | bytes 393248 | tf_op jit(solution)/shard_map/ppermute | solution.py:411
  116.2 1.7 %collective-permute-done.24.more_odd = bf16[2,192,768]{2,1,0:T(8,128)(2,1)S(1)} collective-permute-done((bf16[2,192,768]{2,1,0:T(8,128)(2,1)S(1)}, bf16[2,192,768]{2,1,0:T(8,128)(2,1)S(1)}, u32[]{:S(2)}, u32[]{:S(2)}) %collective-permute-start.24) | collective-permute-done | bytes 589856 | tf_op jit(solution)/shard_map/ppermute | solution.py:360
  117.9 1.4 rows.1
  119.3 1.8 %collective-permute-start.26 = (bf16[96,768]{1,0:T(8,128)(2,1)S(1)}, bf16[96,768]{1,0:T(8,128)(2,1)S(1)}, u32[]{:S(2)}, u32[]{:S(2)}) collective-permute-start(bf16[96,768]{1,0:T(8,128)(2,1)S(1)} %get-tuple-element.92), channel_id=1, source_target_pairs={{0,192},{4,196},{8,200},{12,204},{16,208},{20,212},{24,216},{28,22... | collective-permute-start | bytes 442376 | tf_op jit(solution)/shard_map/ppermute | solution.py:360
  121.1 4.6 %collective-permute-start.22 = (bf16[2,128,768]{2,1,0:T(8,128)(2,1)S(1)}, bf16[2,128,768]{2,1,0:T(8,128)(2,1)S(1)}, u32[]{:S(2)}, u32[]{:S(2)}) collective-permute-start(bf16[2,128,768]{2,1,0:T(8,128)(2,1)S(1)} %add_convert_fusion.2), channel_id=1, source_target_pairs={{0,252},{4,8},{8,4},{12,16},{16,12},{20,24},{24,20},{28,32},{32,28... | collective-permute-start | bytes 1179656 | tf_op jit(solution)/shard_map/ppermute | solution.py:421
  127.2 1.7 %collective-permute-start.28 = (bf16[192,768]{1,0:T(8,128)(2,1)S(1)}, bf16[192,768]{1,0:T(8,128)(2,1)S(1)}, u32[]{:S(2)}, u32[]{:S(2)}) collective-permute-start(bf16[192,768]{1,0:T(8,128)(2,1)S(1)} %get-tuple-element.94), channel_id=1, source_target_pairs={{0,192},{4,196},{8,200},{12,204},{16,208},{20,212},{24,216},{28,22... | collective-permute-start | bytes 884744 | tf_op jit(solution)/shard_map/ppermute | solution.py:360
  128.9 11.9 %collective-permute-done.27.g1 = bf16[192,768]{1,0:T(8,128)(2,1)S(1)} collective-permute-done((bf16[192,768]{1,0:T(8,128)(2,1)S(1)}, bf16[192,768]{1,0:T(8,128)(2,1)S(1)}, u32[]{:S(2)}, u32[]{:S(2)}) %collective-permute-start.27) | collective-permute-done | bytes 294944 | tf_op jit(solution)/shard_map/ppermute | solution.py:360
  140.8 3.5 %collective-permute-done.28.g2 = bf16[192,768]{1,0:T(8,128)(2,1)S(1)} collective-permute-done((bf16[192,768]{1,0:T(8,128)(2,1)S(1)}, bf16[192,768]{1,0:T(8,128)(2,1)S(1)}, u32[]{:S(2)}, u32[]{:S(2)}) %collective-permute-start.28) | collective-permute-done | bytes 294944 | tf_op jit(solution)/shard_map/ppermute | solution.py:360
  145.2 6.4 %collective-permute-start.31 = (bf16[48,768]{1,0:T(8,128)(2,1)S(1)}, bf16[48,768]{1,0:T(8,128)(2,1)S(1)}, u32[]{:S(2)}, u32[]{:S(2)}) collective-permute-start(bf16[48,768]{1,0:T(8,128)(2,1)S(1)} %get-tuple-element.98), channel_id=1, source_target_pairs={{0,12},{4,8},{8,4},{12,0},{16,28},{20,24},{24,20},{28,16},{32,44},... | collective-permute-start | bytes 221192 | tf_op jit(solution)/shard_map/ppermute | solution.py:364
  (67 shorter events, 20.0 us)
Async XLA Ops:
  1.3 22.1 %collective-permute-start.1 = (bf16[128,768]{1,0:T(8,128)(2,1)}, bf16[128,768]{1,0:T(8,128)(2,1)S(1)}, u32[]{:S(2)}, u32[]{:S(2)}) collective-permute-start(bf16[128,768]{1,0:T(8,128)(2,1)} %k0.1), channel_id=1, source_target_pairs={{0,252},{4,8},{8,4},{12,16},{16,12},{20,24},{24,20},{28,32},{32,28... | collective-permute-start | bytes 589832 | tf_op jit(solution)/shard_map/ppermute | solution.py:384
  11.4 13.8 %collective-permute-start = (bf16[128,768]{1,0:T(8,128)(2,1)}, bf16[128,768]{1,0:T(8,128)(2,1)S(1)}, u32[]{:S(2)}, u32[]{:S(2)}) collective-permute-start(bf16[128,768]{1,0:T(8,128)(2,1)} %k0.1), channel_id=1, source_target_pairs={{0,4},{4,0},{8,12},{12,8},{16,20},{20,16},{24,28},{28,24},{32,36},... | collective-permute-start | bytes 589832 | tf_op jit(solution)/shard_map/ppermute | solution.py:383
  11.4 21.8 %collective-permute-start.5 = (bf16[128,768]{1,0:T(8,128)(2,1)}, bf16[128,768]{1,0:T(8,128)(2,1)S(1)}, u32[]{:S(2)}, u32[]{:S(2)}) collective-permute-start(bf16[128,768]{1,0:T(8,128)(2,1)} %v0.3), channel_id=1, source_target_pairs={{0,252},{4,8},{8,4},{12,16},{16,12},{20,24},{24,20},{28,32},{32,28... | collective-permute-start | bytes 589832 | tf_op jit(solution)/shard_map/ppermute | solution.py:384
  13.4 19.8 %collective-permute-start.4 = (bf16[128,768]{1,0:T(8,128)(2,1)}, bf16[128,768]{1,0:T(8,128)(2,1)S(1)}, u32[]{:S(2)}, u32[]{:S(2)}) collective-permute-start(bf16[128,768]{1,0:T(8,128)(2,1)} %v0.3), channel_id=1, source_target_pairs={{0,4},{4,0},{8,12},{12,8},{16,20},{20,16},{24,28},{28,24},{32,36},... | collective-permute-start | bytes 589832 | tf_op jit(solution)/shard_map/ppermute | solution.py:383
  14.3 18.0 %collective-permute-start.6 = (bf16[512,768]{1,0:T(8,128)(2,1)}, bf16[512,768]{1,0:T(8,128)(2,1)S(1)}, u32[]{:S(2)}, u32[]{:S(2)}) collective-permute-start(bf16[512,768]{1,0:T(8,128)(2,1)} %l0.1), channel_id=1, source_target_pairs={{0,1},{1,0},{2,3},{3,2},{4,5},{5,4},{6,7},{7,6},{8,9},{9,8},{10,11... | collective-permute-start | bytes 2359304 | tf_op jit(solution)/shard_map/ppermute | solution.py:379
  25.2 16.4 %collective-permute-start.3 = (bf16[128,768]{1,0:T(8,128)(2,1)S(1)}, bf16[128,768]{1,0:T(8,128)(2,1)S(1)}, u32[]{:S(2)}, u32[]{:S(2)}) collective-permute-start(bf16[128,768]{1,0:T(8,128)(2,1)S(1)} %collective-permute-done.k1), channel_id=1, source_target_pairs={{0,252},{4,8},{8,4},{12,16},{16,12},{20,24},{24,20},{28,32},{32,28... | collective-permute-start | bytes 589832 | tf_op jit(solution)/shard_map/ppermute | solution.py:386
  32.3 11.8 %collective-permute-start.2 = (bf16[128,768]{1,0:T(8,128)(2,1)S(1)}, bf16[128,768]{1,0:T(8,128)(2,1)S(1)}, u32[]{:S(2)}, u32[]{:S(2)}) collective-permute-start(bf16[128,768]{1,0:T(8,128)(2,1)S(1)} %collective-permute-done.1.k2), channel_id=1, source_target_pairs={{0,4},{4,0},{8,12},{12,8},{16,20},{20,16},{24,28},{28,24},{32,36},... | collective-permute-start | bytes 589832 | tf_op jit(solution)/shard_map/ppermute | solution.py:386
  33.2 12.6 %collective-permute-start.8 = (bf16[128,768]{1,0:T(8,128)(2,1)S(1)}, bf16[128,768]{1,0:T(8,128)(2,1)S(1)}, u32[]{:S(2)}, u32[]{:S(2)}) collective-permute-start(bf16[128,768]{1,0:T(8,128)(2,1)S(1)} %collective-permute-done.4.v1), channel_id=1, source_target_pairs={{0,252},{4,8},{8,4},{12,16},{16,12},{20,24},{24,20},{28,32},{32,28... | collective-permute-start | bytes 589832 | tf_op jit(solution)/shard_map/ppermute | solution.py:386
  35.4 11.4 %collective-permute-start.7 = (bf16[128,768]{1,0:T(8,128)(2,1)S(1)}, bf16[128,768]{1,0:T(8,128)(2,1)S(1)}, u32[]{:S(2)}, u32[]{:S(2)}) collective-permute-start(bf16[128,768]{1,0:T(8,128)(2,1)S(1)} %collective-permute-done.5.v2), channel_id=1, source_target_pairs={{0,4},{4,0},{8,12},{12,8},{16,20},{20,16},{24,28},{28,24},{32,36},... | collective-permute-start | bytes 589832 | tf_op jit(solution)/shard_map/ppermute | solution.py:386
  46.9 25.1 %collective-permute-start.9 = (bf16[512,768]{1,0:T(8,128)(2,1)S(1)}, bf16[512,768]{1,0:T(8,128)(2,1)S(1)}, u32[]{:S(2)}, u32[]{:S(2)}) collective-permute-start(bf16[512,768]{1,0:T(8,128)(2,1)S(1)} %copy-done.3), channel_id=1, source_target_pairs={{0,2},{1,3},{2,0},{3,1},{4,6},{5,7},{6,4},{7,5},{8,10},{9,11},{10,... | collective-permute-start | bytes 2359304 | tf_op jit(solution)/shard_map/ppermute | solution.py:391
  61.8 8.7 %collective-permute-start.10 = (bf16[192,768]{1,0:T(8,128)(2,1)S(1)}, bf16[192,768]{1,0:T(8,128)(2,1)S(1)}, u32[]{:S(2)}, u32[]{:S(2)}) collective-permute-start(bf16[192,768]{1,0:T(8,128)(2,1)S(1)} %get-tuple-element.60), channel_id=1, source_target_pairs={{0,16},{4,20},{8,24},{12,28},{16,0},{20,4},{24,8},{28,12},{32,48},... | collective-permute-start | bytes 884744 | tf_op jit(solution)/shard_map/ppermute | solution.py:360
  61.9 10.1 %collective-permute-start.11 = (bf16[192,768]{1,0:T(8,128)(2,1)S(1)}, bf16[192,768]{1,0:T(8,128)(2,1)S(1)}, u32[]{:S(2)}, u32[]{:S(2)}) collective-permute-start(bf16[192,768]{1,0:T(8,128)(2,1)S(1)} %get-tuple-element.61), channel_id=1, source_target_pairs={{0,48},{4,52},{8,56},{12,60},{16,32},{20,36},{24,40},{28,44},{32,1... | collective-permute-start | bytes 884744 | tf_op jit(solution)/shard_map/ppermute | solution.py:360
  72.0 3.4 %collective-permute-start.13 = (bf16[512,1536]{1,0:T(8,128)(2,1)S(1)}, bf16[512,1536]{1,0:T(8,128)(2,1)S(1)}, u32[]{:S(2)}, u32[]{:S(2)}) collective-permute-start(bf16[512,1536]{1,0:T(8,128)(2,1)S(1)} %get-tuple-element.68), channel_id=1, source_target_pairs={{0,1},{1,0},{2,3},{3,2},{4,5},{5,4},{6,7},{7,6},{8,9},{9,8},{10,11... | collective-permute-start | bytes 4718600 | tf_op jit(solution)/shard_map/ppermute | solution.py:399
  72.0 4.6 %collective-permute-start.12 = (bf16[512,768]{1,0:T(8,128)(2,1)S(1)}, bf16[512,768]{1,0:T(8,128)(2,1)S(1)}, u32[]{:S(2)}, u32[]{:S(2)}) collective-permute-start(bf16[512,768]{1,0:T(8,128)(2,1)S(1)} %collective-permute-done.9.l0.c0), channel_id=1, source_target_pairs={{0,1},{1,0},{2,3},{3,2},{4,5},{5,4},{6,7},{7,6},{8,9},{9,8},{10,11... | collective-permute-start | bytes 2359304 | tf_op jit(solution)/shard_map/ppermute | solution.py:398
  73.2 18.2 %collective-permute-start.16 = (bf16[2,192,768]{2,1,0:T(8,128)(2,1)S(1)}, bf16[2,192,768]{2,1,0:T(8,128)(2,1)S(1)}, u32[]{:S(2)}, u32[]{:S(2)}) collective-permute-start(bf16[2,192,768]{2,1,0:T(8,128)(2,1)S(1)} %get-tuple-element.64), channel_id=1, source_target_pairs={{0,16},{4,20},{8,24},{12,28},{16,0},{20,4},{24,8},{28,12},{32,48},... | collective-permute-start | bytes 1769480 | tf_op jit(solution)/shard_map/ppermute | solution.py:360
  73.5 17.8 %collective-permute-start.17 = (bf16[2,192,768]{2,1,0:T(8,128)(2,1)S(1)}, bf16[2,192,768]{2,1,0:T(8,128)(2,1)S(1)}, u32[]{:S(2)}, u32[]{:S(2)}) collective-permute-start(bf16[2,192,768]{2,1,0:T(8,128)(2,1)S(1)} %get-tuple-element.65), channel_id=1, source_target_pairs={{0,48},{4,52},{8,56},{12,60},{16,32},{20,36},{24,40},{28,44},{32,1... | collective-permute-start | bytes 1769480 | tf_op jit(solution)/shard_map/ppermute | solution.py:360
  76.2 28.7 %collective-permute-start.18 = (bf16[512,768]{1,0:T(8,128)(2,1)S(1)}, bf16[512,768]{1,0:T(8,128)(2,1)S(1)}, u32[]{:S(2)}, u32[]{:S(2)}) collective-permute-start(bf16[512,768]{1,0:T(8,128)(2,1)S(1)} %add_convert_fusion.1), channel_id=1, source_target_pairs={{0,2},{1,3},{2,0},{3,1},{4,6},{5,7},{6,4},{7,5},{8,10},{9,11},{10,... | collective-permute-start | bytes 2359304 | tf_op jit(solution)/shard_map/ppermute | solution.py:403
  78.6 16.3 %collective-permute-start.14 = (bf16[192,768]{1,0:T(8,128)(2,1)S(1)}, bf16[192,768]{1,0:T(8,128)(2,1)S(1)}, u32[]{:S(2)}, u32[]{:S(2)}) collective-permute-start(bf16[192,768]{1,0:T(8,128)(2,1)S(1)} %get-tuple-element.71), channel_id=1, source_target_pairs={{0,16},{4,20},{8,24},{12,28},{16,0},{20,4},{24,8},{28,12},{32,48},... | collective-permute-start | bytes 884744 | tf_op jit(solution)/shard_map/ppermute | solution.py:360
  78.9 18.8 %collective-permute-start.15 = (bf16[192,768]{1,0:T(8,128)(2,1)S(1)}, bf16[192,768]{1,0:T(8,128)(2,1)S(1)}, u32[]{:S(2)}, u32[]{:S(2)}) collective-permute-start(bf16[192,768]{1,0:T(8,128)(2,1)S(1)} %get-tuple-element.72), channel_id=1, source_target_pairs={{0,48},{4,52},{8,56},{12,60},{16,32},{20,36},{24,40},{28,44},{32,1... | collective-permute-start | bytes 884744 | tf_op jit(solution)/shard_map/ppermute | solution.py:360
  91.4 14.7 %collective-permute-start.19 = (bf16[2,128,768]{2,1,0:T(8,128)(2,1)S(1)}, bf16[2,128,768]{2,1,0:T(8,128)(2,1)S(1)}, u32[]{:S(2)}, u32[]{:S(2)}) collective-permute-start(bf16[2,128,768]{2,1,0:T(8,128)(2,1)S(1)} %get-tuple-element.75), channel_id=1, source_target_pairs={{0,4},{4,0},{8,12},{12,8},{16,20},{20,16},{24,28},{28,24},{32,36},... | collective-permute-start | bytes 1179656 | tf_op jit(solution)/shard_map/ppermute | solution.py:410
  91.4 24.6 %collective-permute-start.20 = (bf16[2,128,768]{2,1,0:T(8,128)(2,1)S(1)}, bf16[2,128,768]{2,1,0:T(8,128)(2,1)S(1)}, u32[]{:S(2)}, u32[]{:S(2)}) collective-permute-start(bf16[2,128,768]{2,1,0:T(8,128)(2,1)S(1)} %get-tuple-element.76), channel_id=1, source_target_pairs={{0,252},{4,8},{8,4},{12,16},{16,12},{20,24},{24,20},{28,32},{32,28... | collective-permute-start | bytes 1179656 | tf_op jit(solution)/shard_map/ppermute | solution.py:411
  98.5 17.7 %collective-permute-start.23 = (bf16[2,192,768]{2,1,0:T(8,128)(2,1)S(1)}, bf16[2,192,768]{2,1,0:T(8,128)(2,1)S(1)}, u32[]{:S(2)}, u32[]{:S(2)}) collective-permute-start(bf16[2,192,768]{2,1,0:T(8,128)(2,1)S(1)} %get-tuple-element.79), channel_id=1, source_target_pairs={{0,16},{4,20},{8,24},{12,28},{16,0},{20,4},{24,8},{28,12},{32,48},... | collective-permute-start | bytes 1769480 | tf_op jit(solution)/shard_map/ppermute | solution.py:360
  98.6 19.3 %collective-permute-start.24 = (bf16[2,192,768]{2,1,0:T(8,128)(2,1)S(1)}, bf16[2,192,768]{2,1,0:T(8,128)(2,1)S(1)}, u32[]{:S(2)}, u32[]{:S(2)}) collective-permute-start(bf16[2,192,768]{2,1,0:T(8,128)(2,1)S(1)} %get-tuple-element.80), channel_id=1, source_target_pairs={{0,48},{4,52},{8,56},{12,60},{16,32},{20,36},{24,40},{28,44},{32,1... | collective-permute-start | bytes 1769480 | tf_op jit(solution)/shard_map/ppermute | solution.py:360
  119.2 6.5 %collective-permute-start.25 = (bf16[96,768]{1,0:T(8,128)(2,1)S(1)}, bf16[96,768]{1,0:T(8,128)(2,1)S(1)}, u32[]{:S(2)}, u32[]{:S(2)}) collective-permute-start(bf16[96,768]{1,0:T(8,128)(2,1)S(1)} %get-tuple-element.91), channel_id=1, source_target_pairs={{0,64},{4,68},{8,72},{12,76},{16,80},{20,84},{24,88},{28,92},{32,9... | collective-permute-start | bytes 442376 | tf_op jit(solution)/shard_map/ppermute | solution.py:360
  119.3 6.4 %collective-permute-start.26 = (bf16[96,768]{1,0:T(8,128)(2,1)S(1)}, bf16[96,768]{1,0:T(8,128)(2,1)S(1)}, u32[]{:S(2)}, u32[]{:S(2)}) collective-permute-start(bf16[96,768]{1,0:T(8,128)(2,1)S(1)} %get-tuple-element.92), channel_id=1, source_target_pairs={{0,192},{4,196},{8,200},{12,204},{16,208},{20,212},{24,216},{28,22... | collective-permute-start | bytes 442376 | tf_op jit(solution)/shard_map/ppermute | solution.py:360
  121.1 30.5 %collective-permute-start.21 = (bf16[2,128,768]{2,1,0:T(8,128)(2,1)S(1)}, bf16[2,128,768]{2,1,0:T(8,128)(2,1)S(1)}, u32[]{:S(2)}, u32[]{:S(2)}) collective-permute-start(bf16[2,128,768]{2,1,0:T(8,128)(2,1)S(1)} %add_convert_fusion.3), channel_id=1, source_target_pairs={{0,4},{4,0},{8,12},{12,8},{16,20},{20,16},{24,28},{28,24},{32,36},... | collective-permute-start | bytes 1179656 | tf_op jit(solution)/shard_map/ppermute | solution.py:422
  121.1 30.5 %collective-permute-start.22 = (bf16[2,128,768]{2,1,0:T(8,128)(2,1)S(1)}, bf16[2,128,768]{2,1,0:T(8,128)(2,1)S(1)}, u32[]{:S(2)}, u32[]{:S(2)}) collective-permute-start(bf16[2,128,768]{2,1,0:T(8,128)(2,1)S(1)} %add_convert_fusion.2), channel_id=1, source_target_pairs={{0,252},{4,8},{8,4},{12,16},{16,12},{20,24},{24,20},{28,32},{32,28... | collective-permute-start | bytes 1179656 | tf_op jit(solution)/shard_map/ppermute | solution.py:421
  126.4 14.4 %collective-permute-start.27 = (bf16[192,768]{1,0:T(8,128)(2,1)S(1)}, bf16[192,768]{1,0:T(8,128)(2,1)S(1)}, u32[]{:S(2)}, u32[]{:S(2)}) collective-permute-start(bf16[192,768]{1,0:T(8,128)(2,1)S(1)} %get-tuple-element.93), channel_id=1, source_target_pairs={{0,64},{4,68},{8,72},{12,76},{16,80},{20,84},{24,88},{28,92},{32,9... | collective-permute-start | bytes 884744 | tf_op jit(solution)/shard_map/ppermute | solution.py:360
  127.2 17.1 %collective-permute-start.28 = (bf16[192,768]{1,0:T(8,128)(2,1)S(1)}, bf16[192,768]{1,0:T(8,128)(2,1)S(1)}, u32[]{:S(2)}, u32[]{:S(2)}) collective-permute-start(bf16[192,768]{1,0:T(8,128)(2,1)S(1)} %get-tuple-element.94), channel_id=1, source_target_pairs={{0,192},{4,196},{8,200},{12,204},{16,208},{20,212},{24,216},{28,22... | collective-permute-start | bytes 884744 | tf_op jit(solution)/shard_map/ppermute | solution.py:360
  145.0 7.6 %collective-permute-start.29 = (bf16[48,768]{1,0:T(8,128)(2,1)S(1)}, bf16[48,768]{1,0:T(8,128)(2,1)S(1)}, u32[]{:S(2)}, u32[]{:S(2)}) collective-permute-start(bf16[48,768]{1,0:T(8,128)(2,1)S(1)} %get-tuple-element.96), channel_id=1, source_target_pairs={{0,4},{4,0},{8,12},{12,8},{16,20},{20,16},{24,28},{28,24},{32,36},... | collective-permute-start | bytes 221192 | tf_op jit(solution)/shard_map/ppermute | solution.py:364
  145.1 8.3 %collective-permute-start.30 = (bf16[48,768]{1,0:T(8,128)(2,1)S(1)}, bf16[48,768]{1,0:T(8,128)(2,1)S(1)}, u32[]{:S(2)}, u32[]{:S(2)}) collective-permute-start(bf16[48,768]{1,0:T(8,128)(2,1)S(1)} %get-tuple-element.97), channel_id=1, source_target_pairs={{0,8},{4,12},{8,0},{12,4},{16,24},{20,28},{24,16},{28,20},{32,40},... | collective-permute-start | bytes 221192 | tf_op jit(solution)/shard_map/ppermute | solution.py:364
  145.2 9.1 %collective-permute-start.31 = (bf16[48,768]{1,0:T(8,128)(2,1)S(1)}, bf16[48,768]{1,0:T(8,128)(2,1)S(1)}, u32[]{:S(2)}, u32[]{:S(2)}) collective-permute-start(bf16[48,768]{1,0:T(8,128)(2,1)S(1)} %get-tuple-element.98), channel_id=1, source_target_pairs={{0,12},{4,8},{8,4},{12,0},{16,28},{20,24},{24,20},{28,16},{32,44},... | collective-permute-start | bytes 221192 | tf_op jit(solution)/shard_map/ppermute | solution.py:364
  (5 other events, 99.3 us)

commit v6 on v4

--- a/solution.py
+++ b/solution.py
@@ -13,7 +13,7 @@
 VBLK = 128
 ABLK = 32
 RING = 4
-PAIRED = 2
+PAIRED = 3
 SCALE = 1.0 / math.sqrt(HEAD)
 LOG2E = math.log2(math.e)
 NT = (((1,), (1,)), ((), ()))

time: 155 us -> 155 us (level)
    ppermute x6, waiting for transfers between devices: 27.5 us -> 22.4 us  [exchange(): lax.ppermute(send[0], 'vseq', even)]
    ppermute x6, waiting for transfers between devices: 18.4 us -> 22.8 us  [exchange(): lax.ppermute(send[1], 'vseq', odd)]
where the time goes in v6:
time: 155 us; the launch traced here: 154 us
  waiting for transfers between devices  69.5 us (45%)
  starting transfers between devices  46.6 us (30%)
  Pallas kernels  22.2 us (14%)
  local copies, waits for them, and re-layouts  6.81 us (4%)
  matrix products  4.49 us (3%)
  other arithmetic  3.91 us (3%)
    ppermute x6, waiting for transfers between devices, exchange(): lax.ppermute(send[1], 'vseq', odd)  22.8 us
    ppermute x6, waiting for transfers between devices, exchange(): lax.ppermute(send[0], 'vseq', even)  22.4 us
    ppermute x2, starting transfers between devices, halo(): by_b = lax.ppermute(own, 'vseq', pb)  12 us
    ppermute x2, starting transfers between devices, halo(): lax.ppermute(by_a, 'vseq', pb)  9.46 us
    ppermute x1, waiting for transfers between devices, local(): back_b = lax.ppermute(g_bb, 'vseq', pb)  9.2 us
    pallas_call x1, Pallas kernels, forward_call(): call(attend_forward, (heads // PAIRED,), (pos,), [by_head] + [kv_head] *...  8.79 us
    pallas_call x1, Pallas kernels, backward_call(): call(attend_backward, (heads // PAIRED,), (), [by_head] + [kv_head] * 10...  7.26 us
    ppermute x2, waiting for transfers between devices, halo(): lax.ppermute(by_a, 'vseq', pb)  6.91 us
  transfers between devices with their start and end apart: 32, of which 22 were waited for; matrix products, arithmetic and copies ran while one was open for 9% of the time, Pallas kernels for 14%

profile of v6, /device:TPU:32, one launch (start us, length us, event | category | flops | bytes accessed | tf_op | source)
XLA Modules:
  0.0 154.4 jit_solution(1028698628704189822)
XLA Ops:
  1.3 10.0 %collective-permute-start.1 = (bf16[128,768]{1,0:T(8,128)(2,1)}, bf16[128,768]{1,0:T(8,128)(2,1)S(1)}, u32[]{:S(2)}, u32[]{:S(2)}) collective-permute-start(bf16[128,768]{1,0:T(8,128)(2,1)} %k0.1), channel_id=1, source_target_pairs={{0,252},{4,8},{8,4},{12,16},{16,12},{20,24},{24,20},{28,32},{32,28... | collective-permute-start | bytes 589832 | tf_op jit(solution)/shard_map/ppermute | solution.py:392
  11.4 2.0 %collective-permute-start.5 = (bf16[128,768]{1,0:T(8,128)(2,1)}, bf16[128,768]{1,0:T(8,128)(2,1)S(1)}, u32[]{:S(2)}, u32[]{:S(2)}) collective-permute-start(bf16[128,768]{1,0:T(8,128)(2,1)} %v0.3), channel_id=1, source_target_pairs={{0,252},{4,8},{8,4},{12,16},{16,12},{20,24},{24,20},{28,32},{32,28... | collective-permute-start | bytes 589832 | tf_op jit(solution)/shard_map/ppermute | solution.py:392
  16.4 4.7 %dynamic-slice_bitcast_fusion = (bf16[768,768]{1,0:T(8,128)(2,1)S(1)}, bf16[768,768]{1,0:T(8,128)(2,1)S(1)}, bf16[768,768]{1,0:T(8,128)(2,1)S(1)}) fusion(bf16[4,768,768]{2,1,0:T(8,128)(2,1)} %bitcast.36, s32[]{:T(128)} %bitcast.12, s32[]{:T(128)} %bitcast.10, s32[]{:T(128)} %bitcast.5), kind=kLoop, calls=%fused_computation.8 | loop fusion | bytes 7077900 | tf_op jit(solution)/shard_map/jit(dynamic_index_in_dim)/squeeze | solution.py:338
  21.1 1.4 fusion.2
  23.5 1.7 %collective-permute-done.k1 = bf16[128,768]{1,0:T(8,128)(2,1)S(1)} collective-permute-done((bf16[128,768]{1,0:T(8,128)(2,1)}, bf16[128,768]{1,0:T(8,128)(2,1)S(1)}, u32[]{:S(2)}, u32[]{:S(2)}) %collective-permute-start) | collective-permute-done | bytes 196640 | tf_op jit(solution)/shard_map/ppermute | solution.py:391
  25.2 7.2 %collective-permute-start.3 = (bf16[128,768]{1,0:T(8,128)(2,1)S(1)}, bf16[128,768]{1,0:T(8,128)(2,1)S(1)}, u32[]{:S(2)}, u32[]{:S(2)}) collective-permute-start(bf16[128,768]{1,0:T(8,128)(2,1)S(1)} %collective-permute-done.k1), channel_id=1, source_target_pairs={{0,252},{4,8},{8,4},{12,16},{16,12},{20,24},{24,20},{28,32},{32,28... | collective-permute-start | bytes 589832 | tf_op jit(solution)/shard_map/ppermute | solution.py:394
  33.2 2.3 %collective-permute-start.8 = (bf16[128,768]{1,0:T(8,128)(2,1)S(1)}, bf16[128,768]{1,0:T(8,128)(2,1)S(1)}, u32[]{:S(2)}, u32[]{:S(2)}) collective-permute-start(bf16[128,768]{1,0:T(8,128)(2,1)S(1)} %collective-permute-done.4.v1), channel_id=1, source_target_pairs={{0,252},{4,8},{8,4},{12,16},{16,12},{20,24},{24,20},{28,32},{32,28... | collective-permute-start | bytes 589832 | tf_op jit(solution)/shard_map/ppermute | solution.py:394
  36.3 5.3 %collective-permute-done.3.k4 = bf16[128,768]{1,0:T(8,128)(2,1)S(1)} collective-permute-done((bf16[128,768]{1,0:T(8,128)(2,1)S(1)}, bf16[128,768]{1,0:T(8,128)(2,1)S(1)}, u32[]{:S(2)}, u32[]{:S(2)}) %collective-permute-start.3) | collective-permute-done | bytes 196640 | tf_op jit(solution)/shard_map/ppermute | solution.py:394
  41.5 2.6 %collective-permute-done.2.k3 = bf16[128,768]{1,0:T(8,128)(2,1)S(1)} collective-permute-done((bf16[128,768]{1,0:T(8,128)(2,1)S(1)}, bf16[128,768]{1,0:T(8,128)(2,1)S(1)}, u32[]{:S(2)}, u32[]{:S(2)}) %collective-permute-start.2) | collective-permute-done | bytes 196640 | tf_op jit(solution)/shard_map/ppermute | solution.py:394
  44.1 1.6 %collective-permute-done.8.v4 = bf16[128,768]{1,0:T(8,128)(2,1)S(1)} collective-permute-done((bf16[128,768]{1,0:T(8,128)(2,1)S(1)}, bf16[128,768]{1,0:T(8,128)(2,1)S(1)}, u32[]{:S(2)}, u32[]{:S(2)}) %collective-permute-start.8) | collective-permute-done | bytes 196640 | tf_op jit(solution)/shard_map/ppermute | solution.py:394
  46.9 5.9 %collective-permute-start.9 = (bf16[512,768]{1,0:T(8,128)(2,1)S(1)}, bf16[512,768]{1,0:T(8,128)(2,1)S(1)}, u32[]{:S(2)}, u32[]{:S(2)}) collective-permute-start(bf16[512,768]{1,0:T(8,128)(2,1)S(1)} %copy-done.3), channel_id=1, source_target_pairs={{0,2},{1,3},{2,0},{3,1},{4,6},{5,7},{6,4},{7,5},{8,10},{9,11},{10,... | collective-permute-start | bytes 2359304 | tf_op jit(solution)/shard_map/ppermute | solution.py:399
  52.8 8.8 %attend_forward.1 = (bf16[512,768]{1,0:T(8,128)(2,1)S(1)}, bf16[6,640,512]{2,1,0:T(8,128)(2,1)S(1)}, bf16[512,1536]{1,0:T(8,128)(2,1)S(1)}, bf16[2,4,192,768]{3,...) custom-call(s32[36]{0:T(128)S(1)} %get-tuple-element.105.pos, ...), custom_call_target="tpu_custom_call" | custom-call | flops 2013265920 | tf_op jit(solution)/shard_map/attend_forward/pallas_call | solution.py:260
  61.9 8.5 %collective-permute-done.10.got_even = bf16[192,768]{1,0:T(8,128)(2,1)S(1)} collective-permute-done((bf16[192,768]{1,0:T(8,128)(2,1)S(1)}, bf16[192,768]{1,0:T(8,128)(2,1)S(1)}, u32[]{:S(2)}, u32[]{:S(2)}) %collective-permute-start.10) | collective-permute-done | bytes 294944 | tf_op jit(solution)/shard_map/ppermute | solution.py:368
  70.4 1.3 collective-permute-done.11.got_odd
  76.5 2.0 %weight_far.1 = (bf16[2,4,192,768]{3,2,1,0:T(8,128)(2,1)S(1)}, bf16[192,768]{1,0:T(8,128)(2,1)S(1)}, bf16[192,768]{1,0:T(8,128)(2,1)S(1)}) custom-call(s32[36]{0:T(128)S(1)} %get-tuple-element.105.pos, bf16[512,768]{1,0:T(8,128)(2,1)S(1)} %collective-permute-done.9.l0.c0, bf16[512,768]{1,0:T(8,128)(2,1)S(1)} %collective-permute-done.12.l1.c1, ...), custom_call_target="tpu_custom_call" | custom-call | tf_op jit(solution)/shard_map/weight_far/pallas_call | solution.py:140
  78.9 2.3 %collective-permute-start.15 = (bf16[192,768]{1,0:T(8,128)(2,1)S(1)}, bf16[192,768]{1,0:T(8,128)(2,1)S(1)}, u32[]{:S(2)}, u32[]{:S(2)}) collective-permute-start(bf16[192,768]{1,0:T(8,128)(2,1)S(1)} %get-tuple-element.72), channel_id=1, source_target_pairs={{0,48},{4,52},{8,56},{12,60},{16,32},{20,36},{24,40},{28,44},{32,1... | collective-permute-start | bytes 884744 | tf_op jit(solution)/shard_map/ppermute | solution.py:368
  81.1 7.3 %attend_backward.1 = (f32[512,768]{1,0:T(8,128)}, f32[2,128,768]{2,1,0:T(8,128)S(1)}, f32[2,128,768]{2,1,0:T(8,128)S(1)}, f32[2,128,768]{2,1,0:T(8,128)S(1)}, bf...) custom-call(bf16[512,768]{1,0:T(8,128)(2,1)S(1)} %copy-done, bf16[128,768]{1,0:T(8,128)(2,1)S(1)} %copy-done.1, ...), custom_call_target="tpu_custom_call" | custom-call | flops 3019898880 | tf_op jit(solution)/shard_map/attend_backward/pallas_call | solution.py:288
  89.3 10.1 %collective-permute-done.17.near_odd = bf16[2,192,768]{2,1,0:T(8,128)(2,1)S(1)} collective-permute-done((bf16[2,192,768]{2,1,0:T(8,128)(2,1)S(1)}, bf16[2,192,768]{2,1,0:T(8,128)(2,1)S(1)}, u32[]{:S(2)}, u32[]{:S(2)}) %collective-permute-start.17) | collective-permute-done | bytes 589856 | tf_op jit(solution)/shard_map/ppermute | solution.py:368
  99.4 1.3 collective-permute-done.14.got_even
  100.6 3.8 %collective-permute-done.15.got_odd = bf16[192,768]{1,0:T(8,128)(2,1)S(1)} collective-permute-done((bf16[192,768]{1,0:T(8,128)(2,1)S(1)}, bf16[192,768]{1,0:T(8,128)(2,1)S(1)}, u32[]{:S(2)}, u32[]{:S(2)}) %collective-permute-start.15) | collective-permute-done | bytes 294944 | tf_op jit(solution)/shard_map/ppermute | solution.py:368
  105.2 1.3 collective-permute-start.24
  106.5 1.5 fusion
  108.0 1.1 add_convert_fusion
  109.1 9.2 %collective-permute-done.20 = bf16[2,128,768]{2,1,0:T(8,128)(2,1)S(1)} collective-permute-done((bf16[2,128,768]{2,1,0:T(8,128)(2,1)S(1)}, bf16[2,128,768]{2,1,0:T(8,128)(2,1)S(1)}, u32[]{:S(2)}, u32[]{:S(2)}) %collective-permute-start.20) | collective-permute-done | bytes 393248 | tf_op jit(solution)/shard_map/ppermute | solution.py:419
  119.3 1.5 collective-permute-done.24.more_odd
  120.8 1.4 rows.1
  123.0 1.8 %collective-permute-start.22 = (bf16[2,128,768]{2,1,0:T(8,128)(2,1)S(1)}, bf16[2,128,768]{2,1,0:T(8,128)(2,1)S(1)}, u32[]{:S(2)}, u32[]{:S(2)}) collective-permute-start(bf16[2,128,768]{2,1,0:T(8,128)(2,1)S(1)} %add_convert_fusion.2), channel_id=1, source_target_pairs={{0,252},{4,8},{8,4},{12,16},{16,12},{20,24},{24,20},{28,32},{32,28... | collective-permute-start | bytes 1179656 | tf_op jit(solution)/shard_map/ppermute | solution.py:429
  124.8 2.6 %collective-permute-done.25.got_even = bf16[96,768]{1,0:T(8,128)(2,1)S(1)} collective-permute-done((bf16[96,768]{1,0:T(8,128)(2,1)S(1)}, bf16[96,768]{1,0:T(8,128)(2,1)S(1)}, u32[]{:S(2)}, u32[]{:S(2)}) %collective-permute-start.25) | collective-permute-done | bytes 147488 | tf_op jit(solution)/shard_map/ppermute | solution.py:368
  127.4 1.3 collective-permute-done.26.got_odd
  130.8 8.4 %collective-permute-done.27.g1 = bf16[192,768]{1,0:T(8,128)(2,1)S(1)} collective-permute-done((bf16[192,768]{1,0:T(8,128)(2,1)S(1)}, bf16[192,768]{1,0:T(8,128)(2,1)S(1)}, u32[]{:S(2)}, u32[]{:S(2)}) %collective-permute-start.27) | collective-permute-done | bytes 294944 | tf_op jit(solution)/shard_map/ppermute | solution.py:368
  139.2 4.8 %collective-permute-done.28.g2 = bf16[192,768]{1,0:T(8,128)(2,1)S(1)} collective-permute-done((bf16[192,768]{1,0:T(8,128)(2,1)S(1)}, bf16[192,768]{1,0:T(8,128)(2,1)S(1)}, u32[]{:S(2)}, u32[]{:S(2)}) %collective-permute-start.28) | collective-permute-done | bytes 294944 | tf_op jit(solution)/shard_map/ppermute | solution.py:368
  145.0 6.4 %collective-permute-start.31 = (bf16[48,768]{1,0:T(8,128)(2,1)S(1)}, bf16[48,768]{1,0:T(8,128)(2,1)S(1)}, u32[]{:S(2)}, u32[]{:S(2)}) collective-permute-start(bf16[48,768]{1,0:T(8,128)(2,1)S(1)} %get-tuple-element.98), channel_id=1, source_target_pairs={{0,12},{4,8},{8,4},{12,0},{16,28},{20,24},{24,20},{28,16},{32,44},... | collective-permute-start | bytes 221192 | tf_op jit(solution)/shard_map/ppermute | solution.py:372
  (67 shorter events, 22.4 us)
Async XLA Ops:
  1.3 22.1 %collective-permute-start.1 = (bf16[128,768]{1,0:T(8,128)(2,1)}, bf16[128,768]{1,0:T(8,128)(2,1)S(1)}, u32[]{:S(2)}, u32[]{:S(2)}) collective-permute-start(bf16[128,768]{1,0:T(8,128)(2,1)} %k0.1), channel_id=1, source_target_pairs={{0,252},{4,8},{8,4},{12,16},{16,12},{20,24},{24,20},{28,32},{32,28... | collective-permute-start | bytes 589832 | tf_op jit(solution)/shard_map/ppermute | solution.py:392
  11.4 13.8 %collective-permute-start = (bf16[128,768]{1,0:T(8,128)(2,1)}, bf16[128,768]{1,0:T(8,128)(2,1)S(1)}, u32[]{:S(2)}, u32[]{:S(2)}) collective-permute-start(bf16[128,768]{1,0:T(8,128)(2,1)} %k0.1), channel_id=1, source_target_pairs={{0,4},{4,0},{8,12},{12,8},{16,20},{20,16},{24,28},{28,24},{32,36},... | collective-permute-start | bytes 589832 | tf_op jit(solution)/shard_map/ppermute | solution.py:391
  11.4 21.8 %collective-permute-start.5 = (bf16[128,768]{1,0:T(8,128)(2,1)}, bf16[128,768]{1,0:T(8,128)(2,1)S(1)}, u32[]{:S(2)}, u32[]{:S(2)}) collective-permute-start(bf16[128,768]{1,0:T(8,128)(2,1)} %v0.3), channel_id=1, source_target_pairs={{0,252},{4,8},{8,4},{12,16},{16,12},{20,24},{24,20},{28,32},{32,28... | collective-permute-start | bytes 589832 | tf_op jit(solution)/shard_map/ppermute | solution.py:392
  13.4 19.8 %collective-permute-start.4 = (bf16[128,768]{1,0:T(8,128)(2,1)}, bf16[128,768]{1,0:T(8,128)(2,1)S(1)}, u32[]{:S(2)}, u32[]{:S(2)}) collective-permute-start(bf16[128,768]{1,0:T(8,128)(2,1)} %v0.3), channel_id=1, source_target_pairs={{0,4},{4,0},{8,12},{12,8},{16,20},{20,16},{24,28},{28,24},{32,36},... | collective-permute-start | bytes 589832 | tf_op jit(solution)/shard_map/ppermute | solution.py:391
  14.3 18.0 %collective-permute-start.6 = (bf16[512,768]{1,0:T(8,128)(2,1)}, bf16[512,768]{1,0:T(8,128)(2,1)S(1)}, u32[]{:S(2)}, u32[]{:S(2)}) collective-permute-start(bf16[512,768]{1,0:T(8,128)(2,1)} %l0.1), channel_id=1, source_target_pairs={{0,1},{1,0},{2,3},{3,2},{4,5},{5,4},{6,7},{7,6},{8,9},{9,8},{10,11... | collective-permute-start | bytes 2359304 | tf_op jit(solution)/shard_map/ppermute | solution.py:387
  25.2 16.4 %collective-permute-start.3 = (bf16[128,768]{1,0:T(8,128)(2,1)S(1)}, bf16[128,768]{1,0:T(8,128)(2,1)S(1)}, u32[]{:S(2)}, u32[]{:S(2)}) collective-permute-start(bf16[128,768]{1,0:T(8,128)(2,1)S(1)} %collective-permute-done.k1), channel_id=1, source_target_pairs={{0,252},{4,8},{8,4},{12,16},{16,12},{20,24},{24,20},{28,32},{32,28... | collective-permute-start | bytes 589832 | tf_op jit(solution)/shard_map/ppermute | solution.py:394
  32.3 11.8 %collective-permute-start.2 = (bf16[128,768]{1,0:T(8,128)(2,1)S(1)}, bf16[128,768]{1,0:T(8,128)(2,1)S(1)}, u32[]{:S(2)}, u32[]{:S(2)}) collective-permute-start(bf16[128,768]{1,0:T(8,128)(2,1)S(1)} %collective-permute-done.1.k2), channel_id=1, source_target_pairs={{0,4},{4,0},{8,12},{12,8},{16,20},{20,16},{24,28},{28,24},{32,36},... | collective-permute-start | bytes 589832 | tf_op jit(solution)/shard_map/ppermute | solution.py:394
  33.2 12.6 %collective-permute-start.8 = (bf16[128,768]{1,0:T(8,128)(2,1)S(1)}, bf16[128,768]{1,0:T(8,128)(2,1)S(1)}, u32[]{:S(2)}, u32[]{:S(2)}) collective-permute-start(bf16[128,768]{1,0:T(8,128)(2,1)S(1)} %collective-permute-done.4.v1), channel_id=1, source_target_pairs={{0,252},{4,8},{8,4},{12,16},{16,12},{20,24},{24,20},{28,32},{32,28... | collective-permute-start | bytes 589832 | tf_op jit(solution)/shard_map/ppermute | solution.py:394
  35.4 11.4 %collective-permute-start.7 = (bf16[128,768]{1,0:T(8,128)(2,1)S(1)}, bf16[128,768]{1,0:T(8,128)(2,1)S(1)}, u32[]{:S(2)}, u32[]{:S(2)}) collective-permute-start(bf16[128,768]{1,0:T(8,128)(2,1)S(1)} %collective-permute-done.5.v2), channel_id=1, source_target_pairs={{0,4},{4,0},{8,12},{12,8},{16,20},{20,16},{24,28},{28,24},{32,36},... | collective-permute-start | bytes 589832 | tf_op jit(solution)/shard_map/ppermute | solution.py:394
  46.9 24.9 %collective-permute-start.9 = (bf16[512,768]{1,0:T(8,128)(2,1)S(1)}, bf16[512,768]{1,0:T(8,128)(2,1)S(1)}, u32[]{:S(2)}, u32[]{:S(2)}) collective-permute-start(bf16[512,768]{1,0:T(8,128)(2,1)S(1)} %copy-done.3), channel_id=1, source_target_pairs={{0,2},{1,3},{2,0},{3,1},{4,6},{5,7},{6,4},{7,5},{8,10},{9,11},{10,... | collective-permute-start | bytes 2359304 | tf_op jit(solution)/shard_map/ppermute | solution.py:399
  61.6 8.9 %collective-permute-start.10 = (bf16[192,768]{1,0:T(8,128)(2,1)S(1)}, bf16[192,768]{1,0:T(8,128)(2,1)S(1)}, u32[]{:S(2)}, u32[]{:S(2)}) collective-permute-start(bf16[192,768]{1,0:T(8,128)(2,1)S(1)} %get-tuple-element.60), channel_id=1, source_target_pairs={{0,16},{4,20},{8,24},{12,28},{16,0},{20,4},{24,8},{28,12},{32,48},... | collective-permute-start | bytes 884744 | tf_op jit(solution)/shard_map/ppermute | solution.py:368
  61.8 9.9 %collective-permute-start.11 = (bf16[192,768]{1,0:T(8,128)(2,1)S(1)}, bf16[192,768]{1,0:T(8,128)(2,1)S(1)}, u32[]{:S(2)}, u32[]{:S(2)}) collective-permute-start(bf16[192,768]{1,0:T(8,128)(2,1)S(1)} %get-tuple-element.61), channel_id=1, source_target_pairs={{0,48},{4,52},{8,56},{12,60},{16,32},{20,36},{24,40},{28,44},{32,1... | collective-permute-start | bytes 884744 | tf_op jit(solution)/shard_map/ppermute | solution.py:368
  71.7 3.4 %collective-permute-start.13 = (bf16[512,1536]{1,0:T(8,128)(2,1)S(1)}, bf16[512,1536]{1,0:T(8,128)(2,1)S(1)}, u32[]{:S(2)}, u32[]{:S(2)}) collective-permute-start(bf16[512,1536]{1,0:T(8,128)(2,1)S(1)} %get-tuple-element.68), channel_id=1, source_target_pairs={{0,1},{1,0},{2,3},{3,2},{4,5},{5,4},{6,7},{7,6},{8,9},{9,8},{10,11... | collective-permute-start | bytes 4718600 | tf_op jit(solution)/shard_map/ppermute | solution.py:407
  71.7 4.7 %collective-permute-start.12 = (bf16[512,768]{1,0:T(8,128)(2,1)S(1)}, bf16[512,768]{1,0:T(8,128)(2,1)S(1)}, u32[]{:S(2)}, u32[]{:S(2)}) collective-permute-start(bf16[512,768]{1,0:T(8,128)(2,1)S(1)} %collective-permute-done.9.l0.c0), channel_id=1, source_target_pairs={{0,1},{1,0},{2,3},{3,2},{4,5},{5,4},{6,7},{7,6},{8,9},{9,8},{10,11... | collective-permute-start | bytes 2359304 | tf_op jit(solution)/shard_map/ppermute | solution.py:406
  73.0 16.3 %collective-permute-start.16 = (bf16[2,192,768]{2,1,0:T(8,128)(2,1)S(1)}, bf16[2,192,768]{2,1,0:T(8,128)(2,1)S(1)}, u32[]{:S(2)}, u32[]{:S(2)}) collective-permute-start(bf16[2,192,768]{2,1,0:T(8,128)(2,1)S(1)} %get-tuple-element.64), channel_id=1, source_target_pairs={{0,16},{4,20},{8,24},{12,28},{16,0},{20,4},{24,8},{28,12},{32,48},... | collective-permute-start | bytes 1769480 | tf_op jit(solution)/shard_map/ppermute | solution.py:368
  73.5 25.9 %collective-permute-start.17 = (bf16[2,192,768]{2,1,0:T(8,128)(2,1)S(1)}, bf16[2,192,768]{2,1,0:T(8,128)(2,1)S(1)}, u32[]{:S(2)}, u32[]{:S(2)}) collective-permute-start(bf16[2,192,768]{2,1,0:T(8,128)(2,1)S(1)} %get-tuple-element.65), channel_id=1, source_target_pairs={{0,48},{4,52},{8,56},{12,60},{16,32},{20,36},{24,40},{28,44},{32,1... | collective-permute-start | bytes 1769480 | tf_op jit(solution)/shard_map/ppermute | solution.py:368
  75.9 32.0 %collective-permute-start.18 = (bf16[512,768]{1,0:T(8,128)(2,1)S(1)}, bf16[512,768]{1,0:T(8,128)(2,1)S(1)}, u32[]{:S(2)}, u32[]{:S(2)}) collective-permute-start(bf16[512,768]{1,0:T(8,128)(2,1)S(1)} %add_convert_fusion.1), channel_id=1, source_target_pairs={{0,2},{1,3},{2,0},{3,1},{4,6},{5,7},{6,4},{7,5},{8,10},{9,11},{10,... | collective-permute-start | bytes 2359304 | tf_op jit(solution)/shard_map/ppermute | solution.py:411
  78.5 22.2 %collective-permute-start.14 = (bf16[192,768]{1,0:T(8,128)(2,1)S(1)}, bf16[192,768]{1,0:T(8,128)(2,1)S(1)}, u32[]{:S(2)}, u32[]{:S(2)}) collective-permute-start(bf16[192,768]{1,0:T(8,128)(2,1)S(1)} %get-tuple-element.71), channel_id=1, source_target_pairs={{0,16},{4,20},{8,24},{12,28},{16,0},{20,4},{24,8},{28,12},{32,48},... | collective-permute-start | bytes 884744 | tf_op jit(solution)/shard_map/ppermute | solution.py:368
  78.9 25.5 %collective-permute-start.15 = (bf16[192,768]{1,0:T(8,128)(2,1)S(1)}, bf16[192,768]{1,0:T(8,128)(2,1)S(1)}, u32[]{:S(2)}, u32[]{:S(2)}) collective-permute-start(bf16[192,768]{1,0:T(8,128)(2,1)S(1)} %get-tuple-element.72), channel_id=1, source_target_pairs={{0,48},{4,52},{8,56},{12,60},{16,32},{20,36},{24,40},{28,44},{32,1... | collective-permute-start | bytes 884744 | tf_op jit(solution)/shard_map/ppermute | solution.py:368
  89.2 19.9 %collective-permute-start.19 = (bf16[2,128,768]{2,1,0:T(8,128)(2,1)S(1)}, bf16[2,128,768]{2,1,0:T(8,128)(2,1)S(1)}, u32[]{:S(2)}, u32[]{:S(2)}) collective-permute-start(bf16[2,128,768]{2,1,0:T(8,128)(2,1)S(1)} %get-tuple-element.75), channel_id=1, source_target_pairs={{0,4},{4,0},{8,12},{12,8},{16,20},{20,16},{24,28},{28,24},{32,36},... | collective-permute-start | bytes 1179656 | tf_op jit(solution)/shard_map/ppermute | solution.py:418
  99.4 19.0 %collective-permute-start.20 = (bf16[2,128,768]{2,1,0:T(8,128)(2,1)S(1)}, bf16[2,128,768]{2,1,0:T(8,128)(2,1)S(1)}, u32[]{:S(2)}, u32[]{:S(2)}) collective-permute-start(bf16[2,128,768]{2,1,0:T(8,128)(2,1)S(1)} %get-tuple-element.76), channel_id=1, source_target_pairs={{0,252},{4,8},{8,4},{12,16},{16,12},{20,24},{24,20},{28,32},{32,28... | collective-permute-start | bytes 1179656 | tf_op jit(solution)/shard_map/ppermute | solution.py:419
  105.1 14.2 %collective-permute-start.23 = (bf16[2,192,768]{2,1,0:T(8,128)(2,1)S(1)}, bf16[2,192,768]{2,1,0:T(8,128)(2,1)S(1)}, u32[]{:S(2)}, u32[]{:S(2)}) collective-permute-start(bf16[2,192,768]{2,1,0:T(8,128)(2,1)S(1)} %get-tuple-element.79), channel_id=1, source_target_pairs={{0,16},{4,20},{8,24},{12,28},{16,0},{20,4},{24,8},{28,12},{32,48},... | collective-permute-start | bytes 1769480 | tf_op jit(solution)/shard_map/ppermute | solution.py:368
  105.2 15.6 %collective-permute-start.24 = (bf16[2,192,768]{2,1,0:T(8,128)(2,1)S(1)}, bf16[2,192,768]{2,1,0:T(8,128)(2,1)S(1)}, u32[]{:S(2)}, u32[]{:S(2)}) collective-permute-start(bf16[2,192,768]{2,1,0:T(8,128)(2,1)S(1)} %get-tuple-element.80), channel_id=1, source_target_pairs={{0,48},{4,52},{8,56},{12,60},{16,32},{20,36},{24,40},{28,44},{32,1... | collective-permute-start | bytes 1769480 | tf_op jit(solution)/shard_map/ppermute | solution.py:368
  122.2 5.2 %collective-permute-start.25 = (bf16[96,768]{1,0:T(8,128)(2,1)S(1)}, bf16[96,768]{1,0:T(8,128)(2,1)S(1)}, u32[]{:S(2)}, u32[]{:S(2)}) collective-permute-start(bf16[96,768]{1,0:T(8,128)(2,1)S(1)} %get-tuple-element.91), channel_id=1, source_target_pairs={{0,64},{4,68},{8,72},{12,76},{16,80},{20,84},{24,88},{28,92},{32,9... | collective-permute-start | bytes 442376 | tf_op jit(solution)/shard_map/ppermute | solution.py:368
  122.3 6.4 %collective-permute-start.26 = (bf16[96,768]{1,0:T(8,128)(2,1)S(1)}, bf16[96,768]{1,0:T(8,128)(2,1)S(1)}, u32[]{:S(2)}, u32[]{:S(2)}) collective-permute-start(bf16[96,768]{1,0:T(8,128)(2,1)S(1)} %get-tuple-element.92), channel_id=1, source_target_pairs={{0,192},{4,196},{8,200},{12,204},{16,208},{20,212},{24,216},{28,22... | collective-permute-start | bytes 442376 | tf_op jit(solution)/shard_map/ppermute | solution.py:368
  123.0 28.3 %collective-permute-start.21 = (bf16[2,128,768]{2,1,0:T(8,128)(2,1)S(1)}, bf16[2,128,768]{2,1,0:T(8,128)(2,1)S(1)}, u32[]{:S(2)}, u32[]{:S(2)}) collective-permute-start(bf16[2,128,768]{2,1,0:T(8,128)(2,1)S(1)} %add_convert_fusion.3), channel_id=1, source_target_pairs={{0,4},{4,0},{8,12},{12,8},{16,20},{20,16},{24,28},{28,24},{32,36},... | collective-permute-start | bytes 1179656 | tf_op jit(solution)/shard_map/ppermute | solution.py:430
  123.0 28.3 %collective-permute-start.22 = (bf16[2,128,768]{2,1,0:T(8,128)(2,1)S(1)}, bf16[2,128,768]{2,1,0:T(8,128)(2,1)S(1)}, u32[]{:S(2)}, u32[]{:S(2)}) collective-permute-start(bf16[2,128,768]{2,1,0:T(8,128)(2,1)S(1)} %add_convert_fusion.2), channel_id=1, source_target_pairs={{0,252},{4,8},{8,4},{12,16},{16,12},{20,24},{24,20},{28,32},{32,28... | collective-permute-start | bytes 1179656 | tf_op jit(solution)/shard_map/ppermute | solution.py:429
  129.4 9.9 %collective-permute-start.27 = (bf16[192,768]{1,0:T(8,128)(2,1)S(1)}, bf16[192,768]{1,0:T(8,128)(2,1)S(1)}, u32[]{:S(2)}, u32[]{:S(2)}) collective-permute-start(bf16[192,768]{1,0:T(8,128)(2,1)S(1)} %get-tuple-element.93), channel_id=1, source_target_pairs={{0,64},{4,68},{8,72},{12,76},{16,80},{20,84},{24,88},{28,92},{32,9... | collective-permute-start | bytes 884744 | tf_op jit(solution)/shard_map/ppermute | solution.py:368
  130.2 13.9 %collective-permute-start.28 = (bf16[192,768]{1,0:T(8,128)(2,1)S(1)}, bf16[192,768]{1,0:T(8,128)(2,1)S(1)}, u32[]{:S(2)}, u32[]{:S(2)}) collective-permute-start(bf16[192,768]{1,0:T(8,128)(2,1)S(1)} %get-tuple-element.94), channel_id=1, source_target_pairs={{0,192},{4,196},{8,200},{12,204},{16,208},{20,212},{24,216},{28,22... | collective-permute-start | bytes 884744 | tf_op jit(solution)/shard_map/ppermute | solution.py:368
  144.8 7.6 %collective-permute-start.29 = (bf16[48,768]{1,0:T(8,128)(2,1)S(1)}, bf16[48,768]{1,0:T(8,128)(2,1)S(1)}, u32[]{:S(2)}, u32[]{:S(2)}) collective-permute-start(bf16[48,768]{1,0:T(8,128)(2,1)S(1)} %get-tuple-element.96), channel_id=1, source_target_pairs={{0,4},{4,0},{8,12},{12,8},{16,20},{20,16},{24,28},{28,24},{32,36},... | collective-permute-start | bytes 221192 | tf_op jit(solution)/shard_map/ppermute | solution.py:372
  144.9 8.3 %collective-permute-start.30 = (bf16[48,768]{1,0:T(8,128)(2,1)S(1)}, bf16[48,768]{1,0:T(8,128)(2,1)S(1)}, u32[]{:S(2)}, u32[]{:S(2)}) collective-permute-start(bf16[48,768]{1,0:T(8,128)(2,1)S(1)} %get-tuple-element.97), channel_id=1, source_target_pairs={{0,8},{4,12},{8,0},{12,4},{16,24},{20,28},{24,16},{28,20},{32,40},... | collective-permute-start | bytes 221192 | tf_op jit(solution)/shard_map/ppermute | solution.py:372
  145.0 8.7 %collective-permute-start.31 = (bf16[48,768]{1,0:T(8,128)(2,1)S(1)}, bf16[48,768]{1,0:T(8,128)(2,1)S(1)}, u32[]{:S(2)}, u32[]{:S(2)}) collective-permute-start(bf16[48,768]{1,0:T(8,128)(2,1)S(1)} %get-tuple-element.98), channel_id=1, source_target_pairs={{0,12},{4,8},{8,4},{12,0},{16,28},{20,24},{24,20},{28,16},{32,44},... | collective-permute-start | bytes 221192 | tf_op jit(solution)/shard_map/ppermute | solution.py:372
  (5 other events, 99.3 us)
